TPU v7x, 32 devices: a whole 2x2x4 slice. The times are simulated.
32 devices in a mesh: pipe: 4 (over x, core), dp: 8 (over z, y).
Axes of the slice: x: 2, y: 2, z: 4, core: 2. Of those that a mesh axis runs over, the one named last changes fastest.
Arguments:
- x_ckpt: bfloat16 [4, 2, 8, 512, 512], P('pipe', None, 'dp'), may hold values from -6 to 6
- top_cot: bfloat16 [2, 8, 512, 512], P(None, 'dp'), may hold values from -6 to 6
- skip_cot: bfloat16 [2, 8, 512, 512], P(None, 'dp'), may hold values from -6 to 6
- w_conv: bfloat16 [4, 512, 3, 1024], P('pipe', 'dp'), may hold values from -0.15625 to 0.15625
- w_mix: bfloat16 [4, 512, 1024], P('pipe', 'dp'), may hold values from -0.25 to 0.25
Outputs:
- cot_inputs: bfloat16 [4, 2, 8, 512, 512], P('pipe', None, 'dp')
- grad_conv: float32 [4, 512, 3, 1024], P('pipe', 'dp')
- grad_mix: float32 [4, 512, 1024], P('pipe', 'dp')
All inputs are finite; a program needn't handle non-finite values.
Results may differ from a plain program's by a relative error of at most 0.014.
Values may be sent and summed in bfloat16 or wider, within the bound.
No kernel may reach another device: no remote copies, remote signals or barrier semaphores. Data moves between devices by JAX's collectives and lax.ppermute only.
A program may use at most 128 MiB of HBM per device.

v0:
```python
import jax
import jax.numpy as jnp
from jax import lax
from jax.sharding import PartitionSpec as P


def passed_along(value, axis, steps):
    count = lax.axis_size(axis)
    leading, last = (max(0, -steps), min(count, count - steps))
    return lax.ppermute(value, axis, [(source, source + steps) for source in range(leading, last)])


def delay_seq(signal, shift_by):
    samples = signal.shape[1]
    rolled = jnp.roll(signal, shift_by, axis=1)
    positions = lax.broadcasted_iota(jnp.int32, (1, samples, 1), 1)
    return jnp.where(positions >= shift_by, rolled, jnp.zeros_like(rolled))


def advance_seq(signal, shift_by):
    samples = signal.shape[1]
    rolled = jnp.roll(signal, -shift_by, axis=1)
    positions = lax.broadcasted_iota(jnp.int32, (1, samples, 1), 1)
    return jnp.where(positions < samples - shift_by, rolled, jnp.zeros_like(rolled))


def tap_stack(signal, dilation):
    return jnp.stack([delay_seq(signal, offset * dilation) for offset in range(3)], axis=2)


def layer_back(x_rows, grad_next, skip_grad, conv_w, mix_w, dilation):
    channels = x_rows.shape[2]
    tapped_x = tap_stack(x_rows, dilation)
    pre_act = jnp.einsum("slkc,ckn->sln", tapped_x, conv_w, preferred_element_type=jnp.float32)
    filter_act = jnp.tanh(pre_act[..., :channels])
    gate_act = jax.nn.sigmoid(pre_act[..., channels:])
    hidden = (filter_act * gate_act).astype(jnp.bfloat16)
    cot_pair = jnp.concatenate([grad_next, skip_grad], axis=2)
    hid_grad = jnp.einsum("sln,cn->slc", cot_pair, mix_w, preferred_element_type=jnp.float32)
    pre_grad = jnp.concatenate(
        [
            hid_grad * gate_act * (1.0 - filter_act * filter_act),
            hid_grad * filter_act * gate_act * (1.0 - gate_act),
        ],
        axis=2,
    ).astype(jnp.bfloat16)
    back_taps = jnp.einsum("sln,ckn->slkc", pre_grad, conv_w, preferred_element_type=jnp.float32)
    input_grad = grad_next.astype(jnp.float32)
    for offset in range(3):
        input_grad = input_grad + advance_seq(back_taps[:, :, offset], offset * dilation)
    return (input_grad.astype(jnp.bfloat16), tapped_x, hidden, pre_grad, cot_pair)


def weight_terms(tapped_x, hidden, pre_grad, cot_pair):
    conv_term = jnp.einsum("slkc,sln->ckn", tapped_x, pre_grad, preferred_element_type=jnp.float32)
    mix_term = jnp.einsum("slc,sln->cn", hidden, cot_pair, preferred_element_type=jnp.float32)
    return jnp.concatenate([conv_term.reshape(conv_term.shape[0], -1), mix_term], axis=1)


def local(x_ckpt, top_cot, skip_cot, w_conv, w_mix):
    sec_count = lax.axis_size("pipe")
    sec_index = lax.axis_index("pipe")
    dilation = jnp.left_shift(jnp.int32(1), sec_index)
    conv_full, mix_full = (
        lax.all_gather(w_conv, "dp", axis=1, tiled=True),
        lax.all_gather(w_mix, "dp", axis=1, tiled=True),
    )
    conv_w = conv_full[0]
    mix_w = mix_full[0]
    micro_count, seq_count, samples, channels = x_ckpt.shape[1:]
    all_rows = micro_count * seq_count
    x_rows = x_ckpt[0].reshape(all_rows, samples, channels)
    top_rows = top_cot.reshape(all_rows, samples, channels)
    skip_rows = skip_cot.reshape(all_rows, samples, channels)
    is_last = sec_index == sec_count - 1
    blk_count = all_rows // seq_count
    step_count = sec_count + blk_count - 1
    act_shape = (seq_count, samples, channels)
    pair_shape = (seq_count, samples, 2 * channels)
    grad_init = jnp.zeros((channels, 8 * channels), jnp.float32)
    hid_init = jnp.zeros((1,), jnp.bfloat16)
    pre_init = jnp.zeros((1,), jnp.bfloat16)
    pair_init = jnp.zeros((1,), jnp.bfloat16)

    def step_fn(step_no, state_tuple):
        received, cot_store, grad_acc, hid_store, pre_store, pair_store = state_tuple
        blk_index = step_no - (sec_count - 1 - sec_index)
        is_active = (blk_index >= 0) & (blk_index < blk_count)
        row_start = jnp.clip(blk_index, 0, blk_count - 1) * seq_count
        x_blk = lax.dynamic_slice_in_dim(x_rows, row_start, seq_count, 0)
        top_blk = lax.dynamic_slice_in_dim(top_rows, row_start, seq_count, 0)
        skip_blk = lax.dynamic_slice_in_dim(skip_rows, row_start, seq_count, 0)
        grad_next = jnp.where(is_last, top_blk, received)

        def do_work(unused):
            input_grad, tapped_x, hidden, pre_grad, cot_pair = layer_back(
                x_blk, grad_next, skip_blk, conv_w, mix_w, dilation
            )
            grad_term = weight_terms(tapped_x, hidden, pre_grad, cot_pair)
            return (input_grad, hidden, pre_grad, cot_pair, grad_term)

        def no_work(unused):
            return (
                jnp.zeros(act_shape, jnp.bfloat16),
                jnp.zeros(act_shape, jnp.bfloat16),
                jnp.zeros(pair_shape, jnp.bfloat16),
                jnp.zeros(pair_shape, jnp.bfloat16),
                jnp.zeros_like(grad_acc),
            )

        input_grad, hidden, pre_grad, cot_pair, grad_term = lax.cond(is_active, do_work, no_work, 0)
        grad_acc = grad_acc + grad_term
        cot_store = jnp.where(
            is_active,
            lax.dynamic_update_slice_in_dim(cot_store, input_grad, row_start, 0),
            cot_store,
        )
        received = passed_along(input_grad, "pipe", -1)
        return (received, cot_store, grad_acc, hid_store, pre_store, pair_store)

    initial = (
        jnp.zeros(act_shape, jnp.bfloat16),
        jnp.zeros((all_rows, samples, channels), jnp.bfloat16),
        grad_init,
        hid_init,
        pre_init,
        pair_init,
    )
    final_state = lax.fori_loop(0, step_count, step_fn, initial)
    cot_store, grad_acc, hid_store, pre_store, pair_store = final_state[1:]
    shard_rows = channels // lax.axis_size("dp")
    shares = lax.psum_scatter(grad_acc, "dp", scatter_dimension=0, tiled=True)
    conv_share = shares[:, : 6 * channels].reshape(shard_rows, 3, 2 * channels)
    mix_share = shares[:, 6 * channels :]
    return (
        cot_store.reshape(1, micro_count, seq_count, samples, channels),
        conv_share[None],
        mix_share[None],
    )


def solution(mesh):
    placed = (
        P("pipe", None, "dp", None, None),
        P(None, "dp", None, None),
        P(None, "dp", None, None),
        P("pipe", "dp", None, None),
        P("pipe", "dp", None),
    )
    return jax.shard_map(
        local,
        mesh=mesh,
        in_specs=placed,
        out_specs=(
            P("pipe", None, "dp", None, None),
            P("pipe", "dp", None, None),
            P("pipe", "dp", None),
        ),
        check_vma=False,
    )
```

profile of v0, /device:TPU:0, one launch (start us, length us, event | category | flops | bytes accessed | tf_op | source)
XLA Modules:
  0.0 411.4 jit_solution(6724155865388676737)
XLA Ops:
  8.7 44.3 %all-gather.3.cloned.1.call-done = bf16[1,512,1024]{2,1,0:T(8,128)(2,1)} async-done(((bf16[1,64,1024]{2,1,0:T(8,128)(2,1)}), bf16[1,512,1024]{2,1,0:T(8,128)(2,1)}) %all-gather.3.cloned.1.call-update) | async-done | bytes 1048592 | tf_op jit(solution)/shard_map/all_gather | solution.py:66
  53.0 61.5 %all-gather.5.cloned.1.call-done = bf16[1,512,3,1024]{3,1,2,0:T(8,128)(2,1)} async-done(((bf16[1,64,3,1024]{3,1,2,0:T(8,128)(2,1)}), bf16[1,512,3,1024]{3,1,2,0:T(8,128)(2,1)}) %all-gather.5.cloned.1.call-update) | async-done | bytes 3145744 | tf_op jit(solution)/shard_map/all_gather | solution.py:65
  115.6 126.9 %while.20 = (s32[]{:T(128)}, bf16[1,512,512]{2,1,0:T(8,128)(2,1)S(1)}, bf16[2,512,512]{2,1,0:T(8,128)(2,1)}, f32[512,4096]{0,1:T(8,128)}, s32[]{:T(128)}, /*inde...) while((s32[]{:T(128)}, ...), condition=%wide.region_3.8_spmd.clone, body=%wide.region_0.7_spmd.clone.sunk | while | flops 5937039872 | bytes 117971056 | solution.py:129
  115.6 4.3 %conditional.3 = (bf16[1,512,512]{2,1,0:T(8,128)(2,1)S(1)}, f32[512,4096]{0,1:T(8,128)}) conditional(s32[]{:T(128)} %convert_element_type.39, () %tuple.71, (pred[]{:T(512)}, bf16[2,512,512]{2,1,0:T(8,128)(2,1)}, s32[]{:T(128)}, bf16[1,512,512]{2,1,0:T(8,128)(2,1)S(1)}, bf16[2,512,512]{2,1,0:T(8,128)(2,1)}, /*index=5*/bf16[512,1024]{1,0:T(8,128)(2,1)}, ...), branch_computations={%region_1.1_spmd, %region_2.6_spmd} | conditional | flops 5932583424 | bytes 80746224 | solution.py:111
  115.6 4.3 %broadcast.78 = f32[512,4096]{0,1:T(8,128)} broadcast(f32[]{:T(128)} %constant.135.clone), dimensions={} | broadcast | bytes 8388612 | tf_op jit(solution)/shard_map/broadcast.4
  121.2 8.8 %select_add_fusion.2 = f32[512,4096]{0,1:T(8,128)} fusion(f32[512,4096]{0,1:T(8,128)} %get-tuple-element.522, f32[512,4096]{0,1:T(8,128)} %get-tuple-element.545, pred[]{:T(512)S(6)} %compare.5), kind=kLoop, calls=%fused_computation.59.clone.1 | loop fusion | flops 4194304 | bytes 25165824 | tf_op jit(solution)/shard_map/while/body/eval_jaxpr/add | solution.py:112
  131.2 4.3 %conditional.3 = (bf16[1,512,512]{2,1,0:T(8,128)(2,1)S(1)}, f32[512,4096]{0,1:T(8,128)}) conditional(s32[]{:T(128)} %convert_element_type.39, () %tuple.71, (pred[]{:T(512)}, bf16[2,512,512]{2,1,0:T(8,128)(2,1)}, s32[]{:T(128)}, bf16[1,512,512]{2,1,0:T(8,128)(2,1)S(1)}, bf16[2,512,512]{2,1,0:T(8,128)(2,1)}, /*index=5*/bf16[512,1024]{1,0:T(8,128)(2,1)}, ...), branch_computations={%region_1.1_spmd, %region_2.6_spmd} | conditional | flops 5932583424 | bytes 80746224 | solution.py:111
  131.2 4.3 %broadcast.78 = f32[512,4096]{0,1:T(8,128)} broadcast(f32[]{:T(128)} %constant.135.clone), dimensions={} | broadcast | bytes 8388612 | tf_op jit(solution)/shard_map/broadcast.4
  136.8 11.2 %select_add_fusion.2 = f32[512,4096]{0,1:T(8,128)} fusion(f32[512,4096]{0,1:T(8,128)} %get-tuple-element.522, f32[512,4096]{0,1:T(8,128)} %get-tuple-element.545, pred[]{:T(512)S(6)} %compare.5), kind=kLoop, calls=%fused_computation.59.clone.1 | loop fusion | flops 4194304 | bytes 25165824 | tf_op jit(solution)/shard_map/while/body/eval_jaxpr/add | solution.py:112
  149.2 4.3 %conditional.3 = (bf16[1,512,512]{2,1,0:T(8,128)(2,1)S(1)}, f32[512,4096]{0,1:T(8,128)}) conditional(s32[]{:T(128)} %convert_element_type.39, () %tuple.71, (pred[]{:T(512)}, bf16[2,512,512]{2,1,0:T(8,128)(2,1)}, s32[]{:T(128)}, bf16[1,512,512]{2,1,0:T(8,128)(2,1)S(1)}, bf16[2,512,512]{2,1,0:T(8,128)(2,1)}, /*index=5*/bf16[512,1024]{1,0:T(8,128)(2,1)}, ...), branch_computations={%region_1.1_spmd, %region_2.6_spmd} | conditional | flops 5932583424 | bytes 80746224 | solution.py:111
  149.2 4.3 %broadcast.78 = f32[512,4096]{0,1:T(8,128)} broadcast(f32[]{:T(128)} %constant.135.clone), dimensions={} | broadcast | bytes 8388612 | tf_op jit(solution)/shard_map/broadcast.4
  154.9 11.2 %select_add_fusion.2 = f32[512,4096]{0,1:T(8,128)} fusion(f32[512,4096]{0,1:T(8,128)} %get-tuple-element.522, f32[512,4096]{0,1:T(8,128)} %get-tuple-element.545, pred[]{:T(512)S(6)} %compare.5), kind=kLoop, calls=%fused_computation.59.clone.1 | loop fusion | flops 4194304 | bytes 25165824 | tf_op jit(solution)/shard_map/while/body/eval_jaxpr/add | solution.py:112
  166.2 14.8 %collective-permute-done = bf16[1,512,512]{2,1,0:T(8,128)(2,1)S(1)} collective-permute-done((bf16[1,512,512]{2,1,0:T(8,128)(2,1)S(1)}, bf16[1,512,512]{2,1,0:T(8,128)(2,1)S(1)}, u32[]{:S(2)}, u32[]{:S(2)}) %collective-permute-start) | collective-permute-done | bytes 524320 | tf_op jit(solution)/shard_map/while/body/eval_jaxpr/ppermute | solution.py:10
  181.1 16.7 %conditional.3 = (bf16[1,512,512]{2,1,0:T(8,128)(2,1)S(1)}, f32[512,4096]{0,1:T(8,128)}) conditional(s32[]{:T(128)} %convert_element_type.39, () %tuple.71, (pred[]{:T(512)}, bf16[2,512,512]{2,1,0:T(8,128)(2,1)}, s32[]{:T(128)}, bf16[1,512,512]{2,1,0:T(8,128)(2,1)S(1)}, bf16[2,512,512]{2,1,0:T(8,128)(2,1)}, /*index=5*/bf16[512,1024]{1,0:T(8,128)(2,1)}, ...), branch_computations={%region_1.1_spmd, %region_2.6_spmd} | conditional | flops 5932583424 | bytes 80746224 | solution.py:111
  182.4 1.3 dynamic-slice_select_fusion
  184.7 1.8 convolution_bitcast_fusion.1
  188.6 1.8 convolution_bitcast_fusion
  191.8 1.8 fusion.12
  193.6 4.2 %pad_maximum_fusion = f32[512,4096]{0,1:T(8,128)} fusion(f32[512,1024]{0,1:T(8,128)S(1)} %fusion.13, f32[512,3072]{0,1:T(8,128)S(1)} %bitcast.66), kind=kLoop, calls=%fused_computation | loop fusion | flops 2097152 | bytes 16777216 | tf_op jit(solution)/shard_map/while/body/eval_jaxpr/cond/branch_1_fun/concatenate | solution.py:57
  199.1 11.2 %select_add_fusion.2 = f32[512,4096]{0,1:T(8,128)} fusion(f32[512,4096]{0,1:T(8,128)} %get-tuple-element.522, f32[512,4096]{0,1:T(8,128)} %get-tuple-element.545, pred[]{:T(512)S(6)} %compare.5), kind=kLoop, calls=%fused_computation.59.clone.1 | loop fusion | flops 4194304 | bytes 25165824 | tf_op jit(solution)/shard_map/while/body/eval_jaxpr/add | solution.py:112
  210.5 1.6 collective-permute-done
  212.1 16.7 %conditional.3 = (bf16[1,512,512]{2,1,0:T(8,128)(2,1)S(1)}, f32[512,4096]{0,1:T(8,128)}) conditional(s32[]{:T(128)} %convert_element_type.39, () %tuple.71, (pred[]{:T(512)}, bf16[2,512,512]{2,1,0:T(8,128)(2,1)}, s32[]{:T(128)}, bf16[1,512,512]{2,1,0:T(8,128)(2,1)S(1)}, bf16[2,512,512]{2,1,0:T(8,128)(2,1)}, /*index=5*/bf16[512,1024]{1,0:T(8,128)(2,1)}, ...), branch_computations={%region_1.1_spmd, %region_2.6_spmd} | conditional | flops 5932583424 | bytes 80746224 | solution.py:111
  213.4 1.3 dynamic-slice_select_fusion
  215.8 1.8 convolution_bitcast_fusion.1
  219.6 1.8 convolution_bitcast_fusion
  222.8 1.8 fusion.12
  224.6 4.2 %pad_maximum_fusion = f32[512,4096]{0,1:T(8,128)} fusion(f32[512,1024]{0,1:T(8,128)S(1)} %fusion.13, f32[512,3072]{0,1:T(8,128)S(1)} %bitcast.66), kind=kLoop, calls=%fused_computation | loop fusion | flops 2097152 | bytes 16777216 | tf_op jit(solution)/shard_map/while/body/eval_jaxpr/cond/branch_1_fun/concatenate | solution.py:57
  230.2 11.2 %select_add_fusion.2 = f32[512,4096]{0,1:T(8,128)} fusion(f32[512,4096]{0,1:T(8,128)} %get-tuple-element.522, f32[512,4096]{0,1:T(8,128)} %get-tuple-element.545, pred[]{:T(512)S(6)} %compare.5), kind=kLoop, calls=%fused_computation.59.clone.1 | loop fusion | flops 4194304 | bytes 25165824 | tf_op jit(solution)/shard_map/while/body/eval_jaxpr/add | solution.py:112
  242.5 8.9 %copy.15 = f32[512,4096]{1,0:T(8,128)} copy(f32[512,4096]{0,1:T(8,128)} %get-tuple-element.365) | data formatting | bytes 16777216 | tf_op jit(solution)/shard_map/while | solution.py:129
  251.5 148.6 %reduce-scatter.2.cloned.1.call-done = f32[64,4096]{1,0:T(8,128)} async-done(((f32[512,4096]{1,0:T(8,128)}), f32[64,4096]{1,0:T(8,128)}) %reduce-scatter.2.cloned.1.call-update) | async-done | bytes 1048592 | tf_op jit(solution)/shard_map/reduce_scatter | solution.py:132
  401.8 1.3 copy.16
  403.2 1.7 slice_bitcast_fusion.3
  (73 shorter events, 26.0 us)
Async XLA Ops:
  7.2 45.8 %all-gather.3.cloned.1.call-start = ((), (), s32[]{:S(2)}) async-start(), calls=%async_computation.1 | async-start | bytes 1179648 | tf_op jit(solution)/shard_map/all_gather | solution.py:66
  7.9 106.6 %all-gather.5.cloned.1.call-start = ((), (), s32[]{:S(2)}) async-start(), calls=%async_computation.2 | async-start | bytes 3538944 | tf_op jit(solution)/shard_map/all_gather | solution.py:65
  8.6 391.4 %reduce-scatter.2.cloned.1.call-start = ((), (), s32[]{:S(2)}) async-start(), calls=%async_computation.3 | async-start | bytes 9437184 | tf_op jit(solution)/shard_map/reduce_scatter | solution.py:132
  119.9 10.3 %collective-permute-start = (bf16[1,512,512]{2,1,0:T(8,128)(2,1)S(1)}, bf16[1,512,512]{2,1,0:T(8,128)(2,1)S(1)}, u32[]{:S(2)}, u32[]{:S(2)}) collective-permute-start(bf16[1,512,512]{2,1,0:T(8,128)(2,1)S(1)} %get-tuple-element.521), channel_id=1, source_target_pairs={{8,0},{16,8},{24,16},{9,1},{17,9},{25,17},{10,2},{18,10},{26,18},{... | collective-permute-start | bytes 1572872 | tf_op jit(solution)/shard_map/while/body/eval_jaxpr/ppermute | solution.py:10
  121.2 8.8 %copy-start = (bf16[2,512,512]{2,1,0:T(8,128)(2,1)S(1)}, bf16[2,512,512]{2,1,0:T(8,128)(2,1)}, u32[]{:S(2)}) copy-start(bf16[2,512,512]{2,1,0:T(8,128)(2,1)} %get-tuple-element.544) | copy-start | bytes 3145732 | tf_op jit(solution)/shard_map/while
  130.2 1.0 copy-start.1
  135.5 12.7 %collective-permute-start = (bf16[1,512,512]{2,1,0:T(8,128)(2,1)S(1)}, bf16[1,512,512]{2,1,0:T(8,128)(2,1)S(1)}, u32[]{:S(2)}, u32[]{:S(2)}) collective-permute-start(bf16[1,512,512]{2,1,0:T(8,128)(2,1)S(1)} %get-tuple-element.521), channel_id=1, source_target_pairs={{8,0},{16,8},{24,16},{9,1},{17,9},{25,17},{10,2},{18,10},{26,18},{... | collective-permute-start | bytes 1572872 | tf_op jit(solution)/shard_map/while/body/eval_jaxpr/ppermute | solution.py:10
  136.8 11.2 %copy-start = (bf16[2,512,512]{2,1,0:T(8,128)(2,1)S(1)}, bf16[2,512,512]{2,1,0:T(8,128)(2,1)}, u32[]{:S(2)}) copy-start(bf16[2,512,512]{2,1,0:T(8,128)(2,1)} %get-tuple-element.544) | copy-start | bytes 3145732 | tf_op jit(solution)/shard_map/while
  148.2 1.0 copy-start.1
  153.5 27.5 %collective-permute-start = (bf16[1,512,512]{2,1,0:T(8,128)(2,1)S(1)}, bf16[1,512,512]{2,1,0:T(8,128)(2,1)S(1)}, u32[]{:S(2)}, u32[]{:S(2)}) collective-permute-start(bf16[1,512,512]{2,1,0:T(8,128)(2,1)S(1)} %get-tuple-element.521), channel_id=1, source_target_pairs={{8,0},{16,8},{24,16},{9,1},{17,9},{25,17},{10,2},{18,10},{26,18},{... | collective-permute-start | bytes 1572872 | tf_op jit(solution)/shard_map/while/body/eval_jaxpr/ppermute | solution.py:10
  154.8 11.2 %copy-start = (bf16[2,512,512]{2,1,0:T(8,128)(2,1)S(1)}, bf16[2,512,512]{2,1,0:T(8,128)(2,1)}, u32[]{:S(2)}) copy-start(bf16[2,512,512]{2,1,0:T(8,128)(2,1)} %get-tuple-element.544) | copy-start | bytes 3145732 | tf_op jit(solution)/shard_map/while
  166.2 14.9 %copy-start.1 = (bf16[2,512,512]{2,1,0:T(8,128)(2,1)}, bf16[2,512,512]{2,1,0:T(8,128)(2,1)S(1)}, u32[]{:S(2)}) copy-start(bf16[2,512,512]{2,1,0:T(8,128)(2,1)S(1)} %select_dynamic-update-slice_fusion.2) | copy-start | bytes 3145732 | tf_op jit(solution)/shard_map/while
  181.1 3.6 copy-start.2
  184.7 1.9 copy-start.3
  197.8 14.3 %collective-permute-start = (bf16[1,512,512]{2,1,0:T(8,128)(2,1)S(1)}, bf16[1,512,512]{2,1,0:T(8,128)(2,1)S(1)}, u32[]{:S(2)}, u32[]{:S(2)}) collective-permute-start(bf16[1,512,512]{2,1,0:T(8,128)(2,1)S(1)} %get-tuple-element.521), channel_id=1, source_target_pairs={{8,0},{16,8},{24,16},{9,1},{17,9},{25,17},{10,2},{18,10},{26,18},{... | collective-permute-start | bytes 1572872 | tf_op jit(solution)/shard_map/while/body/eval_jaxpr/ppermute | solution.py:10
  199.1 11.2 %copy-start = (bf16[2,512,512]{2,1,0:T(8,128)(2,1)S(1)}, bf16[2,512,512]{2,1,0:T(8,128)(2,1)}, u32[]{:S(2)}) copy-start(bf16[2,512,512]{2,1,0:T(8,128)(2,1)} %get-tuple-element.544) | copy-start | bytes 3145732 | tf_op jit(solution)/shard_map/while
  210.5 1.6 copy-start.1
  212.1 3.6 copy-start.2
  215.7 1.9 copy-start.3
  228.9 12.7 %collective-permute-start = (bf16[1,512,512]{2,1,0:T(8,128)(2,1)S(1)}, bf16[1,512,512]{2,1,0:T(8,128)(2,1)S(1)}, u32[]{:S(2)}, u32[]{:S(2)}) collective-permute-start(bf16[1,512,512]{2,1,0:T(8,128)(2,1)S(1)} %get-tuple-element.521), channel_id=1, source_target_pairs={{8,0},{16,8},{24,16},{9,1},{17,9},{25,17},{10,2},{18,10},{26,18},{... | collective-permute-start | bytes 1572872 | tf_op jit(solution)/shard_map/while/body/eval_jaxpr/ppermute | solution.py:10
  230.1 11.2 %copy-start = (bf16[2,512,512]{2,1,0:T(8,128)(2,1)S(1)}, bf16[2,512,512]{2,1,0:T(8,128)(2,1)}, u32[]{:S(2)}) copy-start(bf16[2,512,512]{2,1,0:T(8,128)(2,1)} %get-tuple-element.544) | copy-start | bytes 3145732 | tf_op jit(solution)/shard_map/while
  241.5 1.0 copy-start.1
Sparse Core Ops, SparseCore 0:
  10.1 42.8 all-gather.2
  55.2 59.2 all-gather.4
  251.6 148.4 reduce-scatter.1
where the time goes:
time: 412 us; the launch traced here: 411 us
  waiting for transfers between devices  272 us (66%)
  other arithmetic  70 us (17%)
  local copies, waits for them, and re-layouts  33.5 us (8%)
  matrix products  14.9 us (4%)
  between operations  13.8 us (3%)
  starting transfers between devices  6.51 us (2%)
    reduce_scatter x1, waiting for transfers between devices, local(): shares = lax.psum_scatter(grad_acc, 'dp', scatter_dimension=0, tiled=True)  149 us
    all_gather x1, waiting for transfers between devices, local(): lax.all_gather(w_conv, 'dp', axis=1, tiled=True)  61.5 us
    add x5, other arithmetic, step_fn(): grad_acc = grad_acc + grad_term  53.6 us
    all_gather x1, waiting for transfers between devices, local(): lax.all_gather(w_mix, 'dp', axis=1, tiled=True)  44.3 us
    ppermute x5, waiting for transfers between devices, passed_along(): lax.ppermute(value, axis, [(source, source + steps) for source in range(l...  16.4 us
    another operation x7, local copies, waits for them, and re-layouts  13.1 us
    while x1, local copies, waits for them, and re-layouts, local(): final_state = lax.fori_loop(0, step_count, step_fn, initial)  8.92 us
    concatenate x2, other arithmetic, weight_terms(): jnp.concatenate([conv_term.reshape(conv_term.shape[0], -1), mix_term], ax...  8.43 us
  transfers between devices with their start and end apart: 8, of which 5 were waited for; matrix products, arithmetic and copies ran while one was open for 13% of the time, Pallas kernels for 0%

commit v1 on v0

v1 whole, which is shorter than its diff:
```python
import functools

import jax
import jax.numpy as jnp
from jax import lax
from jax.experimental import pallas as pl
from jax.experimental.pallas import tpu as pltpu
from jax.sharding import PartitionSpec as P

F32 = jnp.float32
BF16 = jnp.bfloat16
NT = (((1,), (1,)), ((), ()))


def ring_order(count):
    return list(range(0, count, 2)) + list(range(count - 1 - count % 2, 0, -2))


def ring_pairs(order):
    count = len(order)
    right = [(order[i], order[(i + 1) % count]) for i in range(count)]
    left = [(order[(i + 1) % count], order[i]) for i in range(count)]
    return right, left


def chain_kernel(
    dilation, flags, g_hbm, hs_hbm, a1_hbm, a2_hbm, w_hbm, _pg, _ig, _gk, pg_hbm, ig_hbm, gk_hbm,
    g, hs, a1, a2, wm, wc, pg, ig, bt, sems,
):
    samples, channels = g.shape
    padding = bt.shape[1] - samples

    @pl.when(flags[0] == 1)
    def _():
        def load(source, target, number):
            copy = pltpu.make_async_copy(source, target, sems.at[number])
            copy.start()
            return copy

        get_g = load(g_hbm, g, 0)
        get_wm = load(w_hbm.at[3, :, pl.ds(0, channels)], wm, 1)
        get_hs = load(hs_hbm, hs, 2)
        get_a1 = load(a1_hbm, a1, 3)
        get_a2 = load(a2_hbm, a2, 4)
        get_wc = [load(w_hbm.at[k], wc.at[k], 5 + k) for k in range(3)]
        get_g.wait()
        keep_g = load(g, gk_hbm, 8)
        get_wm.wait()
        hid = lax.dot_general(g[...], wm[...], NT, preferred_element_type=F32)
        get_hs.wait()
        hid = hid + hs[...]
        get_a1.wait()
        pg[:, :channels] = (hid * a1[...]).astype(BF16)
        get_a2.wait()
        pg[:, channels:] = (hid * a2[...]).astype(BF16)
        put_pg = load(pg, pg_hbm, 9)
        for k in range(3):
            get_wc[k].wait()
            bt[k, :samples, :] = lax.dot_general(pg[...], wc[k], NT, preferred_element_type=F32)
            if k:
                bt[k, samples:, :] = jnp.zeros((padding, channels), F32)
        rows = 64
        for start in range(0, samples, rows):
            total = g[start : start + rows, :].astype(F32) + bt[0, start : start + rows, :]
            total = total + bt[1, start + dilation : start + dilation + rows, :]
            total = total + bt[2, start + 2 * dilation : start + 2 * dilation + rows, :]
            ig[start : start + rows, :] = total.astype(BF16)
        put_ig = load(ig, ig_hbm, 10)
        keep_g.wait()
        put_pg.wait()
        put_ig.wait()


def chain_call(dilation, flags, g, hs, a1, a2, w_full, held, padding):
    samples, channels = g.shape
    any_spec = pl.BlockSpec(memory_space=pl.ANY)
    shapes = (
        jax.ShapeDtypeStruct((samples, 2 * channels), BF16),
        jax.ShapeDtypeStruct((samples, channels), BF16),
        jax.ShapeDtypeStruct((samples, channels), BF16),
    )
    return pl.pallas_call(
        functools.partial(chain_kernel, dilation),
        out_shape=shapes,
        in_specs=[pl.BlockSpec(memory_space=pltpu.SMEM)] + [any_spec] * 8,
        out_specs=[any_spec] * 3,
        scratch_shapes=[
            pltpu.VMEM((samples, channels), BF16),
            pltpu.VMEM((samples, channels), F32),
            pltpu.VMEM((samples, channels), F32),
            pltpu.VMEM((samples, channels), F32),
            pltpu.VMEM((channels, channels), BF16),
            pltpu.VMEM((3, channels, 2 * channels), BF16),
            pltpu.VMEM((samples, 2 * channels), BF16),
            pltpu.VMEM((samples, channels), BF16),
            pltpu.VMEM((3, samples + padding, channels), F32),
            pltpu.SemaphoreType.DMA((11,)),
        ],
        input_output_aliases={6: 0, 7: 1, 8: 2},
        compiler_params=pltpu.CompilerParams(vmem_limit_bytes=24 * 2**20),
        cost_estimate=pl.CostEstimate(flops=2 * 10**9, bytes_accessed=8 * 2**20, transcendentals=0),
    )(flags, g, hs, a1, a2, w_full, *held)


def local(x_ckpt, top_cot, skip_cot, w_conv, w_mix):
    sections = lax.axis_size("pipe")
    section = lax.axis_index("pipe")
    replicas = lax.axis_size("dp")
    replica = lax.axis_index("dp")
    micro, seqs, samples, channels = x_ckpt.shape[1:]
    rows = micro * seqs * samples
    part = w_conv.shape[1]
    dilation = jnp.left_shift(jnp.int32(1), section)

    order = ring_order(replicas)
    right, left = ring_pairs(order)
    half = replicas // 2
    owners = jnp.array(order, jnp.int32)
    place = jnp.array([order.index(i) for i in range(replicas)], jnp.int32)[replica]

    def owner(offset):
        return owners[lax.rem(place + offset + replicas, replicas)]

    shard = jnp.concatenate([w_conv[0].transpose(1, 0, 2), w_mix], axis=0)
    w_full = jnp.zeros((4, channels, 2 * channels), BF16)

    def put(full, block, offset, first=0):
        return lax.dynamic_update_slice(full, block, (first, owner(offset) * part, 0))

    w_full = put(w_full, shard, 0)
    from_left, from_right = shard, shard
    for step in range(1, half):
        from_left = lax.ppermute(from_left, "dp", right)
        from_right = lax.ppermute(from_right, "dp", left)
        w_full = put(w_full, from_left, -step)
        w_full = put(w_full, from_right, step)
    w_full = put(w_full, lax.ppermute(from_left[:2], "dp", right), -half, 0)
    w_full = put(w_full, lax.ppermute(from_right[2:], "dp", left), half, 2)

    x_rows = x_ckpt[0].reshape(micro * seqs, samples, channels)
    positions = lax.broadcasted_iota(jnp.int32, (1, samples, 1), 1)
    taps = [x_rows]
    for k in (1, 2):
        rolled = jnp.roll(x_rows, k * dilation, axis=1)
        taps.append(jnp.where(positions >= k * dilation, rolled, jnp.zeros_like(rolled)))
    taps = jnp.concatenate(taps, axis=2).reshape(rows, 3 * channels)
    skip_rows = skip_cot.reshape(rows, channels)
    top_rows = top_cot.reshape(micro, seqs * samples, channels)

    w_taps = w_full[:3].reshape(3 * channels, 2 * channels)
    pre = jnp.dot(taps, w_taps, preferred_element_type=F32)
    filt = jnp.tanh(pre[:, :channels])
    gate = jax.nn.sigmoid(pre[:, channels:])
    hidden = (filt * gate).astype(BF16)
    a1 = gate * (1.0 - filt * filt)
    a2 = filt * gate * (1.0 - gate)
    h_skip = lax.dot_general(skip_rows, w_full[3, :, channels:], NT, preferred_element_type=F32)

    block = seqs * samples
    padding = max(16, 2 * 2 ** (sections - 1))

    def cut(array, m):
        return lax.slice_in_dim(array, m * block, (m + 1) * block, axis=0)

    parts = [(cut(h_skip, m), cut(a1, m), cut(a2, m)) for m in range(micro)]
    g = [top_rows[m] for m in range(micro)]
    held = [
        (jnp.zeros((block, 2 * channels), BF16), jnp.zeros((block, channels), BF16), jnp.zeros((block, channels), BF16))
        for m in range(micro)
    ]
    for stage in range(sections - 1, -1, -1):
        flags = (section == stage).astype(jnp.int32).reshape(1)
        for m in range(micro):
            held[m] = chain_call(2**stage, flags, g[m], *parts[m], w_full, held[m], padding)
            if stage:
                g[m] = lax.ppermute(held[m][1], "pipe", [(stage, stage - 1)])

    pre_grad = jnp.concatenate([h[0] for h in held], axis=0)
    cot = jnp.stack([h[1] for h in held], axis=0)
    g_all = jnp.concatenate([h[2] for h in held], axis=0)
    pair = jnp.concatenate([g_all, skip_rows], axis=1)
    over_rows = (((0,), (0,)), ((), ()))
    conv_term = lax.dot_general(taps, pre_grad, over_rows, preferred_element_type=F32).astype(BF16)
    mix_term = lax.dot_general(hidden, pair, over_rows, preferred_element_type=F32).astype(BF16)
    terms = jnp.concatenate([conv_term, mix_term], axis=0).reshape(4, channels, 2 * channels)

    def term(offset, first=0, count=4):
        return lax.dynamic_slice(terms, (first, owner(offset) * part, 0), (count, part, 2 * channels))

    to_right = lax.ppermute(term(half, 0, 2), "dp", right)
    to_left = lax.ppermute(term(-half, 2, 2), "dp", left)
    for dist in range(half - 1, 0, -1):
        mine_r, mine_l = term(dist), term(-dist)
        if dist == half - 1:
            zero = jnp.zeros_like(to_right)
            to_right = jnp.concatenate([to_right, zero], axis=0)
            to_left = jnp.concatenate([zero, to_left], axis=0)
        sum_r = (mine_r.astype(F32) + to_right.astype(F32)).astype(BF16)
        sum_l = (mine_l.astype(F32) + to_left.astype(F32)).astype(BF16)
        to_right = lax.ppermute(sum_r, "dp", right)
        to_left = lax.ppermute(sum_l, "dp", left)
    share = term(0).astype(F32) + to_right.astype(F32) + to_left.astype(F32)
    return (
        cot.reshape(1, micro, seqs, samples, channels),
        share[:3].transpose(1, 0, 2)[None],
        share[3][None],
    )


def solution(mesh):
    placed = (
        P("pipe", None, "dp", None, None),
        P(None, "dp", None, None),
        P(None, "dp", None, None),
        P("pipe", "dp", None, None),
        P("pipe", "dp", None),
    )
    return jax.shard_map(
        local,
        mesh=mesh,
        in_specs=placed,
        out_specs=(
            P("pipe", None, "dp", None, None),
            P("pipe", "dp", None, None),
            P("pipe", "dp", None),
        ),
        check_vma=False,
    )
```

time: 412 us -> 208 us (0.50)
  waiting for transfers between devices: 272 us -> 91.4 us
  other arithmetic: 70 us -> 9.71 us
  starting transfers between devices: 6.51 us -> 26.5 us
  Pallas kernels: 0 us -> 11.8 us
  local copies, waits for them, and re-layouts: 33.5 us -> 44.1 us
  matrix products: 14.9 us -> 10.7 us
    reduce_scatter x1 -> x0, waiting for transfers between devices: 149 us -> none  [local(): shares = lax.psum_scatter(grad_acc, 'dp', scatter_dimension=0, tiled=True)]
    all_gather x2 -> x0, waiting for transfers between devices: 106 us -> none  [the longest x1 61.5 us: local(): lax.all_gather(w_conv, 'dp', axis=1, tiled=True)]
    ppermute x5 -> x22, waiting for transfers between devices: 16.4 us -> 91.4 us  [the longest x3 27.5 us: local(): to_left = lax.ppermute(sum_l, 'dp', left)]
    add x5 -> x1, other arithmetic: 53.6 us -> 0.26 us  [local(): share = term(0).astype(F32) + to_right.astype(F32) + to_left.astype(F32)]
    ppermute x5 -> x22, starting transfers between devices: 6.4 us -> 26.5 us  [the longest x6 8.65 us: local(): g[m] = lax.ppermute(held[m][1], 'pipe', [(stage, stage - 1)])]
    unnamed x1 -> x98, local copies, waits for them, and re-layouts: 1.34 us -> 21.3 us
    while x21 -> x0, local copies, waits for them, and re-layouts: 11.8 us -> none  [the longest x1 8.92 us: local(): final_state = lax.fori_loop(0, step_count, step_fn, initial)]
    pallas_call x0 -> x8, Pallas kernels: none -> 11.8 us  [chain_call(): pl.pallas_call(functools.partial(chain_kernel, dilation), out_shape=shape...]
  transfers between devices with their start and end apart: 8 -> 22, of which waited for: 5 -> 12; matrix products, arithmetic and copies ran while one was open for 13% -> 8% of each run, Pallas kernels for 0% -> 3%
where the time goes in v1:
time: 208 us; the launch traced here: 207 us
  waiting for transfers between devices  91.4 us (44%)
  local copies, waits for them, and re-layouts  44.1 us (21%)
  starting transfers between devices  26.5 us (13%)
  between operations  13 us (6%)
  Pallas kernels  11.8 us (6%)
  matrix products  10.7 us (5%)
  other arithmetic  9.71 us (5%)
    ppermute x3, waiting for transfers between devices, local(): to_left = lax.ppermute(sum_l, 'dp', left)  27.5 us
    unnamed x98, local copies, waits for them, and re-layouts  21.3 us
    ppermute x3, waiting for transfers between devices, local(): from_left = lax.ppermute(from_left, 'dp', right)  19.2 us
    ppermute x6, waiting for transfers between devices, local(): g[m] = lax.ppermute(held[m][1], 'pipe', [(stage, stage - 1)])  15.4 us
    ppermute x3, waiting for transfers between devices, local(): to_right = lax.ppermute(sum_r, 'dp', right)  14 us
    pallas_call x8, Pallas kernels, chain_call(): pl.pallas_call(functools.partial(chain_kernel, dilation), out_shape=shape...  11.8 us
    dynamic_update_slice x8, local copies, waits for them, and re-layouts, put(): lax.dynamic_update_slice(full, block, (first, owner(offset) * part, 0))  9.69 us
    ppermute x6, starting transfers between devices, local(): g[m] = lax.ppermute(held[m][1], 'pipe', [(stage, stage - 1)])  8.65 us
  transfers between devices with their start and end apart: 22, of which 12 were waited for; matrix products, arithmetic and copies ran while one was open for 8% of the time, Pallas kernels for 3%

profile of v1, /device:TPU:0, one launch (start us, length us, event | category | flops | bytes accessed | tf_op | source)
XLA Modules:
  0.0 207.2 jit_solution(12338336409629445774)
XLA Ops:
  7.9 1.7 fusion.30
  10.3 2.6 %broadcast_in_dim.20 = bf16[4,512,1024]{2,1,0:T(8,128)(2,1)} broadcast(bf16[]{:T(256)} %constant.94.clone.1), dimensions={} | broadcast | bytes 4194306 | tf_op jit(solution)/shard_map/broadcast_in_dim | solution.py:125
  13.8 3.1 %collective-permute-start = (bf16[4,64,1024]{2,1,0:T(8,128)(2,1)S(1)}, bf16[4,64,1024]{2,1,0:T(8,128)(2,1)S(1)}, u32[]{:S(2)}, u32[]{:S(2)}) collective-permute-start(bf16[4,64,1024]{2,1,0:T(8,128)(2,1)S(1)} %get-tuple-element.71), channel_id=1, source_target_pairs={{0,2},{2,4},{4,6},{6,7},{7,5},{5,3},{3,1},{1,0},{8,10},{10,12},{12... | collective-permute-start | bytes 1572872 | tf_op jit(solution)/shard_map/ppermute | solution.py:133
  16.9 11.8 %collective-permute-done = bf16[4,64,1024]{2,1,0:T(8,128)(2,1)S(1)} collective-permute-done((bf16[4,64,1024]{2,1,0:T(8,128)(2,1)S(1)}, bf16[4,64,1024]{2,1,0:T(8,128)(2,1)S(1)}, u32[]{:S(2)}, u32[]{:S(2)}) %collective-permute-start) | collective-permute-done | bytes 524320 | tf_op jit(solution)/shard_map/ppermute | solution.py:133
  28.7 1.8 collective-permute-start.2
  30.7 3.9 %fusion.22 = (bf16[2,512,512]{2,1,0:T(8,128)(2,1)}, bf16[2,512,512]{2,1,0:T(8,128)(2,1)}) fusion(s32[]{:T(128)S(6)} %select_n.116, bf16[2,512,512]{2,1,0:T(8,128)(2,1)S(1)} %bitcast.63, pred[512]{0:T(512)(128)(4,1)S(1)} %get-tuple-element.83, s32[]{:T(128)S(6)} %select_n.118, pred[512]{0:T(512)(128)(4,1)S(1)} %get-tuple-element.82), kind=kLoop, calls=%fused_computation.31 | loop fusion | flops 5242880 | bytes 3146760 | tf_op jit(solution)/shard_map/jit(_where)/select_n | solution.py:145
  34.6 7.4 %collective-permute-done.2 = bf16[4,64,1024]{2,1,0:T(8,128)(2,1)} collective-permute-done((bf16[4,64,1024]{2,1,0:T(8,128)(2,1)S(1)}, bf16[4,64,1024]{2,1,0:T(8,128)(2,1)}, u32[]{:S(2)}, u32[]{:S(2)}) %collective-permute-start.2) | collective-permute-done | bytes 524320 | tf_op jit(solution)/shard_map/ppermute | solution.py:133
  42.0 1.5 collective-permute-start.4
  50.9 1.9 constant_dynamic-update-slice_fusion.6
  52.8 1.9 constant_dynamic-update-slice_fusion.5
  56.2 1.9 constant_dynamic-update-slice_fusion.4
  61.8 2.7 %collective-permute-done.7 = bf16[2,64,1024]{2,1,0:T(8,128)(2,1)S(1)} collective-permute-done((bf16[2,64,1024]{2,1,0:T(8,128)(2,1)S(1)}, bf16[2,64,1024]{2,1,0:T(8,128)(2,1)S(1)}, u32[]{:S(2)}, u32[]{:S(2)}) %collective-permute-start.7) | collective-permute-done | bytes 262176 | tf_op jit(solution)/shard_map/ppermute | solution.py:138
  65.3 2.2 %slice.70 = bf16[3,512,1024]{2,1,0:T(8,128)(2,1)S(1)} slice(bf16[4,512,1024]{2,1,0:T(8,128)(2,1)} %constant_dynamic-update-slice_fusion.w_hbm), slice={[0:3], [0:512], [0:1024]} | slice | bytes 6291456 | tf_op jit(solution)/shard_map/slice | solution.py:150
  67.5 3.4 %fusion.17 = f32[1024,1024]{1,0:T(8,128)S(1)} fusion(bf16[1536,1024]{1,0:T(8,128)(2,1)S(1)} %bitcast.60, bf16[1024,512]{1,0:T(8,128)(2,1)S(1)} %bitcast.68, bf16[1024,512]{1,0:T(8,128)(2,1)S(1)} %bitcast.66, bf16[1024,512]{1,0:T(8,128)(2,1)S(1)} %bitcast.64), kind=kOutput, calls=%fused_computation.27 | convolution fusion | flops 3230662656 | bytes 10485760 | tf_op jit(solution)/shard_map/dot_general | solution.py:151
  74.5 1.8 convolution_bitcast_fusion
  88.5 1.6 collective-permute-start.9
  102.0 15.4 %collective-permute-done.10.g_hbm = bf16[512,512]{1,0:T(8,128)(2,1)} collective-permute-done((bf16[512,512]{1,0:T(8,128)(2,1)}, bf16[512,512]{1,0:T(8,128)(2,1)}, u32[]{:S(2)}, u32[]{:S(2)}) %collective-permute-start.10) | collective-permute-done | bytes 524320 | tf_op jit(solution)/shard_map/ppermute | solution.py:176
  122.1 5.4 %shard_map.97 = (bf16[512,1024]{1,0:T(8,128)(2,1)S(1)}, bf16[512,512]{1,0:T(8,128)(2,1)}, bf16[512,512]{1,0:T(8,128)(2,1)S(1)}) custom-call(s32[1]{0:T(128)} %bitcast.flags, bf16[512,512]{1,0:T(8,128)(2,1)} %collective-permute-done.10.g_hbm, f32[512,512]{1,0:T(8,128)S(1)} %copy-done.19, ...), custom_call_target="tpu_custom_call", output_to_operand_aliasing={{0}: (6, {}), {1}: (7, {}), {2}: (8, {})} | custom-call | flops 2000000000 | bytes 8388608 | tf_op jit(solution)/shard_map/pallas_call | solution.py:82
  128.4 5.4 %shard_map.101 = (bf16[512,1024]{1,0:T(8,128)(2,1)S(1)}, bf16[512,512]{1,0:T(8,128)(2,1)}, bf16[512,512]{1,0:T(8,128)(2,1)S(1)}) custom-call(s32[1]{0:T(128)} %bitcast.flags, bf16[512,512]{1,0:T(8,128)(2,1)} %collective-permute-done.13.g_hbm, f32[512,512]{1,0:T(8,128)S(1)} %copy-done.7, ...), custom_call_target="tpu_custom_call", output_to_operand_aliasing={{0}: (6, {}), {1}: (7, {}), {2}: (8, {})} | custom-call | flops 2000000000 | bytes 8388608 | tf_op jit(solution)/shard_map/pallas_call | solution.py:82
  133.9 3.9 %convolution_convert_fusion = bf16[1536,1024]{1,0:T(8,128)(2,1)S(1)} fusion(bf16[512,1024]{1,0:T(8,128)(2,1)S(1)} %get-tuple-element.49, bf16[512,1024]{1,0:T(8,128)(2,1)S(1)} %get-tuple-element.48, bf16[1024,512]{1,0:T(8,128)(2,1)S(1)} %bitcast.69, bf16[1024,512]{1,0:T(8,128)(2,1)S(1)} %bitcast.67, bf16[1024,512]{1,0:T(8,128)(2,1)S(1)} %bitcast.65), kind=kOutput, calls=%fused_computation.1 | convolution fusion | flops 3236429824 | bytes 8388608 | tf_op jit(solution)/shard_map/dot_general | solution.py:183
  137.8 1.6 fusion.14
  139.9 1.6 collective-permute-start.14
  141.6 6.0 %collective-permute-done.14 = bf16[2,64,1024]{2,1,0:T(8,128)(2,1)S(1)} collective-permute-done((bf16[2,64,1024]{2,1,0:T(8,128)(2,1)S(1)}, bf16[2,64,1024]{2,1,0:T(8,128)(2,1)S(1)}, u32[]{:S(2)}, u32[]{:S(2)}) %collective-permute-start.14) | collective-permute-done | bytes 262176 | tf_op jit(solution)/shard_map/ppermute | solution.py:190
  147.6 1.6 collective-permute-start.15
  149.3 10.7 %collective-permute-done.15 = bf16[4,64,1024]{2,1,0:T(8,128)(2,1)S(1)} collective-permute-done((bf16[4,64,1024]{2,1,0:T(8,128)(2,1)S(1)}, bf16[4,64,1024]{2,1,0:T(8,128)(2,1)S(1)}, u32[]{:S(2)}, u32[]{:S(2)}) %collective-permute-start.15) | collective-permute-done | bytes 524320 | tf_op jit(solution)/shard_map/ppermute | solution.py:200
  160.1 1.6 collective-permute-start.16
  162.2 5.9 %collective-permute-done.18 = bf16[2,64,1024]{2,1,0:T(8,128)(2,1)S(1)} collective-permute-done((bf16[2,64,1024]{2,1,0:T(8,128)(2,1)S(1)}, bf16[2,64,1024]{2,1,0:T(8,128)(2,1)S(1)}, u32[]{:S(2)}, u32[]{:S(2)}) %collective-permute-start.18) | collective-permute-done | bytes 262176 | tf_op jit(solution)/shard_map/ppermute | solution.py:191
  168.2 3.4 %collective-permute-done.16 = bf16[4,64,1024]{2,1,0:T(8,128)(2,1)S(1)} collective-permute-done((bf16[4,64,1024]{2,1,0:T(8,128)(2,1)S(1)}, bf16[4,64,1024]{2,1,0:T(8,128)(2,1)S(1)}, u32[]{:S(2)}, u32[]{:S(2)}) %collective-permute-start.16) | collective-permute-done | bytes 524320 | tf_op jit(solution)/shard_map/ppermute | solution.py:200
  172.4 11.3 %collective-permute-done.19 = bf16[4,64,1024]{2,1,0:T(8,128)(2,1)S(1)} collective-permute-done((bf16[4,64,1024]{2,1,0:T(8,128)(2,1)S(1)}, bf16[4,64,1024]{2,1,0:T(8,128)(2,1)S(1)}, u32[]{:S(2)}, u32[]{:S(2)}) %collective-permute-start.19) | collective-permute-done | bytes 524320 | tf_op jit(solution)/shard_map/ppermute | solution.py:201
  186.0 9.8 %collective-permute-done.20 = bf16[4,64,1024]{2,1,0:T(8,128)(2,1)S(1)} collective-permute-done((bf16[4,64,1024]{2,1,0:T(8,128)(2,1)S(1)}, bf16[4,64,1024]{2,1,0:T(8,128)(2,1)S(1)}, u32[]{:S(2)}, u32[]{:S(2)}) %collective-permute-start.20) | collective-permute-done | bytes 524320 | tf_op jit(solution)/shard_map/ppermute | solution.py:201
  196.6 2.3 %maximum_bitcast_fusion = bf16[1,2,1,512,512]{4,3,2,1,0:T(8,128)(2,1)} fusion(bf16[1,512,512]{2,1,0:T(8,128)(2,1)} %bitcast.35, bf16[1,512,512]{2,1,0:T(8,128)(2,1)} %bitcast.33), kind=kLoop, calls=%fused_computation.32 | loop fusion | flops 524288 | bytes 2097152
  198.9 6.4 %collective-permute-done.21 = bf16[4,64,1024]{2,1,0:T(8,128)(2,1)S(1)} collective-permute-done((bf16[4,64,1024]{2,1,0:T(8,128)(2,1)S(1)}, bf16[4,64,1024]{2,1,0:T(8,128)(2,1)S(1)}, u32[]{:S(2)}, u32[]{:S(2)}) %collective-permute-start.21) | collective-permute-done | bytes 524320 | tf_op jit(solution)/shard_map/ppermute | solution.py:201
  (161 shorter events, 50.7 us)
Async XLA Ops:
  0.6 12.3 %copy-start.47 = (bf16[1,64,3,1024]{3,1,2,0:T(8,128)(2,1)S(1)}, bf16[1,64,3,1024]{3,1,2,0:T(8,128)(2,1)}, u32[]{:S(2)}) copy-start(bf16[1,64,3,1024]{3,1,2,0:T(8,128)(2,1)} %param.12) | copy-start | bytes 1179652
  0.6 12.2 %copy-start.48 = (bf16[1,64,1024]{2,1,0:T(8,128)(2,1)S(1)}, bf16[1,64,1024]{2,1,0:T(8,128)(2,1)}, u32[]{:S(2)}) copy-start(bf16[1,64,1024]{2,1,0:T(8,128)(2,1)} %param.13) | copy-start | bytes 393220
  0.7 30.1 %copy-start.40 = (bf16[1,2,1,512,512]{4,3,2,1,0:T(8,128)(2,1)S(1)}, bf16[1,2,1,512,512]{4,3,2,1,0:T(8,128)(2,1)}, u32[]{:S(2)}) copy-start(bf16[1,2,1,512,512]{4,3,2,1,0:T(8,128)(2,1)} %param.9) | copy-start | bytes 3145732
  10.3 33.8 %copy-start.39 = (bf16[2,1,512,512]{3,2,1,0:T(8,128)(2,1)S(1)}, bf16[2,1,512,512]{3,2,1,0:T(8,128)(2,1)}, u32[]{:S(2)}) copy-start(bf16[2,1,512,512]{3,2,1,0:T(8,128)(2,1)} %param.10) | copy-start | bytes 3145732
  13.8 14.9 %collective-permute-start = (bf16[4,64,1024]{2,1,0:T(8,128)(2,1)S(1)}, bf16[4,64,1024]{2,1,0:T(8,128)(2,1)S(1)}, u32[]{:S(2)}, u32[]{:S(2)}) collective-permute-start(bf16[4,64,1024]{2,1,0:T(8,128)(2,1)S(1)} %get-tuple-element.71), channel_id=1, source_target_pairs={{0,2},{2,4},{4,6},{6,7},{7,5},{5,3},{3,1},{1,0},{8,10},{10,12},{12... | collective-permute-start | bytes 1572872 | tf_op jit(solution)/shard_map/ppermute | solution.py:133
  16.9 13.7 %collective-permute-start.1 = (bf16[4,64,1024]{2,1,0:T(8,128)(2,1)S(1)}, bf16[4,64,1024]{2,1,0:T(8,128)(2,1)}, u32[]{:S(2)}, u32[]{:S(2)}) collective-permute-start(bf16[4,64,1024]{2,1,0:T(8,128)(2,1)S(1)} %get-tuple-element.71), channel_id=1, source_target_pairs={{2,0},{4,2},{6,4},{7,6},{5,7},{3,5},{1,3},{0,1},{10,8},{12,10},{14... | collective-permute-start | bytes 1572872 | tf_op jit(solution)/shard_map/ppermute | solution.py:134
  28.7 13.3 %collective-permute-start.2 = (bf16[4,64,1024]{2,1,0:T(8,128)(2,1)S(1)}, bf16[4,64,1024]{2,1,0:T(8,128)(2,1)}, u32[]{:S(2)}, u32[]{:S(2)}) collective-permute-start(bf16[4,64,1024]{2,1,0:T(8,128)(2,1)S(1)} %collective-permute-done), channel_id=1, source_target_pairs={{0,2},{2,4},{4,6},{6,7},{7,5},{5,3},{3,1},{1,0},{8,10},{10,12},{12... | collective-permute-start | bytes 1572872 | tf_op jit(solution)/shard_map/ppermute | solution.py:133
  30.6 13.0 %collective-permute-start.3 = (bf16[4,64,1024]{2,1,0:T(8,128)(2,1)}, bf16[4,64,1024]{2,1,0:T(8,128)(2,1)}, u32[]{:S(2)}, u32[]{:S(2)}) collective-permute-start(bf16[4,64,1024]{2,1,0:T(8,128)(2,1)} %collective-permute-done.1), channel_id=1, source_target_pairs={{2,0},{4,2},{6,4},{7,6},{5,7},{3,5},{1,3},{0,1},{10,8},{12,10},{14... | collective-permute-start | bytes 1572872 | tf_op jit(solution)/shard_map/ppermute | solution.py:134
  42.0 12.6 %collective-permute-start.4 = (bf16[4,64,1024]{2,1,0:T(8,128)(2,1)}, bf16[4,64,1024]{2,1,0:T(8,128)(2,1)S(1)}, u32[]{:S(2)}, u32[]{:S(2)}) collective-permute-start(bf16[4,64,1024]{2,1,0:T(8,128)(2,1)} %collective-permute-done.2), channel_id=1, source_target_pairs={{0,2},{2,4},{4,6},{6,7},{7,5},{5,3},{3,1},{1,0},{8,10},{10,12},{12... | collective-permute-start | bytes 1572872 | tf_op jit(solution)/shard_map/ppermute | solution.py:133
  43.6 14.5 %collective-permute-start.5 = (bf16[4,64,1024]{2,1,0:T(8,128)(2,1)}, bf16[4,64,1024]{2,1,0:T(8,128)(2,1)S(1)}, u32[]{:S(2)}, u32[]{:S(2)}) collective-permute-start(bf16[4,64,1024]{2,1,0:T(8,128)(2,1)} %collective-permute-done.3), channel_id=1, source_target_pairs={{2,0},{4,2},{6,4},{7,6},{5,7},{3,5},{1,3},{0,1},{10,8},{12,10},{14... | collective-permute-start | bytes 1572872 | tf_op jit(solution)/shard_map/ppermute | solution.py:134
  54.7 6.4 %collective-permute-start.6 = (bf16[2,64,1024]{2,1,0:T(8,128)(2,1)S(1)}, bf16[2,64,1024]{2,1,0:T(8,128)(2,1)S(1)}, u32[]{:S(2)}, u32[]{:S(2)}) collective-permute-start(bf16[2,64,1024]{2,1,0:T(8,128)(2,1)S(1)} %slice.66), channel_id=1, source_target_pairs={{0,2},{2,4},{4,6},{6,7},{7,5},{5,3},{3,1},{1,0},{8,10},{10,12},{12... | collective-permute-start | bytes 786440 | tf_op jit(solution)/shard_map/ppermute | solution.py:137
  58.1 6.4 %collective-permute-start.7 = (bf16[2,64,1024]{2,1,0:T(8,128)(2,1)S(1)}, bf16[2,64,1024]{2,1,0:T(8,128)(2,1)S(1)}, u32[]{:S(2)}, u32[]{:S(2)}) collective-permute-start(bf16[2,64,1024]{2,1,0:T(8,128)(2,1)S(1)} %slice.67), channel_id=1, source_target_pairs={{2,0},{4,2},{6,4},{7,6},{5,7},{3,5},{1,3},{0,1},{10,8},{12,10},{14... | collective-permute-start | bytes 786440 | tf_op jit(solution)/shard_map/ppermute | solution.py:138
  59.6 7.9 %copy-start.41 = (bf16[1,2,1,512,512]{4,3,2,1,0:T(8,128)(2,1)S(1)}, bf16[1,2,1,512,512]{4,3,2,1,0:T(8,128)(2,1)}, u32[]{:S(2)}) copy-start(bf16[1,2,1,512,512]{4,3,2,1,0:T(8,128)(2,1)} %param.9) | copy-start | bytes 3145732
  59.6 7.9 %copy-start.43 = (bf16[2,512,512]{2,1,0:T(8,128)(2,1)S(1)}, bf16[2,512,512]{2,1,0:T(8,128)(2,1)}, u32[]{:S(2)}) copy-start(bf16[2,512,512]{2,1,0:T(8,128)(2,1)} %get-tuple-element.69) | copy-start | bytes 3145732
  59.6 7.9 %copy-start.45 = (bf16[2,512,512]{2,1,0:T(8,128)(2,1)S(1)}, bf16[2,512,512]{2,1,0:T(8,128)(2,1)}, u32[]{:S(2)}) copy-start(bf16[2,512,512]{2,1,0:T(8,128)(2,1)} %get-tuple-element.70) | copy-start | bytes 3145732
  73.3 7.0 %copy-start = (f32[512,512]{1,0:T(8,128)}, f32[512,512]{1,0:T(8,128)S(1)}, u32[]{:S(2)}) copy-start(f32[512,512]{1,0:T(8,128)S(1)} %get-tuple-element.64.a1_hbm) | copy-start | bytes 3145732
  77.8 5.1 %collective-permute-start.8 = (bf16[512,512]{1,0:T(8,128)(2,1)}, bf16[512,512]{1,0:T(8,128)(2,1)}, u32[]{:S(2)}, u32[]{:S(2)}) collective-permute-start(bf16[512,512]{1,0:T(8,128)(2,1)} %get-tuple-element.28._ig), channel_id=1, source_target_pairs={{24,16},{25,17},{26,18},{27,19},{28,20},{29,21},{30,22},{31,23}} | collective-permute-start | bytes 1572872 | tf_op jit(solution)/shard_map/ppermute | solution.py:176
  81.4 8.7 %collective-permute-start.11 = (bf16[512,512]{1,0:T(8,128)(2,1)}, bf16[512,512]{1,0:T(8,128)(2,1)}, u32[]{:S(2)}, u32[]{:S(2)}) collective-permute-start(bf16[512,512]{1,0:T(8,128)(2,1)} %get-tuple-element.38._ig), channel_id=1, source_target_pairs={{24,16},{25,17},{26,18},{27,19},{28,20},{29,21},{30,22},{31,23}} | collective-permute-start | bytes 1572872 | tf_op jit(solution)/shard_map/ppermute | solution.py:176
  88.5 4.0 %collective-permute-start.9 = (bf16[512,512]{1,0:T(8,128)(2,1)}, bf16[512,512]{1,0:T(8,128)(2,1)}, u32[]{:S(2)}, u32[]{:S(2)}) collective-permute-start(bf16[512,512]{1,0:T(8,128)(2,1)} %get-tuple-element.31._ig), channel_id=1, source_target_pairs={{16,8},{17,9},{18,10},{19,11},{20,12},{21,13},{22,14},{23,15}} | collective-permute-start | bytes 1572872 | tf_op jit(solution)/shard_map/ppermute | solution.py:176
  91.0 8.5 %collective-permute-start.12 = (bf16[512,512]{1,0:T(8,128)(2,1)}, bf16[512,512]{1,0:T(8,128)(2,1)}, u32[]{:S(2)}, u32[]{:S(2)}) collective-permute-start(bf16[512,512]{1,0:T(8,128)(2,1)} %get-tuple-element.41._ig), channel_id=1, source_target_pairs={{16,8},{17,9},{18,10},{19,11},{20,12},{21,13},{22,14},{23,15}} | collective-permute-start | bytes 1572872 | tf_op jit(solution)/shard_map/ppermute | solution.py:176
  98.1 19.3 %collective-permute-start.10 = (bf16[512,512]{1,0:T(8,128)(2,1)}, bf16[512,512]{1,0:T(8,128)(2,1)}, u32[]{:S(2)}, u32[]{:S(2)}) collective-permute-start(bf16[512,512]{1,0:T(8,128)(2,1)} %get-tuple-element.34._ig), channel_id=1, source_target_pairs={{8,0},{9,1},{10,2},{11,3},{12,4},{13,5},{14,6},{15,7}} | collective-permute-start | bytes 1572872 | tf_op jit(solution)/shard_map/ppermute | solution.py:176
  100.7 27.7 %collective-permute-start.13 = (bf16[512,512]{1,0:T(8,128)(2,1)}, bf16[512,512]{1,0:T(8,128)(2,1)}, u32[]{:S(2)}, u32[]{:S(2)}) collective-permute-start(bf16[512,512]{1,0:T(8,128)(2,1)} %get-tuple-element.44._ig), channel_id=1, source_target_pairs={{8,0},{9,1},{10,2},{11,3},{12,4},{13,5},{14,6},{15,7}} | collective-permute-start | bytes 1572872 | tf_op jit(solution)/shard_map/ppermute | solution.py:176
  122.1 6.3 %copy-start.7 = (f32[512,512]{1,0:T(8,128)S(1)}, f32[512,512]{1,0:T(8,128)}, u32[]{:S(2)}) copy-start(f32[512,512]{1,0:T(8,128)} %copy-done.4) | copy-start | bytes 3145732
  122.1 6.3 %copy-start.25 = (bf16[512,512]{1,0:T(8,128)(2,1)S(1)}, bf16[512,512]{1,0:T(8,128)(2,1)}, u32[]{:S(2)}) copy-start(bf16[512,512]{1,0:T(8,128)(2,1)} %copy-done.24) | copy-start | bytes 1572868
  139.9 7.6 %collective-permute-start.14 = (bf16[2,64,1024]{2,1,0:T(8,128)(2,1)S(1)}, bf16[2,64,1024]{2,1,0:T(8,128)(2,1)S(1)}, u32[]{:S(2)}, u32[]{:S(2)}) collective-permute-start(bf16[2,64,1024]{2,1,0:T(8,128)(2,1)S(1)} %get-tuple-element.57), channel_id=1, source_target_pairs={{0,2},{2,4},{4,6},{6,7},{7,5},{5,3},{3,1},{1,0},{8,10},{10,12},{12... | collective-permute-start | bytes 786440 | tf_op jit(solution)/shard_map/ppermute | solution.py:190
  147.6 12.3 %collective-permute-start.15 = (bf16[4,64,1024]{2,1,0:T(8,128)(2,1)S(1)}, bf16[4,64,1024]{2,1,0:T(8,128)(2,1)S(1)}, u32[]{:S(2)}, u32[]{:S(2)}) collective-permute-start(bf16[4,64,1024]{2,1,0:T(8,128)(2,1)S(1)} %add_convert_fusion.5), channel_id=1, source_target_pairs={{0,2},{2,4},{4,6},{6,7},{7,5},{5,3},{3,1},{1,0},{8,10},{10,12},{12... | collective-permute-start | bytes 1572872 | tf_op jit(solution)/shard_map/ppermute | solution.py:200
  160.1 11.4 %collective-permute-start.16 = (bf16[4,64,1024]{2,1,0:T(8,128)(2,1)S(1)}, bf16[4,64,1024]{2,1,0:T(8,128)(2,1)S(1)}, u32[]{:S(2)}, u32[]{:S(2)}) collective-permute-start(bf16[4,64,1024]{2,1,0:T(8,128)(2,1)S(1)} %add_convert_fusion.4), channel_id=1, source_target_pairs={{0,2},{2,4},{4,6},{6,7},{7,5},{5,3},{3,1},{1,0},{8,10},{10,12},{12... | collective-permute-start | bytes 1572872 | tf_op jit(solution)/shard_map/ppermute | solution.py:200
  161.8 6.4 %collective-permute-start.18 = (bf16[2,64,1024]{2,1,0:T(8,128)(2,1)S(1)}, bf16[2,64,1024]{2,1,0:T(8,128)(2,1)S(1)}, u32[]{:S(2)}, u32[]{:S(2)}) collective-permute-start(bf16[2,64,1024]{2,1,0:T(8,128)(2,1)S(1)} %get-tuple-element.58), channel_id=1, source_target_pairs={{2,0},{4,2},{6,4},{7,6},{5,7},{3,5},{1,3},{0,1},{10,8},{12,10},{14... | collective-permute-start | bytes 786440 | tf_op jit(solution)/shard_map/ppermute | solution.py:191
  171.8 11.9 %collective-permute-start.19 = (bf16[4,64,1024]{2,1,0:T(8,128)(2,1)S(1)}, bf16[4,64,1024]{2,1,0:T(8,128)(2,1)S(1)}, u32[]{:S(2)}, u32[]{:S(2)}) collective-permute-start(bf16[4,64,1024]{2,1,0:T(8,128)(2,1)S(1)} %get-tuple-element.56), channel_id=1, source_target_pairs={{2,0},{4,2},{6,4},{7,6},{5,7},{3,5},{1,3},{0,1},{10,8},{12,10},{14... | collective-permute-start | bytes 1572872 | tf_op jit(solution)/shard_map/ppermute | solution.py:201
  183.9 11.9 %collective-permute-start.20 = (bf16[4,64,1024]{2,1,0:T(8,128)(2,1)S(1)}, bf16[4,64,1024]{2,1,0:T(8,128)(2,1)S(1)}, u32[]{:S(2)}, u32[]{:S(2)}) collective-permute-start(bf16[4,64,1024]{2,1,0:T(8,128)(2,1)S(1)} %add_convert_fusion.1), channel_id=1, source_target_pairs={{2,0},{4,2},{6,4},{7,6},{5,7},{3,5},{1,3},{0,1},{10,8},{12,10},{14... | collective-permute-start | bytes 1572872 | tf_op jit(solution)/shard_map/ppermute | solution.py:201
  184.5 14.4 %collective-permute-start.17 = (bf16[4,64,1024]{2,1,0:T(8,128)(2,1)S(1)}, bf16[4,64,1024]{2,1,0:T(8,128)(2,1)S(1)}, u32[]{:S(2)}, u32[]{:S(2)}) collective-permute-start(bf16[4,64,1024]{2,1,0:T(8,128)(2,1)S(1)} %get-tuple-element.55), channel_id=1, source_target_pairs={{0,2},{2,4},{4,6},{6,7},{7,5},{5,3},{3,1},{1,0},{8,10},{10,12},{12... | collective-permute-start | bytes 1572872 | tf_op jit(solution)/shard_map/ppermute | solution.py:200
  196.0 9.2 %collective-permute-start.21 = (bf16[4,64,1024]{2,1,0:T(8,128)(2,1)S(1)}, bf16[4,64,1024]{2,1,0:T(8,128)(2,1)S(1)}, u32[]{:S(2)}, u32[]{:S(2)}) collective-permute-start(bf16[4,64,1024]{2,1,0:T(8,128)(2,1)S(1)} %add_convert_fusion), channel_id=1, source_target_pairs={{2,0},{4,2},{6,4},{7,6},{5,7},{3,5},{1,3},{0,1},{10,8},{12,10},{14... | collective-permute-start | bytes 1572872 | tf_op jit(solution)/shard_map/ppermute | solution.py:201
  (39 other events, 89.8 us)

commit v2 on v1

v2 whole, which is shorter than its diff:
```python
import functools

import jax
import jax.numpy as jnp
from jax import lax
from jax.experimental import pallas as pl
from jax.experimental.pallas import tpu as pltpu
from jax.sharding import PartitionSpec as P

F32 = jnp.float32
BF16 = jnp.bfloat16
NT = (((1,), (1,)), ((), ()))
VMEM_BYTES = 56 * 2**20
ANY = pl.BlockSpec(memory_space=pl.ANY)
SMEM = pl.BlockSpec(memory_space=pltpu.SMEM)


def ring_pairs(count):
    order = list(range(0, count, 2)) + list(range(count - 1 - count % 2, 0, -2))
    right = [(order[i], order[(i + 1) % count]) for i in range(count)]
    return right, [(b, a) for a, b in right]


def starter(sems):
    number = iter(range(sems.shape[0]))

    def start(source, target):
        copy = pltpu.make_async_copy(source, target, sems.at[next(number)])
        copy.start()
        return copy

    return start


def forward_kernel(pieces, owners, taps_hbm, skip_hbm, *refs):
    shards, refs = refs[: len(pieces)], refs[len(pieces) :]
    a1_hbm, a2_hbm, hs_hbm, hid_hbm, w_hbm, taps, skip, w, a1, a2, hs, hid, sems = refs
    samples, channels = skip.shape
    start = starter(sems)
    get_taps = start(taps_hbm, taps)
    get_conv, get_mix = [], []
    for (slot, first), shard in zip(pieces, shards):
        count, part = shard.shape[:2]
        offset = pl.multiple_of(owners[slot] * part, part)
        for k in range(count):
            tap = first + k
            copy = start(shard.at[k], w.at[pl.ds(tap * channels + offset, part), :])
            (get_mix if tap == 3 else get_conv).append(copy)
    get_skip = start(skip_hbm, skip)
    get_taps.wait()
    for copy in get_conv:
        copy.wait()
    chunk = samples // 2
    puts = []
    for at in range(0, samples, chunk):
        rows = slice(at, at + chunk)
        pre = jnp.dot(taps[rows, :], w[: 3 * channels, :], preferred_element_type=F32)
        filt = jnp.tanh(pre[:, :channels])
        gate = jax.nn.sigmoid(pre[:, channels:])
        hid[rows, :] = (filt * gate).astype(BF16)
        a1[rows, :] = gate * (1.0 - filt * filt)
        a2[rows, :] = filt * gate * (1.0 - gate)
        if not puts:
            get_skip.wait()
            for copy in get_mix:
                copy.wait()
            puts.append(start(w, w_hbm))
        hs[rows, :] = lax.dot_general(
            skip[rows, :], w[3 * channels :, channels:], NT, preferred_element_type=F32
        )
        for source, target in ((a1, a1_hbm), (a2, a2_hbm), (hs, hs_hbm), (hid, hid_hbm)):
            puts.append(start(source.at[rows, :], target.at[rows, :]))
    for copy in puts:
        copy.wait()


def forward_call(owners, taps, skip, pieces, shards):
    samples, channels = skip.shape
    tile = (samples, channels)
    full = (4 * channels, 2 * channels)
    return pl.pallas_call(
        functools.partial(forward_kernel, pieces),
        out_shape=[jax.ShapeDtypeStruct(tile, F32)] * 3
        + [jax.ShapeDtypeStruct(tile, BF16), jax.ShapeDtypeStruct(full, BF16)],
        in_specs=[SMEM] + [ANY] * (2 + len(shards)),
        out_specs=[ANY] * 5,
        scratch_shapes=[
            pltpu.VMEM(taps.shape, BF16),
            pltpu.VMEM(tile, BF16),
            pltpu.VMEM(full, BF16),
            pltpu.VMEM(tile, F32),
            pltpu.VMEM(tile, F32),
            pltpu.VMEM(tile, F32),
            pltpu.VMEM(tile, BF16),
            pltpu.SemaphoreType.DMA((2 + sum(s.shape[0] for s in shards) + 9,)),
        ],
        compiler_params=pltpu.CompilerParams(vmem_limit_bytes=VMEM_BYTES),
        cost_estimate=pl.CostEstimate(
            flops=8 * samples * channels * channels * 2, bytes_accessed=16 * 2**20, transcendentals=0
        ),
    )(owners, taps, skip, *shards)


def chain_kernel(dilation, held, flags, g_hbm, hs_hbm, a1_hbm, a2_hbm, w_hbm, *refs):
    pg_hbm, ig_hbm, gk_hbm, g, hs, a1, a2, wm, wc, pg, ig, bt, sems = refs[held:]
    samples, channels = g.shape
    padding = bt.shape[1] - samples

    @pl.when(flags[0] == 1)
    def _():
        start = starter(sems)
        get_g = start(g_hbm, g)
        get_wm = start(w_hbm.at[pl.ds(3 * channels, channels), pl.ds(0, channels)], wm)
        get_hs = start(hs_hbm, hs)
        get_a1 = start(a1_hbm, a1)
        get_a2 = start(a2_hbm, a2)
        get_wc = [start(w_hbm.at[pl.ds(k * channels, channels), :], wc.at[k]) for k in range(3)]
        for k in (1, 2):
            bt[k, samples:, :] = jnp.zeros((padding, channels), F32)
        get_g.wait()
        puts = [start(g, gk_hbm)]
        get_wm.wait()
        get_hs.wait()
        chunk = samples // 2
        for at in range(samples - chunk, -1, -chunk):
            rows = slice(at, at + chunk)
            hid = lax.dot_general(g[rows, :], wm[...], NT, preferred_element_type=F32) + hs[rows, :]
            if at == samples - chunk:
                get_a1.wait()
                get_a2.wait()
            pg[rows, :channels] = (hid * a1[rows, :]).astype(BF16)
            pg[rows, channels:] = (hid * a2[rows, :]).astype(BF16)
            for k in range(3):
                if at == samples - chunk:
                    get_wc[k].wait()
                bt[k, rows, :] = lax.dot_general(pg[rows, :], wc[k], NT, preferred_element_type=F32)
            piece = 64
            for first in range(at + chunk - piece, at - 1, -piece):
                last = first + piece
                total = g[first:last, :].astype(F32) + bt[0, first:last, :]
                total = total + bt[1, first + dilation : last + dilation, :]
                total = total + bt[2, first + 2 * dilation : last + 2 * dilation, :]
                ig[first:last, :] = total.astype(BF16)
            puts.append(start(ig.at[rows, :], ig_hbm.at[rows, :]))
            puts.append(start(pg.at[rows, :], pg_hbm.at[rows, :]))
        for copy in puts:
            copy.wait()


def chain_call(dilation, flags, g, hs, a1, a2, w_full, held, padding):
    samples, channels = g.shape
    tile = (samples, channels)
    return pl.pallas_call(
        functools.partial(chain_kernel, dilation, len(held)),
        out_shape=[
            jax.ShapeDtypeStruct((samples, 2 * channels), BF16),
            jax.ShapeDtypeStruct(tile, BF16),
            jax.ShapeDtypeStruct(tile, BF16),
        ],
        in_specs=[SMEM] + [ANY] * (5 + len(held)),
        out_specs=[ANY] * 3,
        scratch_shapes=[
            pltpu.VMEM(tile, BF16),
            pltpu.VMEM(tile, F32),
            pltpu.VMEM(tile, F32),
            pltpu.VMEM(tile, F32),
            pltpu.VMEM((channels, channels), BF16),
            pltpu.VMEM((3, channels, 2 * channels), BF16),
            pltpu.VMEM((samples, 2 * channels), BF16),
            pltpu.VMEM(tile, BF16),
            pltpu.VMEM((3, samples + padding, channels), F32),
            pltpu.SemaphoreType.DMA((13,)),
        ],
        input_output_aliases={6 + i: i for i in range(len(held))},
        compiler_params=pltpu.CompilerParams(vmem_limit_bytes=VMEM_BYTES),
        cost_estimate=pl.CostEstimate(
            flops=8 * samples * channels * channels, bytes_accessed=8 * 2**20, transcendentals=0
        ),
    )(flags, g, hs, a1, a2, w_full, *held)


def local(x_ckpt, top_cot, skip_cot, w_conv, w_mix):
    sections = lax.axis_size("pipe")
    section = lax.axis_index("pipe")
    replicas = lax.axis_size("dp")
    replica = lax.axis_index("dp")
    micro, seqs, samples, channels = x_ckpt.shape[1:]
    rows = micro * seqs * samples
    block = seqs * samples
    part = w_conv.shape[1]
    half = replicas // 2
    dilation = jnp.left_shift(jnp.int32(1), section)
    right, left = ring_pairs(replicas)
    place = jnp.where(replica % 2 == 0, replica // 2, replicas - 1 - replica // 2)

    def owner(offset):
        at = lax.rem(place + (offset + replicas), replicas)
        return jnp.where(at < half, 2 * at, 2 * (replicas - 1 - at) + 1)

    conv = w_conv[0].transpose(1, 0, 2)
    conv_r, conv_l, mix_r, mix_l = conv, conv, w_mix, w_mix
    pieces, shards = [(0, 0), (0, 3)], [conv, w_mix]
    offsets = [0]

    def keep(offset, *blocks):
        offsets.append(offset)
        for first, shard in blocks:
            pieces.append((len(offsets) - 1, first))
            shards.append(shard)

    for step in range(1, half):
        conv_r = lax.ppermute(conv_r, "dp", right)
        conv_l = lax.ppermute(conv_l, "dp", left)
        mix_r = lax.ppermute(mix_r, "dp", right)
        mix_l = lax.ppermute(mix_l, "dp", left)
        keep(-step, (0, conv_r), (3, mix_r))
        keep(step, (0, conv_l), (3, mix_l))
    conv_r = lax.ppermute(conv_r[:2], "dp", right)
    conv_l = lax.ppermute(conv_l[2:], "dp", left)
    mix_l = lax.ppermute(mix_l, "dp", left)
    keep(half, (0, conv_r), (2, conv_l), (3, mix_l))
    owners = jnp.stack([owner(offset) for offset in offsets])

    x_rows = x_ckpt[0].reshape(micro * seqs, samples, channels)
    positions = lax.broadcasted_iota(jnp.int32, (1, samples, 1), 1)
    taps = [x_rows]
    for k in (1, 2):
        rolled = jnp.roll(x_rows, k * dilation, axis=1)
        taps.append(jnp.where(positions >= k * dilation, rolled, jnp.zeros_like(rolled)))
    taps = jnp.concatenate(taps, axis=2).reshape(micro, block, 3 * channels)
    skip = skip_cot.reshape(micro, block, channels)
    g = list(top_cot.reshape(micro, block, channels))
    padding = max(16, 2 * 2 ** (sections - 1))

    hidden, held, ready = [], [()] * micro, []
    for m in range(micro):
        a1, a2, hs, hid, w_full = forward_call(owners, taps[m], skip[m], pieces, shards)
        hidden.append(hid)
        ready.append((hs, a1, a2, w_full))
    for stage in range(sections - 1, -1, -1):
        flags = (section == stage).astype(jnp.int32).reshape(1)
        for m in range(micro):
            held[m] = chain_call(2**stage, flags, g[m], *ready[m], held[m], padding)
            if stage:
                g[m] = lax.ppermute(held[m][1], "pipe", [(stage, stage - 1)])

    pre_grad = jnp.concatenate([h[0] for h in held], axis=0)
    cot = jnp.stack([h[1] for h in held], axis=0)
    g_all = jnp.concatenate([h[2] for h in held], axis=0)
    pair = jnp.concatenate([g_all, skip.reshape(rows, channels)], axis=1)
    over_rows = (((0,), (0,)), ((), ()))
    conv_term = lax.dot_general(
        taps.reshape(rows, 3 * channels), pre_grad, over_rows, preferred_element_type=F32
    ).astype(BF16)
    mix_term = lax.dot_general(
        jnp.concatenate(hidden, axis=0), pair, over_rows, preferred_element_type=F32
    ).astype(BF16)
    terms = jnp.concatenate([conv_term, mix_term], axis=0).reshape(4, channels, 2 * channels)

    def term(offset, first):
        return lax.dynamic_slice(terms, (first, owner(offset) * part, 0), (2, part, 2 * channels))

    def add(mine, theirs):
        if theirs is None:
            return mine
        return (mine.astype(F32) + theirs.astype(F32)).astype(BF16)

    sums = {(1, 0): None, (1, 2): None, (-1, 0): None, (-1, 2): None}
    for dist in range(half, 0, -1):
        for way, first in ((1, 0), (-1, 2), (1, 2), (-1, 0)):
            if dist == half and (way, first) in ((1, 2), (-1, 0)):
                continue
            message = add(term(way * dist, first), sums[way, first])
            sums[way, first] = lax.ppermute(message, "dp", right if way == 1 else left)
    share = [
        term(0, first).astype(F32) + sums[1, first].astype(F32) + sums[-1, first].astype(F32)
        for first in (0, 2)
    ]
    share_conv = jnp.concatenate([share[0], share[1][:1]], axis=0)
    return (
        cot.reshape(1, micro, seqs, samples, channels),
        share_conv.transpose(1, 0, 2)[None],
        share[1][1][None],
    )


def solution(mesh):
    placed = (
        P("pipe", None, "dp", None, None),
        P(None, "dp", None, None),
        P(None, "dp", None, None),
        P("pipe", "dp", None, None),
        P("pipe", "dp", None),
    )
    return jax.shard_map(
        local,
        mesh=mesh,
        in_specs=placed,
        out_specs=(
            P("pipe", None, "dp", None, None),
            P("pipe", "dp", None, None),
            P("pipe", "dp", None),
        ),
        check_vma=False,
    )
```

time: 208 us -> 189 us (0.909)
  local copies, waits for them, and re-layouts: 44.1 us -> 5.74 us
  Pallas kernels: 11.8 us -> 29.2 us
  starting transfers between devices: 26.5 us -> 42.8 us
  between operations: 13 us -> 1.07 us
  matrix products: 10.7 us -> 6.36 us
  other arithmetic: 9.71 us -> 13.8 us
    unnamed x98 -> x36, local copies, waits for them, and re-layouts: 21.3 us -> 0.31 us
    pallas_call x8 -> x10, Pallas kernels: 11.8 us -> 29.2 us  [the longest x2 15.5 us: forward_call(): pl.pallas_call(functools.partial(forward_kernel, pieces), out_shape=[jax....]
    ppermute x16 -> x29, starting transfers between devices: 17.8 us -> 34.3 us  [the longest x14 16.7 us: local(): sums[way, first] = lax.ppermute(message, 'dp', right if way == 1 else left)]
    dynamic_update_slice x8 -> x0, local copies, waits for them, and re-layouts: 9.69 us -> none  [put(): lax.dynamic_update_slice(full, block, (first, owner(offset) * part, 0))]
    ppermute x16 -> x29, waiting for transfers between devices: 76 us -> 66.5 us  [the longest x14 43.6 us: local(): sums[way, first] = lax.ppermute(message, 'dp', right if way == 1 else left)]
    ppermute x6, waiting for transfers between devices: 15.4 us -> 23.1 us  [local(): g[m] = lax.ppermute(held[m][1], 'pipe', [(stage, stage - 1)])]
    convert_element_type x5 -> x6, other arithmetic: 0.99 us -> 5.55 us  [add(): return (mine.astype(F32) + theirs.astype(F32)).astype(BF16)]
    dot_general x4 -> x2, matrix products: 10.7 us -> 6.36 us  [the longest x1 3.91 us: local(): lax.dot_general(taps.reshape(rows, 3 * channels), pre_grad, over_rows, pr...]
  transfers between devices with their start and end apart: 22 -> 35, of which waited for: 12 -> 20; matrix products, arithmetic and copies ran while one was open for 8% -> 6% of each run, Pallas kernels for 3% -> 8%
where the time goes in v2:
time: 189 us
  waiting for transfers between devices  89.6 us (47%)
  starting transfers between devices  42.8 us (23%)
  Pallas kernels  29.2 us (15%)
  other arithmetic  13.8 us (7%)
  matrix products  6.36 us (3%)
  local copies, waits for them, and re-layouts  5.74 us (3%)
    ppermute x14, waiting for transfers between devices, local(): sums[way, first] = lax.ppermute(message, 'dp', right if way == 1 else left)  43.6 us
    ppermute x6, waiting for transfers between devices, local(): g[m] = lax.ppermute(held[m][1], 'pipe', [(stage, stage - 1)])  23.1 us
    ppermute x14, starting transfers between devices, local(): sums[way, first] = lax.ppermute(message, 'dp', right if way == 1 else left)  16.7 us
    pallas_call x2, Pallas kernels, forward_call(): pl.pallas_call(functools.partial(forward_kernel, pieces), out_shape=[jax....  15.5 us
    pallas_call x8, Pallas kernels, chain_call(): pl.pallas_call(functools.partial(chain_kernel, dilation, len(held)), out_...  13.6 us
    ppermute x3, waiting for transfers between devices, local(): conv_l = lax.ppermute(conv_l, 'dp', left)  12.6 us
    ppermute x6, starting transfers between devices, local(): g[m] = lax.ppermute(held[m][1], 'pipe', [(stage, stage - 1)])  8.51 us
    ppermute x3, starting transfers between devices, local(): conv_l = lax.ppermute(conv_l, 'dp', left)  6.98 us
  transfers between devices with their start and end apart: 35, of which 20 were waited for; matrix products, arithmetic and copies ran while one was open for 6% of the time, Pallas kernels for 8%

profile of v2, /device:TPU:0, one launch (start us, length us, event | category | flops | bytes accessed | tf_op | source)
XLA Modules:
  0.0 188.5 jit_solution(12299000874674011344)
XLA Ops:
  0.6 3.0 %collective-permute-start.2 = (bf16[3,64,1024]{2,1,0:T(8,128)(2,1)}, bf16[3,64,1024]{2,1,0:T(8,128)(2,1)S(1)}, u32[]{:S(2)}, u32[]{:S(2)}) collective-permute-start(bf16[3,64,1024]{2,1,0:T(8,128)(2,1)} %bitcast.60), channel_id=1, source_target_pairs={{2,0},{4,2},{6,4},{7,6},{5,7},{3,5},{1,3},{0,1},{10,8},{12,10},{14... | collective-permute-start | bytes 1179656 | tf_op jit(solution)/shard_map/ppermute | solution.py:213
  3.8 1.9 %collective-permute-start.3 = (bf16[1,64,1024]{2,1,0:T(8,128)(2,1)}, bf16[1,64,1024]{2,1,0:T(8,128)(2,1)}, u32[]{:S(2)}, u32[]{:S(2)}) collective-permute-start(bf16[1,64,1024]{2,1,0:T(8,128)(2,1)} %refs_1_.3), channel_id=1, source_target_pairs={{2,0},{4,2},{6,4},{7,6},{5,7},{3,5},{1,3},{0,1},{10,8},{12,10},{14... | collective-permute-start | bytes 393224 | tf_op jit(solution)/shard_map/ppermute | solution.py:215
  5.8 8.1 %collective-permute-done.2.refs_4_ = bf16[3,64,1024]{2,1,0:T(8,128)(2,1)S(1)} collective-permute-done((bf16[3,64,1024]{2,1,0:T(8,128)(2,1)}, bf16[3,64,1024]{2,1,0:T(8,128)(2,1)S(1)}, u32[]{:S(2)}, u32[]{:S(2)}) %collective-permute-start.2) | collective-permute-done | bytes 393248 | tf_op jit(solution)/shard_map/ppermute | solution.py:213
  13.9 2.0 %collective-permute-start.6 = (bf16[3,64,1024]{2,1,0:T(8,128)(2,1)S(1)}, bf16[3,64,1024]{2,1,0:T(8,128)(2,1)S(1)}, u32[]{:S(2)}, u32[]{:S(2)}) collective-permute-start(bf16[3,64,1024]{2,1,0:T(8,128)(2,1)S(1)} %collective-permute-done.2.refs_4_), channel_id=1, source_target_pairs={{2,0},{4,2},{6,4},{7,6},{5,7},{3,5},{1,3},{0,1},{10,8},{12,10},{14... | collective-permute-start | bytes 1179656 | tf_op jit(solution)/shard_map/ppermute | solution.py:213
  16.1 3.1 %fusion.20 = (bf16[2,512,512]{2,1,0:T(8,128)(2,1)S(1)}, bf16[2,512,512]{2,1,0:T(8,128)(2,1)S(1)}) fusion(s32[]{:T(128)S(6)} %select_n.133, bf16[2,512,512]{2,1,0:T(8,128)(2,1)} %bitcast.54, pred[512]{0:T(512)(128)(4,1)S(1)} %get-tuple-element.97, s32[]{:T(128)S(6)} %select_n.135, pred[512]{0:T(512)(128)(4,1)S(1)} %get-tuple-element.96), kind=kLoop, calls=%fused_computation.27 | loop fusion | flops 5242880 | bytes 3146760 | tf_op jit(solution)/shard_map/jit(_where)/select_n | solution.py:229
  19.5 1.9 %collective-permute-start.7 = (bf16[1,64,1024]{2,1,0:T(8,128)(2,1)}, bf16[1,64,1024]{2,1,0:T(8,128)(2,1)S(1)}, u32[]{:S(2)}, u32[]{:S(2)}) collective-permute-start(bf16[1,64,1024]{2,1,0:T(8,128)(2,1)} %collective-permute-done.3.refs_5_), channel_id=1, source_target_pairs={{2,0},{4,2},{6,4},{7,6},{5,7},{3,5},{1,3},{0,1},{10,8},{12,10},{14... | collective-permute-start | bytes 393224 | tf_op jit(solution)/shard_map/ppermute | solution.py:215
  21.5 4.5 %collective-permute-done.6.refs_8_ = bf16[3,64,1024]{2,1,0:T(8,128)(2,1)S(1)} collective-permute-done((bf16[3,64,1024]{2,1,0:T(8,128)(2,1)S(1)}, bf16[3,64,1024]{2,1,0:T(8,128)(2,1)S(1)}, u32[]{:S(2)}, u32[]{:S(2)}) %collective-permute-start.6) | collective-permute-done | bytes 393248 | tf_op jit(solution)/shard_map/ppermute | solution.py:213
  26.0 2.0 %collective-permute-start.10 = (bf16[3,64,1024]{2,1,0:T(8,128)(2,1)S(1)}, bf16[3,64,1024]{2,1,0:T(8,128)(2,1)S(1)}, u32[]{:S(2)}, u32[]{:S(2)}) collective-permute-start(bf16[3,64,1024]{2,1,0:T(8,128)(2,1)S(1)} %collective-permute-done.6.refs_8_), channel_id=1, source_target_pairs={{2,0},{4,2},{6,4},{7,6},{5,7},{3,5},{1,3},{0,1},{10,8},{12,10},{14... | collective-permute-start | bytes 1179656 | tf_op jit(solution)/shard_map/ppermute | solution.py:213
  29.9 2.0 %collective-permute-start.5 = (bf16[1,64,1024]{2,1,0:T(8,128)(2,1)}, bf16[1,64,1024]{2,1,0:T(8,128)(2,1)}, u32[]{:S(2)}, u32[]{:S(2)}) collective-permute-start(bf16[1,64,1024]{2,1,0:T(8,128)(2,1)} %collective-permute-done.1.refs_3_), channel_id=1, source_target_pairs={{0,2},{2,4},{4,6},{6,7},{7,5},{5,3},{3,1},{1,0},{8,10},{10,12},{12... | collective-permute-start | bytes 393224 | tf_op jit(solution)/shard_map/ppermute | solution.py:214
  33.1 6.1 %collective-permute-done.5.refs_7_ = bf16[1,64,1024]{2,1,0:T(8,128)(2,1)} collective-permute-done((bf16[1,64,1024]{2,1,0:T(8,128)(2,1)}, bf16[1,64,1024]{2,1,0:T(8,128)(2,1)}, u32[]{:S(2)}, u32[]{:S(2)}) %collective-permute-start.5) | collective-permute-done | bytes 131104 | tf_op jit(solution)/shard_map/ppermute | solution.py:214
  46.5 2.9 %collective-permute-done.12.refs_14_ = bf16[2,64,1024]{2,1,0:T(8,128)(2,1)} collective-permute-done((bf16[2,64,1024]{2,1,0:T(8,128)(2,1)S(1)}, bf16[2,64,1024]{2,1,0:T(8,128)(2,1)}, u32[]{:S(2)}, u32[]{:S(2)}) %collective-permute-start.12) | collective-permute-done | bytes 262176 | tf_op jit(solution)/shard_map/ppermute | solution.py:218
  49.4 7.8 %shard_map.76 = (f32[512,512]{1,0:T(8,128)}, f32[512,512]{1,0:T(8,128)}, f32[512,512]{1,0:T(8,128)}, bf16[512,512]{1,0:T(8,128)(2,1)}, bf16[2048,1024]{1,0:T(8,128)(2,1)}) custom-call(s32[8]{0:T(128)} %stack.44.owners, bf16[512,1536]{1,0:T(8,128)(2,1)} %get-tuple-element.86.taps_hbm, bf16[512,512]{1,0:T(8,128)(2,1)} %get-tuple-element.88.skip_hbm, ...), custom_call_target="tpu_custom_call" | custom-call | flops 2147483648 | bytes 16777216 | tf_op jit(solution)/shard_map/pallas_call | solution.py:81
  58.8 7.8 %shard_map.81 = (f32[512,512]{1,0:T(8,128)}, f32[512,512]{1,0:T(8,128)}, f32[512,512]{1,0:T(8,128)}, bf16[512,512]{1,0:T(8,128)(2,1)}, bf16[2048,1024]{1,0:T(8,128)(2,1)}) custom-call(s32[8]{0:T(128)} %stack.44.owners, bf16[512,1536]{1,0:T(8,128)(2,1)} %get-tuple-element.87.taps_hbm, bf16[512,512]{1,0:T(8,128)(2,1)} %get-tuple-element.89.skip_hbm, ...), custom_call_target="tpu_custom_call" | custom-call | flops 2147483648 | bytes 16777216 | tf_op jit(solution)/shard_map/pallas_call | solution.py:81
  74.5 19.1 %collective-permute-done.17.g_hbm = bf16[512,512]{1,0:T(8,128)(2,1)} collective-permute-done((bf16[512,512]{1,0:T(8,128)(2,1)}, bf16[512,512]{1,0:T(8,128)(2,1)}, u32[]{:S(2)}, u32[]{:S(2)}) %collective-permute-start.17) | collective-permute-done | bytes 524320 | tf_op jit(solution)/shard_map/ppermute | solution.py:245
  93.7 6.3 %shard_map.80 = (bf16[512,1024]{1,0:T(8,128)(2,1)}, bf16[512,512]{1,0:T(8,128)(2,1)}, bf16[512,512]{1,0:T(8,128)(2,1)}) custom-call(s32[1]{0:T(128)} %bitcast.flags, bf16[512,512]{1,0:T(8,128)(2,1)} %collective-permute-done.17.g_hbm, f32[512,512]{1,0:T(8,128)} %get-tuple-element.38.hs_hbm, ...), custom_call_target="tpu_custom_call", output_to_operand_aliasing={{0}: (6, {}), {1}: (7, {}), {2}: (8, {})} | custom-call | flops 1073741824 | bytes 8388608 | tf_op jit(solution)/shard_map/pallas_call | solution.py:153
  100.0 3.9 %collective-permute-done.20.g_hbm = bf16[512,512]{1,0:T(8,128)(2,1)} collective-permute-done((bf16[512,512]{1,0:T(8,128)(2,1)}, bf16[512,512]{1,0:T(8,128)(2,1)}, u32[]{:S(2)}, u32[]{:S(2)}) %collective-permute-start.20) | collective-permute-done | bytes 524320 | tf_op jit(solution)/shard_map/ppermute | solution.py:245
  103.9 6.4 %shard_map.85 = (bf16[512,1024]{1,0:T(8,128)(2,1)}, bf16[512,512]{1,0:T(8,128)(2,1)}, bf16[512,512]{1,0:T(8,128)(2,1)}) custom-call(s32[1]{0:T(128)} %bitcast.flags, bf16[512,512]{1,0:T(8,128)(2,1)} %collective-permute-done.20.g_hbm, f32[512,512]{1,0:T(8,128)} %get-tuple-element.52.hs_hbm, ...), custom_call_target="tpu_custom_call", output_to_operand_aliasing={{0}: (6, {}), {1}: (7, {}), {2}: (8, {})} | custom-call | flops 1073741824 | bytes 8388608 | tf_op jit(solution)/shard_map/pallas_call | solution.py:153
  110.4 2.5 %fusion.14 = bf16[512,1024]{1,0:T(8,128)(2,1)S(1)} fusion(bf16[1024,512]{1,0:T(8,128)(2,1)S(1)} %bitcast.59, bf16[512,512]{1,0:T(8,128)(2,1)} %get-tuple-element.71, bf16[512,512]{1,0:T(8,128)(2,1)S(1)} %copy-done.5, bf16[512,512]{1,0:T(8,128)(2,1)S(1)} %copy-done.17, bf16[512,512]{1,0:T(8,128)(2,1)S(1)} %copy-done.16), kind=kOutput, calls=%fused_computation.23 | convolution fusion | flops 1082654720 | bytes 4194304 | tf_op jit(solution)/shard_map/dot_general | solution.py:255
  112.9 3.9 %convolution_convert_fusion = bf16[1536,1024]{1,0:T(8,128)(2,1)S(1)} fusion(bf16[1024,512]{1,0:T(8,128)(2,1)S(1)} %bitcast.58, bf16[1024,512]{1,0:T(8,128)(2,1)S(1)} %bitcast.57, bf16[1024,512]{1,0:T(8,128)(2,1)S(1)} %bitcast.56, bf16[512,1024]{1,0:T(8,128)(2,1)S(1)} %copy-done.2, bf16[512,1024]{1,0:T(8,128)(2,1)S(1)} %copy-done.1), kind=kOutput, calls=%fused_computation.1 | convolution fusion | flops 3236429824 | bytes 8388608 | tf_op jit(solution)/shard_map/dot_general | solution.py:252
  117.8 8.5 %collective-permute-done.21 = bf16[2,64,1024]{2,1,0:T(8,128)(2,1)S(1)} collective-permute-done((bf16[2,64,1024]{2,1,0:T(8,128)(2,1)S(1)}, bf16[2,64,1024]{2,1,0:T(8,128)(2,1)S(1)}, u32[]{:S(2)}, u32[]{:S(2)}) %collective-permute-start.21) | collective-permute-done | bytes 262176 | tf_op jit(solution)/shard_map/ppermute | solution.py:274
  128.4 6.9 %collective-permute-done.22 = bf16[2,64,1024]{2,1,0:T(8,128)(2,1)S(1)} collective-permute-done((bf16[2,64,1024]{2,1,0:T(8,128)(2,1)S(1)}, bf16[2,64,1024]{2,1,0:T(8,128)(2,1)S(1)}, u32[]{:S(2)}, u32[]{:S(2)}) %collective-permute-start.22) | collective-permute-done | bytes 262176 | tf_op jit(solution)/shard_map/ppermute | solution.py:274
  136.8 7.0 %collective-permute-done.23 = bf16[2,64,1024]{2,1,0:T(8,128)(2,1)S(1)} collective-permute-done((bf16[2,64,1024]{2,1,0:T(8,128)(2,1)S(1)}, bf16[2,64,1024]{2,1,0:T(8,128)(2,1)S(1)}, u32[]{:S(2)}, u32[]{:S(2)}) %collective-permute-start.23) | collective-permute-done | bytes 262176 | tf_op jit(solution)/shard_map/ppermute | solution.py:274
  145.0 3.0 %collective-permute-start.26 = (bf16[2,64,1024]{2,1,0:T(8,128)(2,1)S(1)}, bf16[2,64,1024]{2,1,0:T(8,128)(2,1)S(1)}, u32[]{:S(2)}, u32[]{:S(2)}) collective-permute-start(bf16[2,64,1024]{2,1,0:T(8,128)(2,1)S(1)} %get-tuple-element.79), channel_id=1, source_target_pairs={{2,0},{4,2},{6,4},{7,6},{5,7},{3,5},{1,3},{0,1},{10,8},{12,10},{14... | collective-permute-start | bytes 786440 | tf_op jit(solution)/shard_map/ppermute | solution.py:274
  148.0 2.0 %collective-permute-start.31 = (bf16[2,64,1024]{2,1,0:T(8,128)(2,1)S(1)}, bf16[2,64,1024]{2,1,0:T(8,128)(2,1)S(1)}, u32[]{:S(2)}, u32[]{:S(2)}) collective-permute-start(bf16[2,64,1024]{2,1,0:T(8,128)(2,1)S(1)} %get-tuple-element.81), channel_id=1, source_target_pairs={{2,0},{4,2},{6,4},{7,6},{5,7},{3,5},{1,3},{0,1},{10,8},{12,10},{14... | collective-permute-start | bytes 786440 | tf_op jit(solution)/shard_map/ppermute | solution.py:274
  150.1 2.2 %collective-permute-done.26 = bf16[2,64,1024]{2,1,0:T(8,128)(2,1)S(1)} collective-permute-done((bf16[2,64,1024]{2,1,0:T(8,128)(2,1)S(1)}, bf16[2,64,1024]{2,1,0:T(8,128)(2,1)S(1)}, u32[]{:S(2)}, u32[]{:S(2)}) %collective-permute-start.26) | collective-permute-done | bytes 262176 | tf_op jit(solution)/shard_map/ppermute | solution.py:274
  153.3 2.5 %collective-permute-start.27 = (bf16[2,64,1024]{2,1,0:T(8,128)(2,1)S(1)}, bf16[2,64,1024]{2,1,0:T(8,128)(2,1)S(1)}, u32[]{:S(2)}, u32[]{:S(2)}) collective-permute-start(bf16[2,64,1024]{2,1,0:T(8,128)(2,1)S(1)} %add_convert_fusion.5), channel_id=1, source_target_pairs={{2,0},{4,2},{6,4},{7,6},{5,7},{3,5},{1,3},{0,1},{10,8},{12,10},{14... | collective-permute-start | bytes 786440 | tf_op jit(solution)/shard_map/ppermute | solution.py:274
  159.0 3.0 %collective-permute-done.24 = bf16[2,64,1024]{2,1,0:T(8,128)(2,1)S(1)} collective-permute-done((bf16[2,64,1024]{2,1,0:T(8,128)(2,1)S(1)}, bf16[2,64,1024]{2,1,0:T(8,128)(2,1)S(1)}, u32[]{:S(2)}, u32[]{:S(2)}) %collective-permute-start.24) | collective-permute-done | bytes 262176 | tf_op jit(solution)/shard_map/ppermute | solution.py:274
  165.5 4.5 %collective-permute-done.32 = bf16[2,64,1024]{2,1,0:T(8,128)(2,1)S(1)} collective-permute-done((bf16[2,64,1024]{2,1,0:T(8,128)(2,1)S(1)}, bf16[2,64,1024]{2,1,0:T(8,128)(2,1)S(1)}, u32[]{:S(2)}, u32[]{:S(2)}) %collective-permute-start.32) | collective-permute-done | bytes 262176 | tf_op jit(solution)/shard_map/ppermute | solution.py:274
  171.9 2.0 %collective-permute-start.33 = (bf16[2,64,1024]{2,1,0:T(8,128)(2,1)S(1)}, bf16[2,64,1024]{2,1,0:T(8,128)(2,1)S(1)}, u32[]{:S(2)}, u32[]{:S(2)}) collective-permute-start(bf16[2,64,1024]{2,1,0:T(8,128)(2,1)S(1)} %get-tuple-element.85), channel_id=1, source_target_pairs={{2,0},{4,2},{6,4},{7,6},{5,7},{3,5},{1,3},{0,1},{10,8},{12,10},{14... | collective-permute-start | bytes 786440 | tf_op jit(solution)/shard_map/ppermute | solution.py:274
  174.0 4.3 %collective-permute-done.33 = bf16[2,64,1024]{2,1,0:T(8,128)(2,1)S(1)} collective-permute-done((bf16[2,64,1024]{2,1,0:T(8,128)(2,1)S(1)}, bf16[2,64,1024]{2,1,0:T(8,128)(2,1)S(1)}, u32[]{:S(2)}, u32[]{:S(2)}) %collective-permute-start.33) | collective-permute-done | bytes 262176 | tf_op jit(solution)/shard_map/ppermute | solution.py:274
  179.4 2.0 %collective-permute-start.34 = (bf16[2,64,1024]{2,1,0:T(8,128)(2,1)S(1)}, bf16[2,64,1024]{2,1,0:T(8,128)(2,1)S(1)}, u32[]{:S(2)}, u32[]{:S(2)}) collective-permute-start(bf16[2,64,1024]{2,1,0:T(8,128)(2,1)S(1)} %add_convert_fusion), channel_id=1, source_target_pairs={{2,0},{4,2},{6,4},{7,6},{5,7},{3,5},{1,3},{0,1},{10,8},{12,10},{14... | collective-permute-start | bytes 786440 | tf_op jit(solution)/shard_map/ppermute | solution.py:274
  182.4 3.3 %collective-permute-done.34 = bf16[2,64,1024]{2,1,0:T(8,128)(2,1)S(1)} collective-permute-done((bf16[2,64,1024]{2,1,0:T(8,128)(2,1)S(1)}, bf16[2,64,1024]{2,1,0:T(8,128)(2,1)S(1)}, u32[]{:S(2)}, u32[]{:S(2)}) %collective-permute-start.34) | collective-permute-done | bytes 262176 | tf_op jit(solution)/shard_map/ppermute | solution.py:274
  (108 shorter events, 41.0 us)
Async XLA Ops:
  0.6 13.2 %collective-permute-start.2 = (bf16[3,64,1024]{2,1,0:T(8,128)(2,1)}, bf16[3,64,1024]{2,1,0:T(8,128)(2,1)S(1)}, u32[]{:S(2)}, u32[]{:S(2)}) collective-permute-start(bf16[3,64,1024]{2,1,0:T(8,128)(2,1)} %bitcast.60), channel_id=1, source_target_pairs={{2,0},{4,2},{6,4},{7,6},{5,7},{3,5},{1,3},{0,1},{10,8},{12,10},{14... | collective-permute-start | bytes 1179656 | tf_op jit(solution)/shard_map/ppermute | solution.py:213
  3.7 12.3 %collective-permute-start = (bf16[3,64,1024]{2,1,0:T(8,128)(2,1)}, bf16[3,64,1024]{2,1,0:T(8,128)(2,1)}, u32[]{:S(2)}, u32[]{:S(2)}) collective-permute-start(bf16[3,64,1024]{2,1,0:T(8,128)(2,1)} %bitcast.61), channel_id=1, source_target_pairs={{0,2},{2,4},{4,6},{6,7},{7,5},{5,3},{3,1},{1,0},{8,10},{10,12},{12... | collective-permute-start | bytes 1179656 | tf_op jit(solution)/shard_map/ppermute | solution.py:212
  3.8 15.7 %collective-permute-start.3 = (bf16[1,64,1024]{2,1,0:T(8,128)(2,1)}, bf16[1,64,1024]{2,1,0:T(8,128)(2,1)}, u32[]{:S(2)}, u32[]{:S(2)}) collective-permute-start(bf16[1,64,1024]{2,1,0:T(8,128)(2,1)} %refs_1_.3), channel_id=1, source_target_pairs={{2,0},{4,2},{6,4},{7,6},{5,7},{3,5},{1,3},{0,1},{10,8},{12,10},{14... | collective-permute-start | bytes 393224 | tf_op jit(solution)/shard_map/ppermute | solution.py:215
  5.7 24.2 %collective-permute-start.1 = (bf16[1,64,1024]{2,1,0:T(8,128)(2,1)}, bf16[1,64,1024]{2,1,0:T(8,128)(2,1)}, u32[]{:S(2)}, u32[]{:S(2)}) collective-permute-start(bf16[1,64,1024]{2,1,0:T(8,128)(2,1)} %refs_1_.3), channel_id=1, source_target_pairs={{0,2},{2,4},{4,6},{6,7},{7,5},{5,3},{3,1},{1,0},{8,10},{10,12},{12... | collective-permute-start | bytes 393224 | tf_op jit(solution)/shard_map/ppermute | solution.py:214
  13.9 12.1 %collective-permute-start.6 = (bf16[3,64,1024]{2,1,0:T(8,128)(2,1)S(1)}, bf16[3,64,1024]{2,1,0:T(8,128)(2,1)S(1)}, u32[]{:S(2)}, u32[]{:S(2)}) collective-permute-start(bf16[3,64,1024]{2,1,0:T(8,128)(2,1)S(1)} %collective-permute-done.2.refs_4_), channel_id=1, source_target_pairs={{2,0},{4,2},{6,4},{7,6},{5,7},{3,5},{1,3},{0,1},{10,8},{12,10},{14... | collective-permute-start | bytes 1179656 | tf_op jit(solution)/shard_map/ppermute | solution.py:213
  16.0 12.0 %collective-permute-start.4 = (bf16[3,64,1024]{2,1,0:T(8,128)(2,1)}, bf16[3,64,1024]{2,1,0:T(8,128)(2,1)S(1)}, u32[]{:S(2)}, u32[]{:S(2)}) collective-permute-start(bf16[3,64,1024]{2,1,0:T(8,128)(2,1)} %collective-permute-done.refs_2_), channel_id=1, source_target_pairs={{0,2},{2,4},{4,6},{6,7},{7,5},{5,3},{3,1},{1,0},{8,10},{10,12},{12... | collective-permute-start | bytes 1179656 | tf_op jit(solution)/shard_map/ppermute | solution.py:212
  19.5 12.4 %collective-permute-start.7 = (bf16[1,64,1024]{2,1,0:T(8,128)(2,1)}, bf16[1,64,1024]{2,1,0:T(8,128)(2,1)S(1)}, u32[]{:S(2)}, u32[]{:S(2)}) collective-permute-start(bf16[1,64,1024]{2,1,0:T(8,128)(2,1)} %collective-permute-done.3.refs_5_), channel_id=1, source_target_pairs={{2,0},{4,2},{6,4},{7,6},{5,7},{3,5},{1,3},{0,1},{10,8},{12,10},{14... | collective-permute-start | bytes 393224 | tf_op jit(solution)/shard_map/ppermute | solution.py:215
  26.0 15.2 %collective-permute-start.10 = (bf16[3,64,1024]{2,1,0:T(8,128)(2,1)S(1)}, bf16[3,64,1024]{2,1,0:T(8,128)(2,1)S(1)}, u32[]{:S(2)}, u32[]{:S(2)}) collective-permute-start(bf16[3,64,1024]{2,1,0:T(8,128)(2,1)S(1)} %collective-permute-done.6.refs_8_), channel_id=1, source_target_pairs={{2,0},{4,2},{6,4},{7,6},{5,7},{3,5},{1,3},{0,1},{10,8},{12,10},{14... | collective-permute-start | bytes 1179656 | tf_op jit(solution)/shard_map/ppermute | solution.py:213
  27.9 14.9 %collective-permute-start.8 = (bf16[3,64,1024]{2,1,0:T(8,128)(2,1)S(1)}, bf16[3,64,1024]{2,1,0:T(8,128)(2,1)S(1)}, u32[]{:S(2)}, u32[]{:S(2)}) collective-permute-start(bf16[3,64,1024]{2,1,0:T(8,128)(2,1)S(1)} %collective-permute-done.4.refs_6_), channel_id=1, source_target_pairs={{0,2},{2,4},{4,6},{6,7},{7,5},{5,3},{3,1},{1,0},{8,10},{10,12},{12... | collective-permute-start | bytes 1179656 | tf_op jit(solution)/shard_map/ppermute | solution.py:212
  29.9 9.2 %collective-permute-start.5 = (bf16[1,64,1024]{2,1,0:T(8,128)(2,1)}, bf16[1,64,1024]{2,1,0:T(8,128)(2,1)}, u32[]{:S(2)}, u32[]{:S(2)}) collective-permute-start(bf16[1,64,1024]{2,1,0:T(8,128)(2,1)} %collective-permute-done.1.refs_3_), channel_id=1, source_target_pairs={{0,2},{2,4},{4,6},{6,7},{7,5},{5,3},{3,1},{1,0},{8,10},{10,12},{12... | collective-permute-start | bytes 393224 | tf_op jit(solution)/shard_map/ppermute | solution.py:214
  31.9 7.9 %collective-permute-start.11 = (bf16[1,64,1024]{2,1,0:T(8,128)(2,1)S(1)}, bf16[1,64,1024]{2,1,0:T(8,128)(2,1)}, u32[]{:S(2)}, u32[]{:S(2)}) collective-permute-start(bf16[1,64,1024]{2,1,0:T(8,128)(2,1)S(1)} %collective-permute-done.7.refs_9_), channel_id=1, source_target_pairs={{2,0},{4,2},{6,4},{7,6},{5,7},{3,5},{1,3},{0,1},{10,8},{12,10},{14... | collective-permute-start | bytes 393224 | tf_op jit(solution)/shard_map/ppermute | solution.py:215
  39.2 6.2 %collective-permute-start.9 = (bf16[1,64,1024]{2,1,0:T(8,128)(2,1)}, bf16[1,64,1024]{2,1,0:T(8,128)(2,1)}, u32[]{:S(2)}, u32[]{:S(2)}) collective-permute-start(bf16[1,64,1024]{2,1,0:T(8,128)(2,1)} %collective-permute-done.5.refs_7_), channel_id=1, source_target_pairs={{0,2},{2,4},{4,6},{6,7},{7,5},{5,3},{3,1},{1,0},{8,10},{10,12},{12... | collective-permute-start | bytes 393224 | tf_op jit(solution)/shard_map/ppermute | solution.py:214
  39.8 5.6 %collective-permute-start.14 = (bf16[1,64,1024]{2,1,0:T(8,128)(2,1)}, bf16[1,64,1024]{2,1,0:T(8,128)(2,1)}, u32[]{:S(2)}, u32[]{:S(2)}) collective-permute-start(bf16[1,64,1024]{2,1,0:T(8,128)(2,1)} %collective-permute-done.11.refs_13_), channel_id=1, source_target_pairs={{2,0},{4,2},{6,4},{7,6},{5,7},{3,5},{1,3},{0,1},{10,8},{12,10},{14... | collective-permute-start | bytes 393224 | tf_op jit(solution)/shard_map/ppermute | solution.py:220
  41.2 5.3 %collective-permute-start.13 = (bf16[1,64,1024]{2,1,0:T(8,128)(2,1)S(1)}, bf16[1,64,1024]{2,1,0:T(8,128)(2,1)}, u32[]{:S(2)}, u32[]{:S(2)}) collective-permute-start(bf16[1,64,1024]{2,1,0:T(8,128)(2,1)S(1)} %slice.38), channel_id=1, source_target_pairs={{2,0},{4,2},{6,4},{7,6},{5,7},{3,5},{1,3},{0,1},{10,8},{12,10},{14... | collective-permute-start | bytes 393224 | tf_op jit(solution)/shard_map/ppermute | solution.py:219
  42.9 6.5 %collective-permute-start.12 = (bf16[2,64,1024]{2,1,0:T(8,128)(2,1)S(1)}, bf16[2,64,1024]{2,1,0:T(8,128)(2,1)}, u32[]{:S(2)}, u32[]{:S(2)}) collective-permute-start(bf16[2,64,1024]{2,1,0:T(8,128)(2,1)S(1)} %slice.37), channel_id=1, source_target_pairs={{0,2},{2,4},{4,6},{6,7},{7,5},{5,3},{3,1},{1,0},{8,10},{10,12},{12... | collective-permute-start | bytes 786440 | tf_op jit(solution)/shard_map/ppermute | solution.py:218
  57.3 11.1 %collective-permute-start.15 = (bf16[512,512]{1,0:T(8,128)(2,1)}, bf16[512,512]{1,0:T(8,128)(2,1)}, u32[]{:S(2)}, u32[]{:S(2)}) collective-permute-start(bf16[512,512]{1,0:T(8,128)(2,1)} %get-tuple-element.42.refs_1_), channel_id=1, source_target_pairs={{24,16},{25,17},{26,18},{27,19},{28,20},{29,21},{30,22},{31,23}} | collective-permute-start | bytes 1572872 | tf_op jit(solution)/shard_map/ppermute | solution.py:245
  71.7 21.9 %collective-permute-start.17 = (bf16[512,512]{1,0:T(8,128)(2,1)}, bf16[512,512]{1,0:T(8,128)(2,1)}, u32[]{:S(2)}, u32[]{:S(2)}) collective-permute-start(bf16[512,512]{1,0:T(8,128)(2,1)} %get-tuple-element.48.refs_1_), channel_id=1, source_target_pairs={{8,0},{9,1},{10,2},{11,3},{12,4},{13,5},{14,6},{15,7}} | collective-permute-start | bytes 1572872 | tf_op jit(solution)/shard_map/ppermute | solution.py:245
  73.2 30.7 %collective-permute-start.20 = (bf16[512,512]{1,0:T(8,128)(2,1)}, bf16[512,512]{1,0:T(8,128)(2,1)}, u32[]{:S(2)}, u32[]{:S(2)}) collective-permute-start(bf16[512,512]{1,0:T(8,128)(2,1)} %get-tuple-element.62.refs_1_), channel_id=1, source_target_pairs={{8,0},{9,1},{10,2},{11,3},{12,4},{13,5},{14,6},{15,7}} | collective-permute-start | bytes 1572872 | tf_op jit(solution)/shard_map/ppermute | solution.py:245
  117.3 8.9 %collective-permute-start.21 = (bf16[2,64,1024]{2,1,0:T(8,128)(2,1)S(1)}, bf16[2,64,1024]{2,1,0:T(8,128)(2,1)S(1)}, u32[]{:S(2)}, u32[]{:S(2)}) collective-permute-start(bf16[2,64,1024]{2,1,0:T(8,128)(2,1)S(1)} %get-tuple-element.80), channel_id=1, source_target_pairs={{0,2},{2,4},{4,6},{6,7},{7,5},{5,3},{3,1},{1,0},{8,10},{10,12},{12... | collective-permute-start | bytes 786440 | tf_op jit(solution)/shard_map/ppermute | solution.py:274
  126.3 9.0 %collective-permute-start.22 = (bf16[2,64,1024]{2,1,0:T(8,128)(2,1)S(1)}, bf16[2,64,1024]{2,1,0:T(8,128)(2,1)S(1)}, u32[]{:S(2)}, u32[]{:S(2)}) collective-permute-start(bf16[2,64,1024]{2,1,0:T(8,128)(2,1)S(1)} %add_convert_fusion.9), channel_id=1, source_target_pairs={{0,2},{2,4},{4,6},{6,7},{7,5},{5,3},{3,1},{1,0},{8,10},{10,12},{12... | collective-permute-start | bytes 786440 | tf_op jit(solution)/shard_map/ppermute | solution.py:274
  126.8 10.0 %collective-permute-start.25 = (bf16[2,64,1024]{2,1,0:T(8,128)(2,1)S(1)}, bf16[2,64,1024]{2,1,0:T(8,128)(2,1)S(1)}, u32[]{:S(2)}, u32[]{:S(2)}) collective-permute-start(bf16[2,64,1024]{2,1,0:T(8,128)(2,1)S(1)} %get-tuple-element.83), channel_id=1, source_target_pairs={{2,0},{4,2},{6,4},{7,6},{5,7},{3,5},{1,3},{0,1},{10,8},{12,10},{14... | collective-permute-start | bytes 786440 | tf_op jit(solution)/shard_map/ppermute | solution.py:274
  136.4 7.4 %collective-permute-start.23 = (bf16[2,64,1024]{2,1,0:T(8,128)(2,1)S(1)}, bf16[2,64,1024]{2,1,0:T(8,128)(2,1)S(1)}, u32[]{:S(2)}, u32[]{:S(2)}) collective-permute-start(bf16[2,64,1024]{2,1,0:T(8,128)(2,1)S(1)} %add_convert_fusion.8), channel_id=1, source_target_pairs={{0,2},{2,4},{4,6},{6,7},{7,5},{5,3},{3,1},{1,0},{8,10},{10,12},{12... | collective-permute-start | bytes 786440 | tf_op jit(solution)/shard_map/ppermute | solution.py:274
  145.0 7.2 %collective-permute-start.26 = (bf16[2,64,1024]{2,1,0:T(8,128)(2,1)S(1)}, bf16[2,64,1024]{2,1,0:T(8,128)(2,1)S(1)}, u32[]{:S(2)}, u32[]{:S(2)}) collective-permute-start(bf16[2,64,1024]{2,1,0:T(8,128)(2,1)S(1)} %get-tuple-element.79), channel_id=1, source_target_pairs={{2,0},{4,2},{6,4},{7,6},{5,7},{3,5},{1,3},{0,1},{10,8},{12,10},{14... | collective-permute-start | bytes 786440 | tf_op jit(solution)/shard_map/ppermute | solution.py:274
  148.0 9.5 %collective-permute-start.31 = (bf16[2,64,1024]{2,1,0:T(8,128)(2,1)S(1)}, bf16[2,64,1024]{2,1,0:T(8,128)(2,1)S(1)}, u32[]{:S(2)}, u32[]{:S(2)}) collective-permute-start(bf16[2,64,1024]{2,1,0:T(8,128)(2,1)S(1)} %get-tuple-element.81), channel_id=1, source_target_pairs={{2,0},{4,2},{6,4},{7,6},{5,7},{3,5},{1,3},{0,1},{10,8},{12,10},{14... | collective-permute-start | bytes 786440 | tf_op jit(solution)/shard_map/ppermute | solution.py:274
  150.0 9.0 %collective-permute-start.28 = (bf16[2,64,1024]{2,1,0:T(8,128)(2,1)S(1)}, bf16[2,64,1024]{2,1,0:T(8,128)(2,1)S(1)}, u32[]{:S(2)}, u32[]{:S(2)}) collective-permute-start(bf16[2,64,1024]{2,1,0:T(8,128)(2,1)S(1)} %get-tuple-element.82), channel_id=1, source_target_pairs={{0,2},{2,4},{4,6},{6,7},{7,5},{5,3},{3,1},{1,0},{8,10},{10,12},{12... | collective-permute-start | bytes 786440 | tf_op jit(solution)/shard_map/ppermute | solution.py:274
  150.1 11.9 %collective-permute-start.24 = (bf16[2,64,1024]{2,1,0:T(8,128)(2,1)S(1)}, bf16[2,64,1024]{2,1,0:T(8,128)(2,1)S(1)}, u32[]{:S(2)}, u32[]{:S(2)}) collective-permute-start(bf16[2,64,1024]{2,1,0:T(8,128)(2,1)S(1)} %get-tuple-element.78), channel_id=1, source_target_pairs={{0,2},{2,4},{4,6},{6,7},{7,5},{5,3},{3,1},{1,0},{8,10},{10,12},{12... | collective-permute-start | bytes 786440 | tf_op jit(solution)/shard_map/ppermute | solution.py:274
  153.3 8.7 %collective-permute-start.27 = (bf16[2,64,1024]{2,1,0:T(8,128)(2,1)S(1)}, bf16[2,64,1024]{2,1,0:T(8,128)(2,1)S(1)}, u32[]{:S(2)}, u32[]{:S(2)}) collective-permute-start(bf16[2,64,1024]{2,1,0:T(8,128)(2,1)S(1)} %add_convert_fusion.5), channel_id=1, source_target_pairs={{2,0},{4,2},{6,4},{7,6},{5,7},{3,5},{1,3},{0,1},{10,8},{12,10},{14... | collective-permute-start | bytes 786440 | tf_op jit(solution)/shard_map/ppermute | solution.py:274
  163.4 6.6 %collective-permute-start.32 = (bf16[2,64,1024]{2,1,0:T(8,128)(2,1)S(1)}, bf16[2,64,1024]{2,1,0:T(8,128)(2,1)S(1)}, u32[]{:S(2)}, u32[]{:S(2)}) collective-permute-start(bf16[2,64,1024]{2,1,0:T(8,128)(2,1)S(1)} %get-tuple-element.76), channel_id=1, source_target_pairs={{2,0},{4,2},{6,4},{7,6},{5,7},{3,5},{1,3},{0,1},{10,8},{12,10},{14... | collective-permute-start | bytes 786440 | tf_op jit(solution)/shard_map/ppermute | solution.py:274
  164.3 6.4 %collective-permute-start.29 = (bf16[2,64,1024]{2,1,0:T(8,128)(2,1)S(1)}, bf16[2,64,1024]{2,1,0:T(8,128)(2,1)S(1)}, u32[]{:S(2)}, u32[]{:S(2)}) collective-permute-start(bf16[2,64,1024]{2,1,0:T(8,128)(2,1)S(1)} %get-tuple-element.77), channel_id=1, source_target_pairs={{0,2},{2,4},{4,6},{6,7},{7,5},{5,3},{3,1},{1,0},{8,10},{10,12},{12... | collective-permute-start | bytes 786440 | tf_op jit(solution)/shard_map/ppermute | solution.py:274
  171.9 6.4 %collective-permute-start.33 = (bf16[2,64,1024]{2,1,0:T(8,128)(2,1)S(1)}, bf16[2,64,1024]{2,1,0:T(8,128)(2,1)S(1)}, u32[]{:S(2)}, u32[]{:S(2)}) collective-permute-start(bf16[2,64,1024]{2,1,0:T(8,128)(2,1)S(1)} %get-tuple-element.85), channel_id=1, source_target_pairs={{2,0},{4,2},{6,4},{7,6},{5,7},{3,5},{1,3},{0,1},{10,8},{12,10},{14... | collective-permute-start | bytes 786440 | tf_op jit(solution)/shard_map/ppermute | solution.py:274
  173.9 8.5 %collective-permute-start.30 = (bf16[2,64,1024]{2,1,0:T(8,128)(2,1)S(1)}, bf16[2,64,1024]{2,1,0:T(8,128)(2,1)S(1)}, u32[]{:S(2)}, u32[]{:S(2)}) collective-permute-start(bf16[2,64,1024]{2,1,0:T(8,128)(2,1)S(1)} %get-tuple-element.84), channel_id=1, source_target_pairs={{0,2},{2,4},{4,6},{6,7},{7,5},{5,3},{3,1},{1,0},{8,10},{10,12},{12... | collective-permute-start | bytes 786440 | tf_op jit(solution)/shard_map/ppermute | solution.py:274
  179.4 6.4 %collective-permute-start.34 = (bf16[2,64,1024]{2,1,0:T(8,128)(2,1)S(1)}, bf16[2,64,1024]{2,1,0:T(8,128)(2,1)S(1)}, u32[]{:S(2)}, u32[]{:S(2)}) collective-permute-start(bf16[2,64,1024]{2,1,0:T(8,128)(2,1)S(1)} %add_convert_fusion), channel_id=1, source_target_pairs={{2,0},{4,2},{6,4},{7,6},{5,7},{3,5},{1,3},{0,1},{10,8},{12,10},{14... | collective-permute-start | bytes 786440 | tf_op jit(solution)/shard_map/ppermute | solution.py:274
  (21 other events, 202.8 us)

commit v3 on v0

v3 whole, which is shorter than its diff:
```python
import functools

import jax
import jax.numpy as jnp
from jax import lax
from jax.experimental import pallas as pl
from jax.experimental.pallas import tpu as pltpu
from jax.sharding import PartitionSpec as P

F32 = jnp.float32
BF16 = jnp.bfloat16
NT = (((1,), (1,)), ((), ()))
TN = (((0,), (0,)), ((), ()))
SMEM = pl.BlockSpec(memory_space=pltpu.SMEM)
VMEM = pl.BlockSpec(memory_space=pltpu.VMEM)
PARAMS = pltpu.CompilerParams(vmem_limit_bytes=24 * 2**20)


def ring_pairs(count):
    order = list(range(0, count, 2)) + list(range(count - 1 - count % 2, 0, -2))
    right = [(order[i], order[(i + 1) % count]) for i in range(count)]
    return right, [(b, a) for a, b in right]


def in_vmem(*arrays):
    return [pltpu.with_memory_space_constraint(array, pltpu.VMEM) for array in arrays]


def cost(flops, moved):
    return pl.CostEstimate(flops=flops, bytes_accessed=moved, transcendentals=0)


def owner_row(where, replicas, part, offset):
    at = lax.rem(where[0] + (offset + replicas), replicas)
    owner = jnp.where(at < replicas // 2, 2 * at, 2 * (replicas - 1 - at) + 1)
    return pl.multiple_of(owner * part, part)


def prepare_kernel(where, x, taps_t):
    seqs, samples, channels = x.shape
    dilation = jnp.left_shift(jnp.int32(1), where[1])
    wide = 128
    for s in range(seqs):
        columns = slice(s * samples, (s + 1) * samples)
        for at in range(0, channels, wide):
            turned = x[s, :, at : at + wide].astype(F32).T
            position = lax.broadcasted_iota(jnp.int32, turned.shape, 1)
            taps_t[at : at + wide, columns] = turned.astype(BF16)
            for k in (1, 2):
                delayed = jnp.where(position >= k * dilation, pltpu.roll(turned, k * dilation, 1), 0.0)
                taps_t[k * channels + at : k * channels + at + wide, columns] = delayed.astype(BF16)


def prepare_call(where, x):
    seqs, samples, channels = x.shape
    return pl.pallas_call(
        prepare_kernel,
        out_shape=pltpu.VMEM((3 * channels, seqs * samples), BF16),
        in_specs=[SMEM, VMEM],
        out_specs=VMEM,
        compiler_params=PARAMS,
        cost_estimate=cost(2**20, 2**22),
    )(where, x)


def tap_rows(taps_t, row, part, columns, first=0, last=3):
    channels = taps_t.shape[0] // 3
    return jnp.concatenate(
        [taps_t[pl.ds(k * channels + row, part), columns] for k in range(first, last)], axis=0
    )


def partial_kernel(replicas, offsets, where, taps_t, *refs):
    count = len(offsets)
    convs, mixes, refs = refs[:count], refs[count : 2 * count], refs[2 * count :]
    acc, w = refs[-2:]
    rows = taps_t.shape[1]
    channels = w.shape[0] // 4
    part = convs[0].shape[1]
    chunk = min(256, rows)
    places = [owner_row(where, replicas, part, offset) for offset in offsets]
    for at in range(0, rows, chunk):
        columns = slice(at, at + chunk)
        total = refs[0][columns, :] if len(refs) == 4 else None
        for row, conv in zip(places, convs):
            term = lax.dot_general(
                tap_rows(taps_t, row, part, columns),
                conv[...].reshape(3 * part, -1),
                TN,
                preferred_element_type=F32,
            )
            total = term if total is None else total + term
        acc[columns, :] = total
    for row, conv, mix in zip(places, convs, mixes):
        for k in range(3):
            w[pl.ds(k * channels + row, part), :] = conv[k]
        w[pl.ds(3 * channels + row, part), :] = mix[0]


def partial_call(replicas, offsets, where, taps_t, convs, mixes, held):
    part, wide = convs[0].shape[1:]
    rows = taps_t.shape[1]
    count = len(offsets)
    inputs = in_vmem(taps_t, *convs, *mixes, *held)
    return pl.pallas_call(
        functools.partial(partial_kernel, replicas, offsets),
        out_shape=[pltpu.VMEM((rows, wide), F32), pltpu.VMEM((2 * wide, wide), BF16)],
        in_specs=[SMEM] + [VMEM] * len(inputs),
        out_specs=[VMEM] * 2,
        input_output_aliases={len(inputs) - 1 + i: i for i in range(len(held))},
        compiler_params=PARAMS,
        cost_estimate=cost(6 * rows * part * count * wide, 2**20),
    )(where, *inputs)


def forward_kernel(replicas, index, store, where, taps_t, conv_a, conv_b, mix, acc, w_in, *refs):
    a1, a2, hid_t = refs[:3]
    samples, channels = a1.shape
    part = mix.shape[1]
    row = owner_row(where, replicas, part, replicas // 2)
    ahead = conv_a.shape[0]
    chunk = min(256, samples)
    for at in range(0, samples, chunk):
        columns = slice(index * samples + at, index * samples + at + chunk)
        pre = acc[columns, :]
        for conv, first, last in ((conv_a, 0, ahead), (conv_b, ahead, 3)):
            pre = pre + lax.dot_general(
                tap_rows(taps_t, row, part, columns, first, last),
                conv[...].reshape((last - first) * part, -1),
                TN,
                preferred_element_type=F32,
            )
        filt = jnp.tanh(pre[:, :channels])
        gate = jax.nn.sigmoid(pre[:, channels:])
        a1[at : at + chunk, :] = (gate * (1.0 - filt * filt)).astype(BF16)
        a2[at : at + chunk, :] = (filt * gate * (1.0 - gate)).astype(BF16)
        hid_t[:, at : at + chunk] = (filt * gate).T.astype(BF16)
    if store:
        w = refs[3]
        blocks = [conv_a[k] for k in range(ahead)] + [conv_b[k] for k in range(3 - ahead)] + [mix[0]]
        for k, block in enumerate(blocks):
            w[pl.ds(k * channels + row, part), :] = block


def forward_call(replicas, index, micro, store, where, taps_t, conv_a, conv_b, mix, acc, w):
    rows, wide = acc.shape
    channels = wide // 2
    samples = rows // micro
    inputs = in_vmem(taps_t, conv_a, conv_b, mix, acc, w)
    return pl.pallas_call(
        functools.partial(forward_kernel, replicas, index, store),
        out_shape=[pltpu.VMEM((samples, channels), BF16)] * 2
        + [pltpu.VMEM((channels, samples), BF16)]
        + ([pltpu.VMEM(w.shape, BF16)] if store else []),
        in_specs=[SMEM] + [VMEM] * 6,
        out_specs=[VMEM] * (4 if store else 3),
        input_output_aliases={6: 3} if store else {},
        compiler_params=PARAMS,
        cost_estimate=cost(2**28, 2**22),
    )(where, *inputs)


def chain_kernel(stage, index, where, g, skip, a1, a2, w, *refs):
    pg, ig, gk, bt = refs[-4:]
    samples, channels = g.shape
    padding = bt.shape[1] - samples
    dilation = 2**stage

    @pl.when(where[1] == stage)
    def _():
        for k in (1, 2):
            bt[k, samples:, :] = jnp.zeros((padding, channels), F32)
        chunk = samples // 2
        for at in range(samples - chunk, -1, -chunk):
            rows = slice(at, at + chunk)
            hid = lax.dot_general(
                g[rows, :], w[3 * channels :, :channels], NT, preferred_element_type=F32
            ) + lax.dot_general(
                skip[index, rows, :], w[3 * channels :, channels:], NT, preferred_element_type=F32
            )
            pg[rows, :channels] = (hid * a1[rows, :].astype(F32)).astype(BF16)
            pg[rows, channels:] = (hid * a2[rows, :].astype(F32)).astype(BF16)
            for k in range(3):
                bt[k, rows, :] = lax.dot_general(
                    pg[rows, :], w[k * channels : (k + 1) * channels, :], NT, preferred_element_type=F32
                )
            piece = 64
            for first in range(at + chunk - piece, at - 1, -piece):
                last = first + piece
                total = g[first:last, :].astype(F32) + bt[0, first:last, :]
                total = total + bt[1, first + dilation : last + dilation, :]
                total = total + bt[2, first + 2 * dilation : last + 2 * dilation, :]
                ig[first:last, :] = total.astype(BF16)
        gk[...] = g[...]


def chain_call(stage, index, padding, where, g, skip, a1, a2, w, held):
    samples, channels = g.shape
    tile = (samples, channels)
    inputs = in_vmem(g, skip, a1, a2, w, *held)
    return pl.pallas_call(
        functools.partial(chain_kernel, stage, index),
        out_shape=[pltpu.VMEM((samples, 2 * channels), BF16), pltpu.VMEM(tile, BF16), pltpu.VMEM(tile, BF16)],
        in_specs=[SMEM] + [VMEM] * len(inputs),
        out_specs=[VMEM] * 3,
        scratch_shapes=[pltpu.VMEM((3, samples + padding, channels), F32)],
        input_output_aliases={6 + i: i for i in range(len(held))},
        compiler_params=PARAMS,
        cost_estimate=cost(8 * samples * channels * channels, 2**22),
    )(where, *inputs)


def term_kernel(replicas, offsets, micro, where, taps_t, skip, *refs):
    hids, refs = refs[:micro], refs[micro:]
    pgs, refs = refs[:micro], refs[micro:]
    gs, refs = refs[:micro], refs[micro:]
    outs = refs[-2 * len(offsets) :]
    samples, wide = pgs[0].shape
    channels = wide // 2
    part = channels // replicas
    places = [owner_row(where, replicas, part, offset) for offset in offsets]
    conv, mix_g, mix_s = None, None, None
    for m in range(micro):
        columns = slice(m * samples, (m + 1) * samples)
        lhs = jnp.concatenate([tap_rows(taps_t, row, part, columns) for row in places], axis=0)
        lhs_mix = jnp.concatenate([hids[m][pl.ds(row, part), :] for row in places], axis=0)
        new = [
            jnp.dot(lhs, pgs[m][...], preferred_element_type=F32),
            jnp.dot(lhs_mix, gs[m][...], preferred_element_type=F32),
            jnp.dot(lhs_mix, skip[m], preferred_element_type=F32),
        ]
        conv, mix_g, mix_s = new if m == 0 else (conv + new[0], mix_g + new[1], mix_s + new[2])
    for slot in range(len(offsets)):
        low, high = outs[2 * slot : 2 * slot + 2]
        at = slot * 3 * part
        for k, target in enumerate((low.at[0], low.at[1], high.at[0])):
            target[...] = conv[at + k * part : at + (k + 1) * part, :].astype(low.dtype)
        here = slice(slot * part, (slot + 1) * part)
        high[1, :, :channels] = mix_g[here, :].astype(low.dtype)
        high[1, :, channels:] = mix_s[here, :].astype(low.dtype)


def term_call(replicas, offsets, kind, where, taps_t, skip, hid_t, pre_grads, gs, tokens):
    micro, samples, channels = skip.shape
    part = channels // replicas
    inputs = in_vmem(taps_t, skip, *hid_t, *pre_grads, *gs, *tokens)
    outs = 2 * len(offsets)
    return pl.pallas_call(
        functools.partial(term_kernel, replicas, offsets, micro),
        out_shape=[pltpu.VMEM((2, part, 2 * channels), kind)] * outs,
        in_specs=[SMEM] + [VMEM] * len(inputs),
        out_specs=[VMEM] * outs,
        compiler_params=PARAMS,
        cost_estimate=cost(2**29 * len(offsets), 2**20),
    )(where, *inputs)


def add_kernel(mine_r, mine_l, got_r, got_l, *refs):
    out_r, out_l = refs[-2:]
    out_r[...] = (mine_r[...].astype(F32) + got_r[...].astype(F32)).astype(BF16)
    out_l[...] = (mine_l[...].astype(F32) + got_l[...].astype(F32)).astype(BF16)


def add_call(mine, got, tokens):
    inputs = in_vmem(*mine, *got, *tokens)
    return pl.pallas_call(
        add_kernel,
        out_shape=[pltpu.VMEM(got[0].shape, BF16)] * 2,
        in_specs=[VMEM] * len(inputs),
        out_specs=[VMEM] * 2,
        compiler_params=PARAMS,
        cost_estimate=cost(2**18, 2**19),
    )(*inputs)


def final_kernel(low, high, low_r, low_l, high_r, high_l, conv, mix):
    conv[0:2] = low[...] + (low_r[...].astype(F32) + low_l[...].astype(F32))
    total = high[...] + (high_r[...].astype(F32) + high_l[...].astype(F32))
    conv[2] = total[0]
    mix[...] = total[1]


def final_call(*blocks):
    part, wide = blocks[0].shape[1:]
    return pl.pallas_call(
        final_kernel,
        out_shape=[jax.ShapeDtypeStruct((3, part, wide), F32), jax.ShapeDtypeStruct((part, wide), F32)],
        in_specs=[VMEM] * 6,
        out_specs=[VMEM] * 2,
        compiler_params=PARAMS,
        cost_estimate=cost(2**19, 2**20),
    )(*in_vmem(*blocks))


def local(x_ckpt, top_cot, skip_cot, w_conv, w_mix):
    sections = lax.axis_size("pipe")
    replicas = lax.axis_size("dp")
    replica = lax.axis_index("dp")
    micro, seqs, samples, channels = x_ckpt.shape[1:]
    block = seqs * samples
    half = replicas // 2
    right, left = ring_pairs(replicas)
    place = jnp.where(replica % 2 == 0, replica // 2, replicas - 1 - replica // 2)
    where = jnp.stack([place, lax.axis_index("pipe")]).astype(jnp.int32)

    taps_t = prepare_call(where, x_ckpt[0].reshape(micro * seqs, samples, channels))
    conv = w_conv[0].transpose(1, 0, 2)
    conv_r, conv_l, mix_r, mix_l = conv, conv, w_mix, w_mix
    held = partial_call(replicas, (0,), where, taps_t, [conv], [w_mix], [])
    for step in range(1, half):
        conv_r = lax.ppermute(conv_r, "dp", right)
        conv_l = lax.ppermute(conv_l, "dp", left)
        mix_r = lax.ppermute(mix_r, "dp", right)
        mix_l = lax.ppermute(mix_l, "dp", left)
        held = partial_call(
            replicas, (-step, step), where, taps_t, [conv_r, conv_l], [mix_r, mix_l], held
        )
    acc, w_full = held
    conv_r = lax.ppermute(conv_r[:2], "dp", right)
    conv_l = lax.ppermute(conv_l[2:], "dp", left)
    mix_l = lax.ppermute(mix_l, "dp", left)

    skip = skip_cot.reshape(micro, block, channels)
    g = list(top_cot.reshape(micro, block, channels))
    padding = max(16, 2 * 2 ** (sections - 1))
    hid_t, held, ready = [], [()] * micro, []
    for m in range(micro):
        a1, a2, hid, *stored = forward_call(
            replicas, m, micro, m == 0, where, taps_t, conv_r, conv_l, mix_l, acc, w_full
        )
        if stored:
            w_full = stored[0]
        hid_t.append(hid)
        ready.append((a1, a2))
    for stage in range(sections - 1, -1, -1):
        for m in range(micro):
            held[m] = chain_call(stage, m, padding, where, g[m], skip, *ready[m], w_full, held[m])
            if stage:
                g[m] = lax.ppermute(held[m][1], "pipe", [(stage, stage - 1)])
    pre_grads, cots, gs = zip(*held)
    cot = jnp.stack(cots, axis=0)

    def terms(dist, tokens, kind=BF16):
        offsets = (dist,) if dist in (0, half) else (dist, -dist)
        return term_call(replicas, offsets, kind, where, taps_t, skip, hid_t, pre_grads, gs, tokens)

    def send(to_right, to_left):
        return lax.ppermute(to_right, "dp", right), lax.ppermute(to_left, "dp", left)

    low, high = terms(half, ())
    got_one = send(low, high)
    mine = terms(half - 1, (low,))
    got_two = send(mine[1], mine[2])
    token = ()
    for dist in range(half - 1, 0, -1):
        if dist < half - 1:
            out = add_call((mine[1], mine[2]), got_two, token)
            token = out[:1]
            got_two = send(*out)
        out = add_call((mine[0], mine[3]), got_one, token)
        token = out[:1]
        got_one = send(*out)
        if dist > 1:
            mine = terms(dist - 1, token)
    low, high = terms(0, token, F32)
    share_conv, share_mix = final_call(low, high, got_one[0], got_two[1], got_two[0], got_one[1])
    return (
        cot.reshape(1, micro, seqs, samples, channels),
        share_conv.transpose(1, 0, 2)[None],
        share_mix[None],
    )


def solution(mesh):
    placed = (
        P("pipe", None, "dp", None, None),
        P(None, "dp", None, None),
        P(None, "dp", None, None),
        P("pipe", "dp", None, None),
        P("pipe", "dp", None),
    )
    return jax.shard_map(
        local,
        mesh=mesh,
        in_specs=placed,
        out_specs=(
            P("pipe", None, "dp", None, None),
            P("pipe", "dp", None, None),
            P("pipe", "dp", None),
        ),
        check_vma=False,
    )
```

time: 412 us -> 133 us (0.32)
  waiting for transfers between devices: 272 us -> 55.7 us
  other arithmetic: 70 us -> 1.14 us
  Pallas kernels: 0 us -> 34.4 us
  starting transfers between devices: 6.51 us -> 38 us
  local copies, waits for them, and re-layouts: 33.5 us -> 2.53 us
  matrix products: 14.9 us -> 0 us
  between operations: 13.8 us -> 1.01 us
    reduce_scatter x1 -> x0, waiting for transfers between devices: 149 us -> none  [local(): shares = lax.psum_scatter(grad_acc, 'dp', scatter_dimension=0, tiled=True)]
    all_gather x2 -> x0, waiting for transfers between devices: 106 us -> none  [the longest x1 61.5 us: local(): lax.all_gather(w_conv, 'dp', axis=1, tiled=True)]
    add x5 -> x0, other arithmetic: 53.6 us -> none  [step_fn(): grad_acc = grad_acc + grad_term]
    ppermute x5 -> x35, waiting for transfers between devices: 16.4 us -> 55.7 us  [the longest x3 15.8 us: local(): conv_r = lax.ppermute(conv_r, 'dp', right)]
    pallas_call x0 -> x26, Pallas kernels: none -> 34.4 us  [the longest x8 10.5 us: chain_call(): pl.pallas_call(functools.partial(chain_kernel, stage, index), out_shape=[...]
    ppermute x5 -> x35, starting transfers between devices: 6.4 us -> 38 us  [the longest x7 11.4 us: send(): lax.ppermute(to_right, 'dp', right)]
    dot_general x10 -> x0, matrix products: 14.9 us -> none  [the longest x2 3.69 us: layer_back(): jnp.einsum('slkc,ckn->sln', tapped_x, conv_w, preferred_element_type=jnp....]
    another operation x8 -> x1, local copies, waits for them, and re-layouts: 13.6 us -> 1.27 us  [local(): g = list(top_cot.reshape(micro, block, channels))]
  transfers between devices with their start and end apart: 8 -> 35, of which waited for: 5 -> 19; matrix products, arithmetic and copies ran while one was open for 13% -> 2% of each run, Pallas kernels for 0% -> 20%
where the time goes in v3:
time: 133 us
  waiting for transfers between devices  55.7 us (42%)
  starting transfers between devices  38 us (29%)
  Pallas kernels  34.4 us (26%)
  local copies, waits for them, and re-layouts  2.53 us (2%)
    ppermute x3, waiting for transfers between devices, local(): conv_r = lax.ppermute(conv_r, 'dp', right)  15.8 us
    ppermute x6, waiting for transfers between devices, local(): g[m] = lax.ppermute(held[m][1], 'pipe', [(stage, stage - 1)])  15.7 us
    ppermute x7, starting transfers between devices, send(): lax.ppermute(to_right, 'dp', right)  11.4 us
    pallas_call x8, Pallas kernels, chain_call(): pl.pallas_call(functools.partial(chain_kernel, stage, index), out_shape=[...  10.5 us
    ppermute x7, waiting for transfers between devices, send(): lax.ppermute(to_left, 'dp', left)  9.54 us
    ppermute x7, waiting for transfers between devices, send(): lax.ppermute(to_right, 'dp', right)  8.66 us
    pallas_call x4, Pallas kernels, partial_call(): pl.pallas_call(functools.partial(partial_kernel, replicas, offsets), out_...  8.62 us
    pallas_call x5, Pallas kernels, term_call(): pl.pallas_call(functools.partial(term_kernel, replicas, offsets, micro),...  8.34 us
  transfers between devices with their start and end apart: 35, of which 19 were waited for; matrix products, arithmetic and copies ran while one was open for 2% of the time, Pallas kernels for 20%

profile of v3, /device:TPU:0, one launch (start us, length us, event | category | flops | bytes accessed | tf_op | source)
XLA Modules:
  0.0 132.7 jit_solution(3925596883052464824)
XLA Ops:
  0.6 3.1 %collective-permute-start = (bf16[3,64,1024]{2,1,0:T(8,128)(2,1)}, bf16[3,64,1024]{2,1,0:T(8,128)(2,1)S(1)}, u32[]{:S(2)}, u32[]{:S(2)}) collective-permute-start(bf16[3,64,1024]{2,1,0:T(8,128)(2,1)} %bitcast.37), channel_id=1, source_target_pairs={{0,2},{2,4},{4,6},{6,7},{7,5},{5,3},{3,1},{1,0},{8,10},{10,12},{12... | collective-permute-start | bytes 1179656 | tf_op jit(solution)/shard_map/ppermute | solution.py:311
  3.7 9.3 %collective-permute-done.refs_0_ = bf16[3,64,1024]{2,1,0:T(8,128)(2,1)S(1)} collective-permute-done((bf16[3,64,1024]{2,1,0:T(8,128)(2,1)}, bf16[3,64,1024]{2,1,0:T(8,128)(2,1)S(1)}, u32[]{:S(2)}, u32[]{:S(2)}) %collective-permute-start) | collective-permute-done | bytes 393248 | tf_op jit(solution)/shard_map/ppermute | solution.py:311
  13.0 1.8 %collective-permute-start.1 = (bf16[3,64,1024]{2,1,0:T(8,128)(2,1)S(1)}, bf16[3,64,1024]{2,1,0:T(8,128)(2,1)S(1)}, u32[]{:S(2)}, u32[]{:S(2)}) collective-permute-start(bf16[3,64,1024]{2,1,0:T(8,128)(2,1)S(1)} %collective-permute-done.refs_0_), channel_id=1, source_target_pairs={{0,2},{2,4},{4,6},{6,7},{7,5},{5,3},{3,1},{1,0},{8,10},{10,12},{12... | collective-permute-start | bytes 1179656 | tf_op jit(solution)/shard_map/ppermute | solution.py:311
  15.0 1.7 %collective-permute-start.8 = (bf16[1,64,1024]{2,1,0:T(8,128)(2,1)}, bf16[1,64,1024]{2,1,0:T(8,128)(2,1)S(1)}, u32[]{:S(2)}, u32[]{:S(2)}) collective-permute-start(bf16[1,64,1024]{2,1,0:T(8,128)(2,1)} %refs_1_.1), channel_id=1, source_target_pairs={{2,0},{4,2},{6,4},{7,6},{5,7},{3,5},{1,3},{0,1},{10,8},{12,10},{14... | collective-permute-start | bytes 393224 | tf_op jit(solution)/shard_map/ppermute | solution.py:314
  16.7 6.5 %collective-permute-done.1.refs_0_ = bf16[3,64,1024]{2,1,0:T(8,128)(2,1)S(1)} collective-permute-done((bf16[3,64,1024]{2,1,0:T(8,128)(2,1)S(1)}, bf16[3,64,1024]{2,1,0:T(8,128)(2,1)S(1)}, u32[]{:S(2)}, u32[]{:S(2)}) %collective-permute-start.1) | collective-permute-done | bytes 393248 | tf_op jit(solution)/shard_map/ppermute | solution.py:311
  24.8 1.6 %collective-permute-start.12 = (bf16[1,64,1024]{2,1,0:T(8,128)(2,1)}, bf16[1,64,1024]{2,1,0:T(8,128)(2,1)}, u32[]{:S(2)}, u32[]{:S(2)}) collective-permute-start(bf16[1,64,1024]{2,1,0:T(8,128)(2,1)} %refs_1_.1), channel_id=1, source_target_pairs={{0,2},{2,4},{4,6},{6,7},{7,5},{5,3},{3,1},{1,0},{8,10},{10,12},{12... | collective-permute-start | bytes 393224 | tf_op jit(solution)/shard_map/ppermute | solution.py:313
  30.6 5.0 %collective-permute-done.12.refs_2_ = bf16[1,64,1024]{2,1,0:T(8,128)(2,1)} collective-permute-done((bf16[1,64,1024]{2,1,0:T(8,128)(2,1)}, bf16[1,64,1024]{2,1,0:T(8,128)(2,1)}, u32[]{:S(2)}, u32[]{:S(2)}) %collective-permute-start.12) | collective-permute-done | bytes 131104 | tf_op jit(solution)/shard_map/ppermute | solution.py:313
  38.9 1.9 %shard_map.76.taps_t = bf16[1536,1024]{1,0:T(8,128)(2,1)S(1)} custom-call(s32[2]{0:T(128)S(1)} %pad_add_fusion.where, bf16[2,512,512]{2,1,0:T(8,128)(2,1)S(1)} %bitcast.36), custom_call_target="tpu_custom_call" | custom-call | flops 1048576 | bytes 4194304 | tf_op jit(solution)/shard_map/pallas_call | solution.py:56
  43.4 1.6 %collective-permute-start.14 = (bf16[1,64,1024]{2,1,0:T(8,128)(2,1)S(1)}, bf16[1,64,1024]{2,1,0:T(8,128)(2,1)S(1)}, u32[]{:S(2)}, u32[]{:S(2)}) collective-permute-start(bf16[1,64,1024]{2,1,0:T(8,128)(2,1)S(1)} %collective-permute-done.13.refs_2_), channel_id=1, source_target_pairs={{0,2},{2,4},{4,6},{6,7},{7,5},{5,3},{3,1},{1,0},{8,10},{10,12},{12... | collective-permute-start | bytes 393224 | tf_op jit(solution)/shard_map/ppermute | solution.py:313
  45.5 2.6 %shard_map.78 = (f32[1024,1024]{1,0:T(8,128)S(1)}, bf16[2048,1024]{1,0:T(8,128)(2,1)S(1)}) custom-call(s32[2]{0:T(128)S(1)} %pad_add_fusion.where, bf16[1536,1024]{1,0:T(8,128)(2,1)S(1)} %shard_map.76.taps_t, bf16[3,64,1024]{2,1,0:T(8,128)(2,1)S(1)} %collective-permute-done.refs_0_, ...), custom_call_target="tpu_custom_call", output_to_operand_aliasing={{0}: (6, {}), {1}: (7, {})} | custom-call | flops 805306368 | bytes 1048576 | tf_op jit(solution)/shard_map/pallas_call | solution.py:105
  49.0 2.6 %shard_map.79 = (f32[1024,1024]{1,0:T(8,128)S(1)}, bf16[2048,1024]{1,0:T(8,128)(2,1)S(1)}) custom-call(s32[2]{0:T(128)S(1)} %pad_add_fusion.where, bf16[1536,1024]{1,0:T(8,128)(2,1)S(1)} %shard_map.76.taps_t, bf16[3,64,1024]{2,1,0:T(8,128)(2,1)S(1)} %collective-permute-done.1.refs_0_, ...), custom_call_target="tpu_custom_call", output_to_operand_aliasing={{0}: (6, {}), {1}: (7, {})} | custom-call | flops 805306368 | bytes 1048576 | tf_op jit(solution)/shard_map/pallas_call | solution.py:105
  51.5 2.2 %shard_map.80 = (f32[1024,1024]{1,0:T(8,128)S(1)}, bf16[2048,1024]{1,0:T(8,128)(2,1)S(1)}) custom-call(s32[2]{0:T(128)S(1)} %pad_add_fusion.where, bf16[1536,1024]{1,0:T(8,128)(2,1)S(1)} %shard_map.76.taps_t, bf16[3,64,1024]{2,1,0:T(8,128)(2,1)S(1)} %collective-permute-done.2.refs_0_, ...), custom_call_target="tpu_custom_call", output_to_operand_aliasing={{0}: (6, {}), {1}: (7, {})} | custom-call | flops 805306368 | bytes 1048576 | tf_op jit(solution)/shard_map/pallas_call | solution.py:105
  53.8 1.7 %shard_map.81 = (bf16[512,512]{1,0:T(8,128)(2,1)S(1)}, bf16[512,512]{1,0:T(8,128)(2,1)S(1)}, bf16[512,512]{1,0:T(8,128)(2,1)S(1)}, bf16[2048,1024]{1,0:T(8,128)(2,1)S(1)}) custom-call(s32[2]{0:T(128)S(1)} %pad_add_fusion.where, bf16[1536,1024]{1,0:T(8,128)(2,1)S(1)} %shard_map.76.taps_t, ...), custom_call_target="tpu_custom_call", output_to_operand_aliasing={{3}: (6, {})} | custom-call | flops 268435456 | bytes 4194304 | tf_op jit(solution)/shard_map/pallas_call | solution.py:150
  56.7 1.7 %shard_map.86 = (bf16[512,512]{1,0:T(8,128)(2,1)S(1)}, bf16[512,512]{1,0:T(8,128)(2,1)S(1)}, bf16[512,512]{1,0:T(8,128)(2,1)S(1)}) custom-call(s32[2]{0:T(128)S(1)} %pad_add_fusion.where, bf16[1536,1024]{1,0:T(8,128)(2,1)S(1)} %shard_map.76.taps_t, bf16[2,64,1024]{2,1,0:T(8,128)(2,1)S(1)} %collective-permute-done.3.conv_a, ...), custom_call_target="tpu_custom_call" | custom-call | flops 268435456 | bytes 4194304 | tf_op jit(solution)/shard_map/pallas_call | solution.py:150
  66.1 13.7 %collective-permute-done.17.g = bf16[512,512]{1,0:T(8,128)(2,1)S(1)} collective-permute-done((bf16[512,512]{1,0:T(8,128)(2,1)S(1)}, bf16[512,512]{1,0:T(8,128)(2,1)S(1)}, u32[]{:S(2)}, u32[]{:S(2)}) %collective-permute-start.17) | collective-permute-done | bytes 524320 | tf_op jit(solution)/shard_map/ppermute | solution.py:339
  79.8 3.6 %shard_map.85 = (bf16[512,1024]{1,0:T(8,128)(2,1)S(1)}, bf16[512,512]{1,0:T(8,128)(2,1)S(1)}, bf16[512,512]{1,0:T(8,128)(2,1)S(1)}) custom-call(s32[2]{0:T(128)S(1)} %pad_add_fusion.where, bf16[512,512]{1,0:T(8,128)(2,1)S(1)} %collective-permute-done.17.g, ...), custom_call_target="tpu_custom_call", output_to_operand_aliasing={{0}: (6, {}), {1}: (7, {}), {2}: (8, {})} | custom-call | flops 1073741824 | bytes 4194304 | tf_op jit(solution)/shard_map/pallas_call | solution.py:201
  83.4 2.0 %collective-permute-done.20.g = bf16[512,512]{1,0:T(8,128)(2,1)S(1)} collective-permute-done((bf16[512,512]{1,0:T(8,128)(2,1)S(1)}, bf16[512,512]{1,0:T(8,128)(2,1)S(1)}, u32[]{:S(2)}, u32[]{:S(2)}) %collective-permute-start.20) | collective-permute-done | bytes 524320 | tf_op jit(solution)/shard_map/ppermute | solution.py:339
  85.4 3.4 %shard_map.90 = (bf16[512,1024]{1,0:T(8,128)(2,1)S(1)}, bf16[512,512]{1,0:T(8,128)(2,1)S(1)}, bf16[512,512]{1,0:T(8,128)(2,1)S(1)}) custom-call(s32[2]{0:T(128)S(1)} %pad_add_fusion.where, bf16[512,512]{1,0:T(8,128)(2,1)S(1)} %collective-permute-done.20.g, ...), custom_call_target="tpu_custom_call", output_to_operand_aliasing={{0}: (6, {}), {1}: (7, {}), {2}: (8, {})} | custom-call | flops 1073741824 | bytes 4194304 | tf_op jit(solution)/shard_map/pallas_call | solution.py:201
  90.3 1.6 %collective-permute-start.21 = (bf16[2,64,1024]{2,1,0:T(8,128)(2,1)S(1)}, bf16[2,64,1024]{2,1,0:T(8,128)(2,1)S(1)}, u32[]{:S(2)}, u32[]{:S(2)}) collective-permute-start(bf16[2,64,1024]{2,1,0:T(8,128)(2,1)S(1)} %get-tuple-element.109.refs_6_), channel_id=1, source_target_pairs={{0,2},{2,4},{4,6},{6,7},{7,5},{5,3},{3,1},{1,0},{8,10},{10,12},{12... | collective-permute-start | bytes 786440 | tf_op jit(solution)/shard_map/ppermute | solution.py:348
  92.3 1.8 %shard_map.92 = (bf16[2,64,1024]{2,1,0:T(8,128)(2,1)S(1)}, bf16[2,64,1024]{2,1,0:T(8,128)(2,1)S(1)}, bf16[2,64,1024]{2,1,0:T(8,128)(2,1)S(1)}, bf16[2,64,1024]{2,1,0:T(8,128)(2,1)S(1)}) custom-call(s32[2]{0:T(128)S(1)} %pad_add_fusion.where, bf16[1536,1024]{1,0:T(8,128)(2,1)S(1)} %shard_map.76.taps_t, bf16[2,512,512]{2,1,0:T(8,128)(2,1)S(1)} %bitcast.30, ...), custom_call_target="tpu_custom_call" | custom-call | flops 1073741824 | bytes 1048576 | tf_op jit(solution)/shard_map/pallas_call | solution.py:248
  94.2 1.6 %collective-permute-start.25 = (bf16[2,64,1024]{2,1,0:T(8,128)(2,1)S(1)}, bf16[2,64,1024]{2,1,0:T(8,128)(2,1)S(1)}, u32[]{:S(2)}, u32[]{:S(2)}) collective-permute-start(bf16[2,64,1024]{2,1,0:T(8,128)(2,1)S(1)} %get-tuple-element.119), channel_id=1, source_target_pairs={{0,2},{2,4},{4,6},{6,7},{7,5},{5,3},{3,1},{1,0},{8,10},{10,12},{12... | collective-permute-start | bytes 786440 | tf_op jit(solution)/shard_map/ppermute | solution.py:348
  96.2 3.3 %collective-permute-done.21.got_r = bf16[2,64,1024]{2,1,0:T(8,128)(2,1)S(1)} collective-permute-done((bf16[2,64,1024]{2,1,0:T(8,128)(2,1)S(1)}, bf16[2,64,1024]{2,1,0:T(8,128)(2,1)S(1)}, u32[]{:S(2)}, u32[]{:S(2)}) %collective-permute-start.21) | collective-permute-done | bytes 262176 | tf_op jit(solution)/shard_map/ppermute | solution.py:348
  101.2 1.6 %collective-permute-start.23 = (bf16[2,64,1024]{2,1,0:T(8,128)(2,1)S(1)}, bf16[2,64,1024]{2,1,0:T(8,128)(2,1)S(1)}, u32[]{:S(2)}, u32[]{:S(2)}) collective-permute-start(bf16[2,64,1024]{2,1,0:T(8,128)(2,1)S(1)} %get-tuple-element.113.refs_6_.refs_0_), channel_id=1, source_target_pairs={{0,2},{2,4},{4,6},{6,7},{7,5},{5,3},{3,1},{1,0},{8,10},{10,12},{12... | collective-permute-start | bytes 786440 | tf_op jit(solution)/shard_map/ppermute | solution.py:348
  103.2 1.8 %shard_map.94 = (bf16[2,64,1024]{2,1,0:T(8,128)(2,1)S(1)}, bf16[2,64,1024]{2,1,0:T(8,128)(2,1)S(1)}, bf16[2,64,1024]{2,1,0:T(8,128)(2,1)S(1)}, bf16[2,64,1024]{2,1,0:T(8,128)(2,1)S(1)}) custom-call(s32[2]{0:T(128)S(1)} %pad_add_fusion.where, bf16[1536,1024]{1,0:T(8,128)(2,1)S(1)} %shard_map.76.taps_t, bf16[2,512,512]{2,1,0:T(8,128)(2,1)S(1)} %bitcast.31, ...), custom_call_target="tpu_custom_call" | custom-call | flops 1073741824 | bytes 1048576 | tf_op jit(solution)/shard_map/pallas_call | solution.py:248
  106.8 1.6 %collective-permute-start.29 = (bf16[2,64,1024]{2,1,0:T(8,128)(2,1)S(1)}, bf16[2,64,1024]{2,1,0:T(8,128)(2,1)S(1)}, u32[]{:S(2)}, u32[]{:S(2)}) collective-permute-start(bf16[2,64,1024]{2,1,0:T(8,128)(2,1)S(1)} %get-tuple-element.121.refs_0_), channel_id=1, source_target_pairs={{0,2},{2,4},{4,6},{6,7},{7,5},{5,3},{3,1},{1,0},{8,10},{10,12},{12... | collective-permute-start | bytes 786440 | tf_op jit(solution)/shard_map/ppermute | solution.py:348
  108.9 1.9 %collective-permute-done.23.got_r = bf16[2,64,1024]{2,1,0:T(8,128)(2,1)S(1)} collective-permute-done((bf16[2,64,1024]{2,1,0:T(8,128)(2,1)S(1)}, bf16[2,64,1024]{2,1,0:T(8,128)(2,1)S(1)}, u32[]{:S(2)}, u32[]{:S(2)}) %collective-permute-start.23) | collective-permute-done | bytes 262176 | tf_op jit(solution)/shard_map/ppermute | solution.py:348
  112.4 1.6 %collective-permute-start.27 = (bf16[2,64,1024]{2,1,0:T(8,128)(2,1)S(1)}, bf16[2,64,1024]{2,1,0:T(8,128)(2,1)S(1)}, u32[]{:S(2)}, u32[]{:S(2)}) collective-permute-start(bf16[2,64,1024]{2,1,0:T(8,128)(2,1)S(1)} %get-tuple-element.122.refs_6_.refs_0_), channel_id=1, source_target_pairs={{0,2},{2,4},{4,6},{6,7},{7,5},{5,3},{3,1},{1,0},{8,10},{10,12},{12... | collective-permute-start | bytes 786440 | tf_op jit(solution)/shard_map/ppermute | solution.py:348
  114.5 1.8 %shard_map.97 = (bf16[2,64,1024]{2,1,0:T(8,128)(2,1)S(1)}, bf16[2,64,1024]{2,1,0:T(8,128)(2,1)S(1)}, bf16[2,64,1024]{2,1,0:T(8,128)(2,1)S(1)}, bf16[2,64,1024]{2,1,0:T(8,128)(2,1)S(1)}) custom-call(s32[2]{0:T(128)S(1)} %pad_add_fusion.where, bf16[1536,1024]{1,0:T(8,128)(2,1)S(1)} %shard_map.76.taps_t, bf16[2,512,512]{2,1,0:T(8,128)(2,1)S(1)} %bitcast.32, ...), custom_call_target="tpu_custom_call" | custom-call | flops 1073741824 | bytes 1048576 | tf_op jit(solution)/shard_map/pallas_call | solution.py:248
  118.5 1.6 %collective-permute-start.33 = (bf16[2,64,1024]{2,1,0:T(8,128)(2,1)S(1)}, bf16[2,64,1024]{2,1,0:T(8,128)(2,1)S(1)}, u32[]{:S(2)}, u32[]{:S(2)}) collective-permute-start(bf16[2,64,1024]{2,1,0:T(8,128)(2,1)S(1)} %get-tuple-element.129.refs_0_), channel_id=1, source_target_pairs={{0,2},{2,4},{4,6},{6,7},{7,5},{5,3},{3,1},{1,0},{8,10},{10,12},{12... | collective-permute-start | bytes 786440 | tf_op jit(solution)/shard_map/ppermute | solution.py:348
  120.1 1.9 %collective-permute-done.27.got_r = bf16[2,64,1024]{2,1,0:T(8,128)(2,1)S(1)} collective-permute-done((bf16[2,64,1024]{2,1,0:T(8,128)(2,1)S(1)}, bf16[2,64,1024]{2,1,0:T(8,128)(2,1)S(1)}, u32[]{:S(2)}, u32[]{:S(2)}) %collective-permute-start.27) | collective-permute-done | bytes 262176 | tf_op jit(solution)/shard_map/ppermute | solution.py:348
  123.6 1.6 %collective-permute-start.31 = (bf16[2,64,1024]{2,1,0:T(8,128)(2,1)S(1)}, bf16[2,64,1024]{2,1,0:T(8,128)(2,1)S(1)}, u32[]{:S(2)}, u32[]{:S(2)}) collective-permute-start(bf16[2,64,1024]{2,1,0:T(8,128)(2,1)S(1)} %get-tuple-element.130.refs_6_), channel_id=1, source_target_pairs={{0,2},{2,4},{4,6},{6,7},{7,5},{5,3},{3,1},{1,0},{8,10},{10,12},{12... | collective-permute-start | bytes 786440 | tf_op jit(solution)/shard_map/ppermute | solution.py:348
  130.1 1.6 %collective-permute-done.34.high_l = bf16[2,64,1024]{2,1,0:T(8,128)(2,1)S(1)} collective-permute-done((bf16[2,64,1024]{2,1,0:T(8,128)(2,1)S(1)}, bf16[2,64,1024]{2,1,0:T(8,128)(2,1)S(1)}, u32[]{:S(2)}, u32[]{:S(2)}) %collective-permute-start.34) | collective-permute-done | bytes 262176 | tf_op jit(solution)/shard_map/ppermute | solution.py:348
  (77 shorter events, 40.6 us)
Async XLA Ops:
  0.6 12.3 %collective-permute-start = (bf16[3,64,1024]{2,1,0:T(8,128)(2,1)}, bf16[3,64,1024]{2,1,0:T(8,128)(2,1)S(1)}, u32[]{:S(2)}, u32[]{:S(2)}) collective-permute-start(bf16[3,64,1024]{2,1,0:T(8,128)(2,1)} %bitcast.37), channel_id=1, source_target_pairs={{0,2},{2,4},{4,6},{6,7},{7,5},{5,3},{3,1},{1,0},{8,10},{10,12},{12... | collective-permute-start | bytes 1179656 | tf_op jit(solution)/shard_map/ppermute | solution.py:311
  3.7 11.1 %collective-permute-start.4 = (bf16[3,64,1024]{2,1,0:T(8,128)(2,1)}, bf16[3,64,1024]{2,1,0:T(8,128)(2,1)S(1)}, u32[]{:S(2)}, u32[]{:S(2)}) collective-permute-start(bf16[3,64,1024]{2,1,0:T(8,128)(2,1)} %bitcast.38), channel_id=1, source_target_pairs={{2,0},{4,2},{6,4},{7,6},{5,7},{3,5},{1,3},{0,1},{10,8},{12,10},{14... | collective-permute-start | bytes 1179656 | tf_op jit(solution)/shard_map/ppermute | solution.py:312
  13.0 10.3 %collective-permute-start.1 = (bf16[3,64,1024]{2,1,0:T(8,128)(2,1)S(1)}, bf16[3,64,1024]{2,1,0:T(8,128)(2,1)S(1)}, u32[]{:S(2)}, u32[]{:S(2)}) collective-permute-start(bf16[3,64,1024]{2,1,0:T(8,128)(2,1)S(1)} %collective-permute-done.refs_0_), channel_id=1, source_target_pairs={{0,2},{2,4},{4,6},{6,7},{7,5},{5,3},{3,1},{1,0},{8,10},{10,12},{12... | collective-permute-start | bytes 1179656 | tf_op jit(solution)/shard_map/ppermute | solution.py:311
  14.8 13.1 %collective-permute-start.5 = (bf16[3,64,1024]{2,1,0:T(8,128)(2,1)S(1)}, bf16[3,64,1024]{2,1,0:T(8,128)(2,1)S(1)}, u32[]{:S(2)}, u32[]{:S(2)}) collective-permute-start(bf16[3,64,1024]{2,1,0:T(8,128)(2,1)S(1)} %collective-permute-done.4.refs_1_), channel_id=1, source_target_pairs={{2,0},{4,2},{6,4},{7,6},{5,7},{3,5},{1,3},{0,1},{10,8},{12,10},{14... | collective-permute-start | bytes 1179656 | tf_op jit(solution)/shard_map/ppermute | solution.py:312
  15.0 12.3 %collective-permute-start.8 = (bf16[1,64,1024]{2,1,0:T(8,128)(2,1)}, bf16[1,64,1024]{2,1,0:T(8,128)(2,1)S(1)}, u32[]{:S(2)}, u32[]{:S(2)}) collective-permute-start(bf16[1,64,1024]{2,1,0:T(8,128)(2,1)} %refs_1_.1), channel_id=1, source_target_pairs={{2,0},{4,2},{6,4},{7,6},{5,7},{3,5},{1,3},{0,1},{10,8},{12,10},{14... | collective-permute-start | bytes 393224 | tf_op jit(solution)/shard_map/ppermute | solution.py:314
  23.3 17.5 %collective-permute-start.2 = (bf16[3,64,1024]{2,1,0:T(8,128)(2,1)S(1)}, bf16[3,64,1024]{2,1,0:T(8,128)(2,1)S(1)}, u32[]{:S(2)}, u32[]{:S(2)}) collective-permute-start(bf16[3,64,1024]{2,1,0:T(8,128)(2,1)S(1)} %collective-permute-done.1.refs_0_), channel_id=1, source_target_pairs={{0,2},{2,4},{4,6},{6,7},{7,5},{5,3},{3,1},{1,0},{8,10},{10,12},{12... | collective-permute-start | bytes 1179656 | tf_op jit(solution)/shard_map/ppermute | solution.py:311
  24.8 10.8 %collective-permute-start.12 = (bf16[1,64,1024]{2,1,0:T(8,128)(2,1)}, bf16[1,64,1024]{2,1,0:T(8,128)(2,1)}, u32[]{:S(2)}, u32[]{:S(2)}) collective-permute-start(bf16[1,64,1024]{2,1,0:T(8,128)(2,1)} %refs_1_.1), channel_id=1, source_target_pairs={{0,2},{2,4},{4,6},{6,7},{7,5},{5,3},{3,1},{1,0},{8,10},{10,12},{12... | collective-permute-start | bytes 393224 | tf_op jit(solution)/shard_map/ppermute | solution.py:313
  27.3 9.4 %collective-permute-start.9 = (bf16[1,64,1024]{2,1,0:T(8,128)(2,1)S(1)}, bf16[1,64,1024]{2,1,0:T(8,128)(2,1)}, u32[]{:S(2)}, u32[]{:S(2)}) collective-permute-start(bf16[1,64,1024]{2,1,0:T(8,128)(2,1)S(1)} %collective-permute-done.8.refs_3_), channel_id=1, source_target_pairs={{2,0},{4,2},{6,4},{7,6},{5,7},{3,5},{1,3},{0,1},{10,8},{12,10},{14... | collective-permute-start | bytes 393224 | tf_op jit(solution)/shard_map/ppermute | solution.py:314
  27.8 20.2 %collective-permute-start.6 = (bf16[3,64,1024]{2,1,0:T(8,128)(2,1)S(1)}, bf16[3,64,1024]{2,1,0:T(8,128)(2,1)S(1)}, u32[]{:S(2)}, u32[]{:S(2)}) collective-permute-start(bf16[3,64,1024]{2,1,0:T(8,128)(2,1)S(1)} %collective-permute-done.5.refs_1_), channel_id=1, source_target_pairs={{2,0},{4,2},{6,4},{7,6},{5,7},{3,5},{1,3},{0,1},{10,8},{12,10},{14... | collective-permute-start | bytes 1179656 | tf_op jit(solution)/shard_map/ppermute | solution.py:312
  35.6 7.8 %collective-permute-start.13 = (bf16[1,64,1024]{2,1,0:T(8,128)(2,1)}, bf16[1,64,1024]{2,1,0:T(8,128)(2,1)S(1)}, u32[]{:S(2)}, u32[]{:S(2)}) collective-permute-start(bf16[1,64,1024]{2,1,0:T(8,128)(2,1)} %collective-permute-done.12.refs_2_), channel_id=1, source_target_pairs={{0,2},{2,4},{4,6},{6,7},{7,5},{5,3},{3,1},{1,0},{8,10},{10,12},{12... | collective-permute-start | bytes 393224 | tf_op jit(solution)/shard_map/ppermute | solution.py:313
  36.7 8.3 %collective-permute-start.10 = (bf16[1,64,1024]{2,1,0:T(8,128)(2,1)}, bf16[1,64,1024]{2,1,0:T(8,128)(2,1)S(1)}, u32[]{:S(2)}, u32[]{:S(2)}) collective-permute-start(bf16[1,64,1024]{2,1,0:T(8,128)(2,1)} %collective-permute-done.9.refs_3_), channel_id=1, source_target_pairs={{2,0},{4,2},{6,4},{7,6},{5,7},{3,5},{1,3},{0,1},{10,8},{12,10},{14... | collective-permute-start | bytes 393224 | tf_op jit(solution)/shard_map/ppermute | solution.py:314
  40.8 12.9 %collective-permute-start.3 = (bf16[2,64,1024]{2,1,0:T(8,128)(2,1)S(1)}, bf16[2,64,1024]{2,1,0:T(8,128)(2,1)S(1)}, u32[]{:S(2)}, u32[]{:S(2)}) collective-permute-start(bf16[2,64,1024]{2,1,0:T(8,128)(2,1)S(1)} %slice.10), channel_id=1, source_target_pairs={{0,2},{2,4},{4,6},{6,7},{7,5},{5,3},{3,1},{1,0},{8,10},{10,12},{12... | collective-permute-start | bytes 786440 | tf_op jit(solution)/shard_map/ppermute | solution.py:319
  43.4 8.1 %collective-permute-start.14 = (bf16[1,64,1024]{2,1,0:T(8,128)(2,1)S(1)}, bf16[1,64,1024]{2,1,0:T(8,128)(2,1)S(1)}, u32[]{:S(2)}, u32[]{:S(2)}) collective-permute-start(bf16[1,64,1024]{2,1,0:T(8,128)(2,1)S(1)} %collective-permute-done.13.refs_2_), channel_id=1, source_target_pairs={{0,2},{2,4},{4,6},{6,7},{7,5},{5,3},{3,1},{1,0},{8,10},{10,12},{12... | collective-permute-start | bytes 393224 | tf_op jit(solution)/shard_map/ppermute | solution.py:313
  45.0 8.7 %collective-permute-start.11 = (bf16[1,64,1024]{2,1,0:T(8,128)(2,1)S(1)}, bf16[1,64,1024]{2,1,0:T(8,128)(2,1)S(1)}, u32[]{:S(2)}, u32[]{:S(2)}) collective-permute-start(bf16[1,64,1024]{2,1,0:T(8,128)(2,1)S(1)} %collective-permute-done.10.refs_3_), channel_id=1, source_target_pairs={{2,0},{4,2},{6,4},{7,6},{5,7},{3,5},{1,3},{0,1},{10,8},{12,10},{14... | collective-permute-start | bytes 393224 | tf_op jit(solution)/shard_map/ppermute | solution.py:321
  48.1 5.7 %collective-permute-start.7 = (bf16[1,64,1024]{2,1,0:T(8,128)(2,1)S(1)}, bf16[1,64,1024]{2,1,0:T(8,128)(2,1)S(1)}, u32[]{:S(2)}, u32[]{:S(2)}) collective-permute-start(bf16[1,64,1024]{2,1,0:T(8,128)(2,1)S(1)} %slice.11), channel_id=1, source_target_pairs={{2,0},{4,2},{6,4},{7,6},{5,7},{3,5},{1,3},{0,1},{10,8},{12,10},{14... | collective-permute-start | bytes 393224 | tf_op jit(solution)/shard_map/ppermute | solution.py:320
  56.0 3.8 %collective-permute-start.15 = (bf16[512,512]{1,0:T(8,128)(2,1)S(1)}, bf16[512,512]{1,0:T(8,128)(2,1)S(1)}, u32[]{:S(2)}, u32[]{:S(2)}) collective-permute-start(bf16[512,512]{1,0:T(8,128)(2,1)S(1)} %get-tuple-element.81.refs_1_), channel_id=1, source_target_pairs={{24,16},{25,17},{26,18},{27,19},{28,20},{29,21},{30,22},{31,23}} | collective-permute-start | bytes 1572872 | tf_op jit(solution)/shard_map/ppermute | solution.py:339
  63.0 16.8 %collective-permute-start.17 = (bf16[512,512]{1,0:T(8,128)(2,1)S(1)}, bf16[512,512]{1,0:T(8,128)(2,1)S(1)}, u32[]{:S(2)}, u32[]{:S(2)}) collective-permute-start(bf16[512,512]{1,0:T(8,128)(2,1)S(1)} %get-tuple-element.87.refs_1_), channel_id=1, source_target_pairs={{8,0},{9,1},{10,2},{11,3},{12,4},{13,5},{14,6},{15,7}} | collective-permute-start | bytes 1572872 | tf_op jit(solution)/shard_map/ppermute | solution.py:339
  64.8 20.6 %collective-permute-start.20 = (bf16[512,512]{1,0:T(8,128)(2,1)S(1)}, bf16[512,512]{1,0:T(8,128)(2,1)S(1)}, u32[]{:S(2)}, u32[]{:S(2)}) collective-permute-start(bf16[512,512]{1,0:T(8,128)(2,1)S(1)} %get-tuple-element.99.refs_1_), channel_id=1, source_target_pairs={{8,0},{9,1},{10,2},{11,3},{12,4},{13,5},{14,6},{15,7}} | collective-permute-start | bytes 1572872 | tf_op jit(solution)/shard_map/ppermute | solution.py:339
  90.3 9.2 %collective-permute-start.21 = (bf16[2,64,1024]{2,1,0:T(8,128)(2,1)S(1)}, bf16[2,64,1024]{2,1,0:T(8,128)(2,1)S(1)}, u32[]{:S(2)}, u32[]{:S(2)}) collective-permute-start(bf16[2,64,1024]{2,1,0:T(8,128)(2,1)S(1)} %get-tuple-element.109.refs_6_), channel_id=1, source_target_pairs={{0,2},{2,4},{4,6},{6,7},{7,5},{5,3},{3,1},{1,0},{8,10},{10,12},{12... | collective-permute-start | bytes 786440 | tf_op jit(solution)/shard_map/ppermute | solution.py:348
  91.9 9.1 %collective-permute-start.22 = (bf16[2,64,1024]{2,1,0:T(8,128)(2,1)S(1)}, bf16[2,64,1024]{2,1,0:T(8,128)(2,1)S(1)}, u32[]{:S(2)}, u32[]{:S(2)}) collective-permute-start(bf16[2,64,1024]{2,1,0:T(8,128)(2,1)S(1)} %get-tuple-element.112), channel_id=1, source_target_pairs={{2,0},{4,2},{6,4},{7,6},{5,7},{3,5},{1,3},{0,1},{10,8},{12,10},{14... | collective-permute-start | bytes 786440 | tf_op jit(solution)/shard_map/ppermute | solution.py:348
  94.2 11.0 %collective-permute-start.25 = (bf16[2,64,1024]{2,1,0:T(8,128)(2,1)S(1)}, bf16[2,64,1024]{2,1,0:T(8,128)(2,1)S(1)}, u32[]{:S(2)}, u32[]{:S(2)}) collective-permute-start(bf16[2,64,1024]{2,1,0:T(8,128)(2,1)S(1)} %get-tuple-element.119), channel_id=1, source_target_pairs={{0,2},{2,4},{4,6},{6,7},{7,5},{5,3},{3,1},{1,0},{8,10},{10,12},{12... | collective-permute-start | bytes 786440 | tf_op jit(solution)/shard_map/ppermute | solution.py:348
  95.8 10.9 %collective-permute-start.26 = (bf16[2,64,1024]{2,1,0:T(8,128)(2,1)S(1)}, bf16[2,64,1024]{2,1,0:T(8,128)(2,1)S(1)}, u32[]{:S(2)}, u32[]{:S(2)}) collective-permute-start(bf16[2,64,1024]{2,1,0:T(8,128)(2,1)S(1)} %get-tuple-element.120), channel_id=1, source_target_pairs={{2,0},{4,2},{6,4},{7,6},{5,7},{3,5},{1,3},{0,1},{10,8},{12,10},{14... | collective-permute-start | bytes 786440 | tf_op jit(solution)/shard_map/ppermute | solution.py:348
  101.2 9.6 %collective-permute-start.23 = (bf16[2,64,1024]{2,1,0:T(8,128)(2,1)S(1)}, bf16[2,64,1024]{2,1,0:T(8,128)(2,1)S(1)}, u32[]{:S(2)}, u32[]{:S(2)}) collective-permute-start(bf16[2,64,1024]{2,1,0:T(8,128)(2,1)S(1)} %get-tuple-element.113.refs_6_.refs_0_), channel_id=1, source_target_pairs={{0,2},{2,4},{4,6},{6,7},{7,5},{5,3},{3,1},{1,0},{8,10},{10,12},{12... | collective-permute-start | bytes 786440 | tf_op jit(solution)/shard_map/ppermute | solution.py:348
  102.8 9.5 %collective-permute-start.24 = (bf16[2,64,1024]{2,1,0:T(8,128)(2,1)S(1)}, bf16[2,64,1024]{2,1,0:T(8,128)(2,1)S(1)}, u32[]{:S(2)}, u32[]{:S(2)}) collective-permute-start(bf16[2,64,1024]{2,1,0:T(8,128)(2,1)S(1)} %get-tuple-element.116), channel_id=1, source_target_pairs={{2,0},{4,2},{6,4},{7,6},{5,7},{3,5},{1,3},{0,1},{10,8},{12,10},{14... | collective-permute-start | bytes 786440 | tf_op jit(solution)/shard_map/ppermute | solution.py:348
  106.8 9.6 %collective-permute-start.29 = (bf16[2,64,1024]{2,1,0:T(8,128)(2,1)S(1)}, bf16[2,64,1024]{2,1,0:T(8,128)(2,1)S(1)}, u32[]{:S(2)}, u32[]{:S(2)}) collective-permute-start(bf16[2,64,1024]{2,1,0:T(8,128)(2,1)S(1)} %get-tuple-element.121.refs_0_), channel_id=1, source_target_pairs={{0,2},{2,4},{4,6},{6,7},{7,5},{5,3},{3,1},{1,0},{8,10},{10,12},{12... | collective-permute-start | bytes 786440 | tf_op jit(solution)/shard_map/ppermute | solution.py:348
  108.4 9.5 %collective-permute-start.30 = (bf16[2,64,1024]{2,1,0:T(8,128)(2,1)S(1)}, bf16[2,64,1024]{2,1,0:T(8,128)(2,1)S(1)}, u32[]{:S(2)}, u32[]{:S(2)}) collective-permute-start(bf16[2,64,1024]{2,1,0:T(8,128)(2,1)S(1)} %get-tuple-element.128), channel_id=1, source_target_pairs={{2,0},{4,2},{6,4},{7,6},{5,7},{3,5},{1,3},{0,1},{10,8},{12,10},{14... | collective-permute-start | bytes 786440 | tf_op jit(solution)/shard_map/ppermute | solution.py:348
  112.4 9.6 %collective-permute-start.27 = (bf16[2,64,1024]{2,1,0:T(8,128)(2,1)S(1)}, bf16[2,64,1024]{2,1,0:T(8,128)(2,1)S(1)}, u32[]{:S(2)}, u32[]{:S(2)}) collective-permute-start(bf16[2,64,1024]{2,1,0:T(8,128)(2,1)S(1)} %get-tuple-element.122.refs_6_.refs_0_), channel_id=1, source_target_pairs={{0,2},{2,4},{4,6},{6,7},{7,5},{5,3},{3,1},{1,0},{8,10},{10,12},{12... | collective-permute-start | bytes 786440 | tf_op jit(solution)/shard_map/ppermute | solution.py:348
  114.0 9.5 %collective-permute-start.28 = (bf16[2,64,1024]{2,1,0:T(8,128)(2,1)S(1)}, bf16[2,64,1024]{2,1,0:T(8,128)(2,1)S(1)}, u32[]{:S(2)}, u32[]{:S(2)}) collective-permute-start(bf16[2,64,1024]{2,1,0:T(8,128)(2,1)S(1)} %get-tuple-element.125), channel_id=1, source_target_pairs={{2,0},{4,2},{6,4},{7,6},{5,7},{3,5},{1,3},{0,1},{10,8},{12,10},{14... | collective-permute-start | bytes 786440 | tf_op jit(solution)/shard_map/ppermute | solution.py:348
  118.0 10.5 %collective-permute-start.32 = (bf16[2,64,1024]{2,1,0:T(8,128)(2,1)S(1)}, bf16[2,64,1024]{2,1,0:T(8,128)(2,1)S(1)}, u32[]{:S(2)}, u32[]{:S(2)}) collective-permute-start(bf16[2,64,1024]{2,1,0:T(8,128)(2,1)S(1)} %get-tuple-element.133), channel_id=1, source_target_pairs={{2,0},{4,2},{6,4},{7,6},{5,7},{3,5},{1,3},{0,1},{10,8},{12,10},{14... | collective-permute-start | bytes 786440 | tf_op jit(solution)/shard_map/ppermute | solution.py:348
  118.5 10.1 %collective-permute-start.33 = (bf16[2,64,1024]{2,1,0:T(8,128)(2,1)S(1)}, bf16[2,64,1024]{2,1,0:T(8,128)(2,1)S(1)}, u32[]{:S(2)}, u32[]{:S(2)}) collective-permute-start(bf16[2,64,1024]{2,1,0:T(8,128)(2,1)S(1)} %get-tuple-element.129.refs_0_), channel_id=1, source_target_pairs={{0,2},{2,4},{4,6},{6,7},{7,5},{5,3},{3,1},{1,0},{8,10},{10,12},{12... | collective-permute-start | bytes 786440 | tf_op jit(solution)/shard_map/ppermute | solution.py:348
  123.6 6.4 %collective-permute-start.31 = (bf16[2,64,1024]{2,1,0:T(8,128)(2,1)S(1)}, bf16[2,64,1024]{2,1,0:T(8,128)(2,1)S(1)}, u32[]{:S(2)}, u32[]{:S(2)}) collective-permute-start(bf16[2,64,1024]{2,1,0:T(8,128)(2,1)S(1)} %get-tuple-element.130.refs_6_), channel_id=1, source_target_pairs={{0,2},{2,4},{4,6},{6,7},{7,5},{5,3},{3,1},{1,0},{8,10},{10,12},{12... | collective-permute-start | bytes 786440 | tf_op jit(solution)/shard_map/ppermute | solution.py:348
  125.3 6.4 %collective-permute-start.34 = (bf16[2,64,1024]{2,1,0:T(8,128)(2,1)S(1)}, bf16[2,64,1024]{2,1,0:T(8,128)(2,1)S(1)}, u32[]{:S(2)}, u32[]{:S(2)}) collective-permute-start(bf16[2,64,1024]{2,1,0:T(8,128)(2,1)S(1)} %get-tuple-element.134), channel_id=1, source_target_pairs={{2,0},{4,2},{6,4},{7,6},{5,7},{3,5},{1,3},{0,1},{10,8},{12,10},{14... | collective-permute-start | bytes 786440 | tf_op jit(solution)/shard_map/ppermute | solution.py:348
  (7 other events, 15.7 us)

commit v4 on v3

--- a/solution.py
+++ b/solution.py
@@ -11,7 +11,6 @@
 BF16 = jnp.bfloat16
 NT = (((1,), (1,)), ((), ()))
 TN = (((0,), (0,)), ((), ()))
-SMEM = pl.BlockSpec(memory_space=pltpu.SMEM)
 VMEM = pl.BlockSpec(memory_space=pltpu.VMEM)
 PARAMS = pltpu.CompilerParams(vmem_limit_bytes=24 * 2**20)
 
@@ -30,15 +29,18 @@
     return pl.CostEstimate(flops=flops, bytes_accessed=moved, transcendentals=0)
 
 
-def owner_row(where, replicas, part, offset):
-    at = lax.rem(where[0] + (offset + replicas), replicas)
+def owner_row(replicas, part, offset):
+    replica = lax.axis_index("dp")
+    step = replica // 2
+    place = jnp.where(lax.rem(replica, 2) == 0, step, replicas - 1 - step)
+    at = lax.rem(place + (offset + replicas), replicas)
     owner = jnp.where(at < replicas // 2, 2 * at, 2 * (replicas - 1 - at) + 1)
     return pl.multiple_of(owner * part, part)
 
 
-def prepare_kernel(where, x, taps_t):
+def prepare_kernel(x, taps_t):
     seqs, samples, channels = x.shape
-    dilation = jnp.left_shift(jnp.int32(1), where[1])
+    dilation = jnp.left_shift(jnp.int32(1), lax.axis_index("pipe"))
     wide = 128
     for s in range(seqs):
         columns = slice(s * samples, (s + 1) * samples)
@@ -51,16 +53,16 @@
                 taps_t[k * channels + at : k * channels + at + wide, columns] = delayed.astype(BF16)
 
 
-def prepare_call(where, x):
+def prepare_call(x):
     seqs, samples, channels = x.shape
     return pl.pallas_call(
         prepare_kernel,
         out_shape=pltpu.VMEM((3 * channels, seqs * samples), BF16),
-        in_specs=[SMEM, VMEM],
+        in_specs=[VMEM],
         out_specs=VMEM,
         compiler_params=PARAMS,
         cost_estimate=cost(2**20, 2**22),
-    )(where, x)
+    )(x)
 
 
 def tap_rows(taps_t, row, part, columns, first=0, last=3):
@@ -70,18 +72,19 @@
     )
 
 
-def partial_kernel(replicas, offsets, where, taps_t, *refs):
+def partial_kernel(replicas, offsets, taps_t, *refs):
     count = len(offsets)
     convs, mixes, refs = refs[:count], refs[count : 2 * count], refs[2 * count :]
-    acc, w = refs[-2:]
+    first = len(refs) == 2
+    acc, w = refs[:2] if first else refs[2:4]
     rows = taps_t.shape[1]
     channels = w.shape[0] // 4
     part = convs[0].shape[1]
     chunk = min(256, rows)
-    places = [owner_row(where, replicas, part, offset) for offset in offsets]
+    places = [owner_row(replicas, part, offset) for offset in offsets]
     for at in range(0, rows, chunk):
         columns = slice(at, at + chunk)
-        total = refs[0][columns, :] if len(refs) == 4 else None
+        total = None if first else refs[0][columns, :]
         for row, conv in zip(places, convs):
             term = lax.dot_general(
                 tap_rows(taps_t, row, part, columns),
@@ -97,27 +100,30 @@
         w[pl.ds(3 * channels + row, part), :] = mix[0]
 
 
-def partial_call(replicas, offsets, where, taps_t, convs, mixes, held):
+def partial_call(replicas, offsets, taps_t, convs, mixes, held):
     part, wide = convs[0].shape[1:]
     rows = taps_t.shape[1]
     count = len(offsets)
     inputs = in_vmem(taps_t, *convs, *mixes, *held)
     return pl.pallas_call(
         functools.partial(partial_kernel, replicas, offsets),
-        out_shape=[pltpu.VMEM((rows, wide), F32), pltpu.VMEM((2 * wide, wide), BF16)],
-        in_specs=[SMEM] + [VMEM] * len(inputs),
-        out_specs=[VMEM] * 2,
-        input_output_aliases={len(inputs) - 1 + i: i for i in range(len(held))},
+        out_shape=[pltpu.VMEM((rows, wide), F32), pltpu.VMEM((2 * wide, wide), BF16)]
+        + [pltpu.VMEM(mix.shape, BF16) for mix in mixes if held],
+        in_specs=[VMEM] * len(inputs),
+        out_specs=[VMEM] * (2 + count if held else 2),
+        input_output_aliases={1 + 2 * count: 0, 2 + 2 * count: 1, **{1 + count + i: 2 + i for i in range(count)}}
+        if held
+        else {},
         compiler_params=PARAMS,
         cost_estimate=cost(6 * rows * part * count * wide, 2**20),
-    )(where, *inputs)
-
-
-def forward_kernel(replicas, index, store, where, taps_t, conv_a, conv_b, mix, acc, w_in, *refs):
+    )(*inputs)
+
+
+def forward_kernel(replicas, index, store, taps_t, conv_a, conv_b, mix, acc, w_in, *refs):
     a1, a2, hid_t = refs[:3]
     samples, channels = a1.shape
     part = mix.shape[1]
-    row = owner_row(where, replicas, part, replicas // 2)
+    row = owner_row(replicas, part, replicas // 2)
     ahead = conv_a.shape[0]
     chunk = min(256, samples)
     for at in range(0, samples, chunk):
@@ -142,7 +148,7 @@
             w[pl.ds(k * channels + row, part), :] = block
 
 
-def forward_call(replicas, index, micro, store, where, taps_t, conv_a, conv_b, mix, acc, w):
+def forward_call(replicas, index, micro, store, taps_t, conv_a, conv_b, mix, acc, w):
     rows, wide = acc.shape
     channels = wide // 2
     samples = rows // micro
@@ -152,29 +158,29 @@
         out_shape=[pltpu.VMEM((samples, channels), BF16)] * 2
         + [pltpu.VMEM((channels, samples), BF16)]
         + ([pltpu.VMEM(w.shape, BF16)] if store else []),
-        in_specs=[SMEM] + [VMEM] * 6,
+        in_specs=[VMEM] * 6,
         out_specs=[VMEM] * (4 if store else 3),
-        input_output_aliases={6: 3} if store else {},
+        input_output_aliases={5: 3} if store else {},
         compiler_params=PARAMS,
         cost_estimate=cost(2**28, 2**22),
-    )(where, *inputs)
-
-
-def chain_kernel(stage, index, where, g, skip, a1, a2, w, *refs):
-    pg, ig, gk, bt = refs[-4:]
-    samples, channels = g.shape
+    )(*inputs)
+
+
+def chain_kernel(stage, index, g_low, g_high, skip, a1, a2, w, *refs):
+    pg, ig_low, ig_high, gk, bt = refs[-5:]
+    samples, channels = gk.shape
+    chunk = samples // 2
     padding = bt.shape[1] - samples
     dilation = 2**stage
 
-    @pl.when(where[1] == stage)
+    @pl.when(lax.axis_index("pipe") == stage)
     def _():
         for k in (1, 2):
             bt[k, samples:, :] = jnp.zeros((padding, channels), F32)
-        chunk = samples // 2
-        for at in range(samples - chunk, -1, -chunk):
+        for at, g, ig in ((chunk, g_high, ig_high), (0, g_low, ig_low)):
             rows = slice(at, at + chunk)
             hid = lax.dot_general(
-                g[rows, :], w[3 * channels :, :channels], NT, preferred_element_type=F32
+                g[...], w[3 * channels :, :channels], NT, preferred_element_type=F32
             ) + lax.dot_general(
                 skip[index, rows, :], w[3 * channels :, channels:], NT, preferred_element_type=F32
             )
@@ -187,30 +193,31 @@
             piece = 64
             for first in range(at + chunk - piece, at - 1, -piece):
                 last = first + piece
-                total = g[first:last, :].astype(F32) + bt[0, first:last, :]
+                here = slice(first - at, last - at)
+                total = g[here, :].astype(F32) + bt[0, first:last, :]
                 total = total + bt[1, first + dilation : last + dilation, :]
                 total = total + bt[2, first + 2 * dilation : last + 2 * dilation, :]
-                ig[first:last, :] = total.astype(BF16)
-        gk[...] = g[...]
-
-
-def chain_call(stage, index, padding, where, g, skip, a1, a2, w, held):
-    samples, channels = g.shape
-    tile = (samples, channels)
-    inputs = in_vmem(g, skip, a1, a2, w, *held)
+                ig[here, :] = total.astype(BF16)
+            gk[rows, :] = g[...]
+
+
+def chain_call(stage, index, padding, g, skip, a1, a2, w, held):
+    samples, channels = a1.shape
+    half = pltpu.VMEM((samples // 2, channels), BF16)
+    inputs = in_vmem(*g, skip, a1, a2, w, *held)
     return pl.pallas_call(
         functools.partial(chain_kernel, stage, index),
-        out_shape=[pltpu.VMEM((samples, 2 * channels), BF16), pltpu.VMEM(tile, BF16), pltpu.VMEM(tile, BF16)],
-        in_specs=[SMEM] + [VMEM] * len(inputs),
-        out_specs=[VMEM] * 3,
+        out_shape=[pltpu.VMEM((samples, 2 * channels), BF16), half, half, pltpu.VMEM((samples, channels), BF16)],
+        in_specs=[VMEM] * len(inputs),
+        out_specs=[VMEM] * 4,
         scratch_shapes=[pltpu.VMEM((3, samples + padding, channels), F32)],
         input_output_aliases={6 + i: i for i in range(len(held))},
         compiler_params=PARAMS,
         cost_estimate=cost(8 * samples * channels * channels, 2**22),
-    )(where, *inputs)
-
-
-def term_kernel(replicas, offsets, micro, where, taps_t, skip, *refs):
+    )(*inputs)
+
+
+def term_kernel(replicas, offsets, micro, taps_t, skip, *refs):
     hids, refs = refs[:micro], refs[micro:]
     pgs, refs = refs[:micro], refs[micro:]
     gs, refs = refs[:micro], refs[micro:]
@@ -218,7 +225,7 @@
     samples, wide = pgs[0].shape
     channels = wide // 2
     part = channels // replicas
-    places = [owner_row(where, replicas, part, offset) for offset in offsets]
+    places = [owner_row(replicas, part, offset) for offset in offsets]
     conv, mix_g, mix_s = None, None, None
     for m in range(micro):
         columns = slice(m * samples, (m + 1) * samples)
@@ -240,7 +247,7 @@
         high[1, :, channels:] = mix_s[here, :].astype(low.dtype)
 
 
-def term_call(replicas, offsets, kind, where, taps_t, skip, hid_t, pre_grads, gs, tokens):
+def term_call(replicas, offsets, kind, taps_t, skip, hid_t, pre_grads, gs, tokens):
     micro, samples, channels = skip.shape
     part = channels // replicas
     inputs = in_vmem(taps_t, skip, *hid_t, *pre_grads, *gs, *tokens)
@@ -248,11 +255,11 @@
     return pl.pallas_call(
         functools.partial(term_kernel, replicas, offsets, micro),
         out_shape=[pltpu.VMEM((2, part, 2 * channels), kind)] * outs,
-        in_specs=[SMEM] + [VMEM] * len(inputs),
+        in_specs=[VMEM] * len(inputs),
         out_specs=[VMEM] * outs,
         compiler_params=PARAMS,
         cost_estimate=cost(2**29 * len(offsets), 2**20),
-    )(where, *inputs)
+    )(*inputs)
 
 
 def add_kernel(mine_r, mine_l, got_r, got_l, *refs):
@@ -295,25 +302,22 @@
 def local(x_ckpt, top_cot, skip_cot, w_conv, w_mix):
     sections = lax.axis_size("pipe")
     replicas = lax.axis_size("dp")
-    replica = lax.axis_index("dp")
     micro, seqs, samples, channels = x_ckpt.shape[1:]
     block = seqs * samples
     half = replicas // 2
     right, left = ring_pairs(replicas)
-    place = jnp.where(replica % 2 == 0, replica // 2, replicas - 1 - replica // 2)
-    where = jnp.stack([place, lax.axis_index("pipe")]).astype(jnp.int32)
-
-    taps_t = prepare_call(where, x_ckpt[0].reshape(micro * seqs, samples, channels))
+
+    taps_t = prepare_call(x_ckpt[0].reshape(micro * seqs, samples, channels))
     conv = w_conv[0].transpose(1, 0, 2)
     conv_r, conv_l, mix_r, mix_l = conv, conv, w_mix, w_mix
-    held = partial_call(replicas, (0,), where, taps_t, [conv], [w_mix], [])
+    held = partial_call(replicas, (0,), taps_t, [conv], [w_mix], [])
     for step in range(1, half):
         conv_r = lax.ppermute(conv_r, "dp", right)
         conv_l = lax.ppermute(conv_l, "dp", left)
         mix_r = lax.ppermute(mix_r, "dp", right)
         mix_l = lax.ppermute(mix_l, "dp", left)
-        held = partial_call(
-            replicas, (-step, step), where, taps_t, [conv_r, conv_l], [mix_r, mix_l], held
+        *held, mix_r, mix_l = partial_call(
+            replicas, (-step, step), taps_t, [conv_r, conv_l], [mix_r, mix_l], held
         )
     acc, w_full = held
     conv_r = lax.ppermute(conv_r[:2], "dp", right)
@@ -321,12 +325,13 @@
     mix_l = lax.ppermute(mix_l, "dp", left)
 
     skip = skip_cot.reshape(micro, block, channels)
-    g = list(top_cot.reshape(micro, block, channels))
+    top = top_cot.reshape(micro, 2, block // 2, channels)
+    g = [(top[m, 0], top[m, 1]) for m in range(micro)]
     padding = max(16, 2 * 2 ** (sections - 1))
     hid_t, held, ready = [], [()] * micro, []
     for m in range(micro):
         a1, a2, hid, *stored = forward_call(
-            replicas, m, micro, m == 0, where, taps_t, conv_r, conv_l, mix_l, acc, w_full
+            replicas, m, micro, m == 0, taps_t, conv_r, conv_l, mix_l, acc, w_full
         )
         if stored:
             w_full = stored[0]
@@ -334,15 +339,16 @@
         ready.append((a1, a2))
     for stage in range(sections - 1, -1, -1):
         for m in range(micro):
-            held[m] = chain_call(stage, m, padding, where, g[m], skip, *ready[m], w_full, held[m])
+            held[m] = chain_call(stage, m, padding, g[m], skip, *ready[m], w_full, held[m])
             if stage:
-                g[m] = lax.ppermute(held[m][1], "pipe", [(stage, stage - 1)])
-    pre_grads, cots, gs = zip(*held)
-    cot = jnp.stack(cots, axis=0)
+                hop = [(stage, stage - 1)]
+                g[m] = [lax.ppermute(piece, "pipe", hop) for piece in held[m][1:3]]
+    pre_grads, lows, highs, gs = zip(*held)
+    cot = jnp.concatenate([piece for pieces in zip(lows, highs) for piece in pieces], axis=0)
 
     def terms(dist, tokens, kind=BF16):
         offsets = (dist,) if dist in (0, half) else (dist, -dist)
-        return term_call(replicas, offsets, kind, where, taps_t, skip, hid_t, pre_grads, gs, tokens)
+        return term_call(replicas, offsets, kind, taps_t, skip, hid_t, pre_grads, gs, tokens)
 
     def send(to_right, to_left):
         return lax.ppermute(to_right, "dp", right), lax.ppermute(to_left, "dp", left)

time: 133 us -> 134 us (level)
  Pallas kernels: 34.4 us -> 22.4 us
  waiting for transfers between devices: 55.7 us -> 66.6 us
  starting transfers between devices: 38 us -> 41.3 us
    ppermute x4, waiting for transfers between devices: 0.96 us -> 8.1 us  [local(): mix_l = lax.ppermute(mix_l, 'dp', left)]
    ppermute x6 -> x12, starting transfers between devices: 5.36 us -> 10.8 us  [local(): g[m] = [lax.ppermute(piece, 'pipe', hop) for piece in held[m][1:3]]]
    pallas_call x8, Pallas kernels: 10.5 us -> 5.84 us  [chain_call(): pl.pallas_call(functools.partial(chain_kernel, stage, index), out_shape=[...]
    pallas_call x4, Pallas kernels: 8.62 us -> 5.75 us  [partial_call(): pl.pallas_call(functools.partial(partial_kernel, replicas, offsets), out_...]
    pallas_call x5, Pallas kernels: 8.34 us -> 5.58 us  [term_call(): pl.pallas_call(functools.partial(term_kernel, replicas, offsets, micro),...]
    ppermute x7, waiting for transfers between devices: 8.66 us -> 10.8 us  [send(): lax.ppermute(to_right, 'dp', right)]
    ppermute x4, starting transfers between devices: 3.6 us -> 1.63 us  [local(): mix_l = lax.ppermute(mix_l, 'dp', left)]
    ppermute x3, waiting for transfers between devices: 15.8 us -> 13.9 us  [local(): conv_r = lax.ppermute(conv_r, 'dp', right)]
  transfers between devices with their start and end apart: 35 -> 41, of which waited for: 19 -> 27; matrix products, arithmetic and copies ran while one was open for 2% -> 1% of each run, Pallas kernels for 20% -> 12%
where the time goes in v4:
time: 134 us
  waiting for transfers between devices  66.6 us (50%)
  starting transfers between devices  41.3 us (31%)
  Pallas kernels  22.4 us (17%)
  local copies, waits for them, and re-layouts  1.42 us (1%)
    ppermute x12, waiting for transfers between devices, local(): g[m] = [lax.ppermute(piece, 'pipe', hop) for piece in held[m][1:3]]  16.1 us
    ppermute x3, waiting for transfers between devices, local(): conv_r = lax.ppermute(conv_r, 'dp', right)  13.9 us
    ppermute x7, starting transfers between devices, send(): lax.ppermute(to_right, 'dp', right)  11.2 us
    ppermute x12, starting transfers between devices, local(): g[m] = [lax.ppermute(piece, 'pipe', hop) for piece in held[m][1:3]]  10.8 us
    ppermute x7, waiting for transfers between devices, send(): lax.ppermute(to_right, 'dp', right)  10.8 us
    ppermute x7, waiting for transfers between devices, send(): lax.ppermute(to_left, 'dp', left)  9.74 us
    ppermute x4, waiting for transfers between devices, local(): mix_l = lax.ppermute(mix_l, 'dp', left)  8.1 us
    ppermute x3, starting transfers between devices, local(): conv_r = lax.ppermute(conv_r, 'dp', right)  6.67 us
  transfers between devices with their start and end apart: 41, of which 27 were waited for; matrix products, arithmetic and copies ran while one was open for 1% of the time, Pallas kernels for 12%

profile of v4, /device:TPU:0, one launch (start us, length us, event | category | flops | bytes accessed | tf_op | source)
XLA Modules:
  0.0 133.7 jit_solution(7458522203534168152)
XLA Ops:
  0.6 3.1 %collective-permute-start = (bf16[3,64,1024]{2,1,0:T(8,128)(2,1)}, bf16[3,64,1024]{2,1,0:T(8,128)(2,1)S(1)}, u32[]{:S(2)}, u32[]{:S(2)}) collective-permute-start(bf16[3,64,1024]{2,1,0:T(8,128)(2,1)} %bitcast.35), channel_id=1, source_target_pairs={{0,2},{2,4},{4,6},{6,7},{7,5},{5,3},{3,1},{1,0},{8,10},{10,12},{12... | collective-permute-start | bytes 1179656 | tf_op jit(solution)/shard_map/ppermute | solution.py:315
  3.7 9.3 %collective-permute-done.refs_0_ = bf16[3,64,1024]{2,1,0:T(8,128)(2,1)S(1)} collective-permute-done((bf16[3,64,1024]{2,1,0:T(8,128)(2,1)}, bf16[3,64,1024]{2,1,0:T(8,128)(2,1)S(1)}, u32[]{:S(2)}, u32[]{:S(2)}) %collective-permute-start) | collective-permute-done | bytes 393248 | tf_op jit(solution)/shard_map/ppermute | solution.py:315
  13.0 1.8 %collective-permute-start.1 = (bf16[3,64,1024]{2,1,0:T(8,128)(2,1)S(1)}, bf16[3,64,1024]{2,1,0:T(8,128)(2,1)S(1)}, u32[]{:S(2)}, u32[]{:S(2)}) collective-permute-start(bf16[3,64,1024]{2,1,0:T(8,128)(2,1)S(1)} %collective-permute-done.refs_0_), channel_id=1, source_target_pairs={{0,2},{2,4},{4,6},{6,7},{7,5},{5,3},{3,1},{1,0},{8,10},{10,12},{12... | collective-permute-start | bytes 1179656 | tf_op jit(solution)/shard_map/ppermute | solution.py:315
  15.0 1.8 %collective-permute-start.8 = (bf16[1,64,1024]{2,1,0:T(8,128)(2,1)}, bf16[1,64,1024]{2,1,0:T(8,128)(2,1)S(1)}, u32[]{:S(2)}, u32[]{:S(2)}) collective-permute-start(bf16[1,64,1024]{2,1,0:T(8,128)(2,1)} %refs_1_.1), channel_id=1, source_target_pairs={{0,2},{2,4},{4,6},{6,7},{7,5},{5,3},{3,1},{1,0},{8,10},{10,12},{12... | collective-permute-start | bytes 393224 | tf_op jit(solution)/shard_map/ppermute | solution.py:317
  20.4 4.6 %collective-permute-done.1.refs_0_ = bf16[3,64,1024]{2,1,0:T(8,128)(2,1)S(1)} collective-permute-done((bf16[3,64,1024]{2,1,0:T(8,128)(2,1)S(1)}, bf16[3,64,1024]{2,1,0:T(8,128)(2,1)S(1)}, u32[]{:S(2)}, u32[]{:S(2)}) %collective-permute-start.1) | collective-permute-done | bytes 393248 | tf_op jit(solution)/shard_map/ppermute | solution.py:315
  25.0 1.8 %collective-permute-start.2 = (bf16[3,64,1024]{2,1,0:T(8,128)(2,1)S(1)}, bf16[3,64,1024]{2,1,0:T(8,128)(2,1)S(1)}, u32[]{:S(2)}, u32[]{:S(2)}) collective-permute-start(bf16[3,64,1024]{2,1,0:T(8,128)(2,1)S(1)} %collective-permute-done.1.refs_0_), channel_id=1, source_target_pairs={{0,2},{2,4},{4,6},{6,7},{7,5},{5,3},{3,1},{1,0},{8,10},{10,12},{12... | collective-permute-start | bytes 1179656 | tf_op jit(solution)/shard_map/ppermute | solution.py:315
  29.4 1.7 %shard_map.78 = (f32[1024,1024]{1,0:T(8,128)S(1)}, bf16[2048,1024]{1,0:T(8,128)(2,1)S(1)}, bf16[1,64,1024]{2,1,0:T(8,128)(2,1)S(1)}, bf16[1,64,1024]{2,1,0:T(8,128)(2,1)S(1)}) custom-call(bf16[1536,1024]{1,0:T(8,128)(2,1)S(1)} %shard_map.76.taps_t, ...), custom_call_target="tpu_custom_call", output_to_operand_aliasing={{0}: (5, {}), {1}: (6, {}), {2}: (3, {}), {3}: (4, {})} | custom-call | flops 805306368 | bytes 1048576 | tf_op jit(solution)/shard_map/pallas_call | solution.py:108
  31.1 1.6 %collective-permute-start.10 = (bf16[1,64,1024]{2,1,0:T(8,128)(2,1)S(1)}, bf16[1,64,1024]{2,1,0:T(8,128)(2,1)S(1)}, u32[]{:S(2)}, u32[]{:S(2)}) collective-permute-start(bf16[1,64,1024]{2,1,0:T(8,128)(2,1)S(1)} %get-tuple-element.85), channel_id=1, source_target_pairs={{0,2},{2,4},{4,6},{6,7},{7,5},{5,3},{3,1},{1,0},{8,10},{10,12},{12... | collective-permute-start | bytes 393224 | tf_op jit(solution)/shard_map/ppermute | solution.py:317
  33.1 4.2 %collective-permute-done.10.refs_2_ = bf16[1,64,1024]{2,1,0:T(8,128)(2,1)S(1)} collective-permute-done((bf16[1,64,1024]{2,1,0:T(8,128)(2,1)S(1)}, bf16[1,64,1024]{2,1,0:T(8,128)(2,1)S(1)}, u32[]{:S(2)}, u32[]{:S(2)}) %collective-permute-start.10) | collective-permute-done | bytes 131104 | tf_op jit(solution)/shard_map/ppermute | solution.py:317
  38.5 1.7 %shard_map.79 = (f32[1024,1024]{1,0:T(8,128)S(1)}, bf16[2048,1024]{1,0:T(8,128)(2,1)S(1)}, bf16[1,64,1024]{2,1,0:T(8,128)(2,1)S(1)}, bf16[1,64,1024]{2,1,0:T(8,128)(2,1)S(1)}) custom-call(bf16[1536,1024]{1,0:T(8,128)(2,1)S(1)} %shard_map.76.taps_t, ...), custom_call_target="tpu_custom_call", output_to_operand_aliasing={{0}: (5, {}), {1}: (6, {}), {2}: (3, {}), {3}: (4, {})} | custom-call | flops 805306368 | bytes 1048576 | tf_op jit(solution)/shard_map/pallas_call | solution.py:108
  40.2 1.6 %collective-permute-start.12 = (bf16[1,64,1024]{2,1,0:T(8,128)(2,1)S(1)}, bf16[1,64,1024]{2,1,0:T(8,128)(2,1)S(1)}, u32[]{:S(2)}, u32[]{:S(2)}) collective-permute-start(bf16[1,64,1024]{2,1,0:T(8,128)(2,1)S(1)} %get-tuple-element.89), channel_id=1, source_target_pairs={{0,2},{2,4},{4,6},{6,7},{7,5},{5,3},{3,1},{1,0},{8,10},{10,12},{12... | collective-permute-start | bytes 393224 | tf_op jit(solution)/shard_map/ppermute | solution.py:317
  42.3 1.6 %collective-permute-start.3 = (bf16[2,64,1024]{2,1,0:T(8,128)(2,1)S(1)}, bf16[2,64,1024]{2,1,0:T(8,128)(2,1)S(1)}, u32[]{:S(2)}, u32[]{:S(2)}) collective-permute-start(bf16[2,64,1024]{2,1,0:T(8,128)(2,1)S(1)} %slice.26), channel_id=1, source_target_pairs={{0,2},{2,4},{4,6},{6,7},{7,5},{5,3},{3,1},{1,0},{8,10},{10,12},{12... | collective-permute-start | bytes 786440 | tf_op jit(solution)/shard_map/ppermute | solution.py:323
  43.9 1.6 %collective-permute-done.12.refs_2_ = bf16[1,64,1024]{2,1,0:T(8,128)(2,1)S(1)} collective-permute-done((bf16[1,64,1024]{2,1,0:T(8,128)(2,1)S(1)}, bf16[1,64,1024]{2,1,0:T(8,128)(2,1)S(1)}, u32[]{:S(2)}, u32[]{:S(2)}) %collective-permute-start.12) | collective-permute-done | bytes 131104 | tf_op jit(solution)/shard_map/ppermute | solution.py:317
  46.9 1.7 %shard_map.80 = (f32[1024,1024]{1,0:T(8,128)S(1)}, bf16[2048,1024]{1,0:T(8,128)(2,1)S(1)}, bf16[1,64,1024]{2,1,0:T(8,128)(2,1)S(1)}, bf16[1,64,1024]{2,1,0:T(8,128)(2,1)S(1)}) custom-call(bf16[1536,1024]{1,0:T(8,128)(2,1)S(1)} %shard_map.76.taps_t, ...), custom_call_target="tpu_custom_call", output_to_operand_aliasing={{0}: (5, {}), {1}: (6, {}), {2}: (3, {}), {3}: (4, {})} | custom-call | flops 805306368 | bytes 1048576 | tf_op jit(solution)/shard_map/pallas_call | solution.py:108
  49.6 4.0 %collective-permute-done.14.mix = bf16[1,64,1024]{2,1,0:T(8,128)(2,1)S(1)} collective-permute-done((bf16[1,64,1024]{2,1,0:T(8,128)(2,1)S(1)}, bf16[1,64,1024]{2,1,0:T(8,128)(2,1)S(1)}, u32[]{:S(2)}, u32[]{:S(2)}) %collective-permute-start.14) | collective-permute-done | bytes 131104 | tf_op jit(solution)/shard_map/ppermute | solution.py:325
  68.6 11.7 %collective-permute-done.19.g_low = bf16[256,512]{1,0:T(8,128)(2,1)S(1)} collective-permute-done((bf16[256,512]{1,0:T(8,128)(2,1)S(1)}, bf16[256,512]{1,0:T(8,128)(2,1)S(1)}, u32[]{:S(2)}, u32[]{:S(2)}) %collective-permute-start.19) | collective-permute-done | bytes 262176 | tf_op jit(solution)/shard_map/ppermute | solution.py:345
  81.7 2.8 %shard_map.85 = (bf16[512,1024]{1,0:T(8,128)(2,1)S(1)}, bf16[256,512]{1,0:T(8,128)(2,1)S(1)}, bf16[256,512]{1,0:T(8,128)(2,1)S(1)}, bf16[512,512]{1,0:T(8,128)(2,1)S(1)}) custom-call(bf16[256,512]{1,0:T(8,128)(2,1)S(1)} %collective-permute-done.19.g_low, ...), custom_call_target="tpu_custom_call", output_to_operand_aliasing={{0}: (6, {}), {1}: (7, {}), {2}: (8, {}), {3}: (9, {})} | custom-call | flops 1073741824 | bytes 4194304 | tf_op jit(solution)/shard_map/pallas_call | solution.py:208
  87.5 2.8 %shard_map.90 = (bf16[512,1024]{1,0:T(8,128)(2,1)S(1)}, bf16[256,512]{1,0:T(8,128)(2,1)S(1)}, bf16[256,512]{1,0:T(8,128)(2,1)S(1)}, bf16[512,512]{1,0:T(8,128)(2,1)S(1)}) custom-call(bf16[256,512]{1,0:T(8,128)(2,1)S(1)} %collective-permute-done.25.g_low, ...), custom_call_target="tpu_custom_call", output_to_operand_aliasing={{0}: (6, {}), {1}: (7, {}), {2}: (8, {}), {3}: (9, {})} | custom-call | flops 1073741824 | bytes 4194304 | tf_op jit(solution)/shard_map/pallas_call | solution.py:208
  91.2 1.6 %collective-permute-start.27 = (bf16[2,64,1024]{2,1,0:T(8,128)(2,1)S(1)}, bf16[2,64,1024]{2,1,0:T(8,128)(2,1)S(1)}, u32[]{:S(2)}, u32[]{:S(2)}) collective-permute-start(bf16[2,64,1024]{2,1,0:T(8,128)(2,1)S(1)} %get-tuple-element.135.refs_6_), channel_id=1, source_target_pairs={{0,2},{2,4},{4,6},{6,7},{7,5},{5,3},{3,1},{1,0},{8,10},{10,12},{12... | collective-permute-start | bytes 786440 | tf_op jit(solution)/shard_map/ppermute | solution.py:354
  94.6 1.6 %collective-permute-start.31 = (bf16[2,64,1024]{2,1,0:T(8,128)(2,1)S(1)}, bf16[2,64,1024]{2,1,0:T(8,128)(2,1)S(1)}, u32[]{:S(2)}, u32[]{:S(2)}) collective-permute-start(bf16[2,64,1024]{2,1,0:T(8,128)(2,1)S(1)} %get-tuple-element.145), channel_id=1, source_target_pairs={{0,2},{2,4},{4,6},{6,7},{7,5},{5,3},{3,1},{1,0},{8,10},{10,12},{12... | collective-permute-start | bytes 786440 | tf_op jit(solution)/shard_map/ppermute | solution.py:354
  96.6 3.9 %collective-permute-done.27.got_r = bf16[2,64,1024]{2,1,0:T(8,128)(2,1)S(1)} collective-permute-done((bf16[2,64,1024]{2,1,0:T(8,128)(2,1)S(1)}, bf16[2,64,1024]{2,1,0:T(8,128)(2,1)S(1)}, u32[]{:S(2)}, u32[]{:S(2)}) %collective-permute-start.27) | collective-permute-done | bytes 262176 | tf_op jit(solution)/shard_map/ppermute | solution.py:354
  100.5 1.6 %collective-permute-done.28.got_l = bf16[2,64,1024]{2,1,0:T(8,128)(2,1)S(1)} collective-permute-done((bf16[2,64,1024]{2,1,0:T(8,128)(2,1)S(1)}, bf16[2,64,1024]{2,1,0:T(8,128)(2,1)S(1)}, u32[]{:S(2)}, u32[]{:S(2)}) %collective-permute-start.28) | collective-permute-done | bytes 262176 | tf_op jit(solution)/shard_map/ppermute | solution.py:354
  102.2 1.6 %collective-permute-start.29 = (bf16[2,64,1024]{2,1,0:T(8,128)(2,1)S(1)}, bf16[2,64,1024]{2,1,0:T(8,128)(2,1)S(1)}, u32[]{:S(2)}, u32[]{:S(2)}) collective-permute-start(bf16[2,64,1024]{2,1,0:T(8,128)(2,1)S(1)} %get-tuple-element.139.refs_6_.refs_0_), channel_id=1, source_target_pairs={{0,2},{2,4},{4,6},{6,7},{7,5},{5,3},{3,1},{1,0},{8,10},{10,12},{12... | collective-permute-start | bytes 786440 | tf_op jit(solution)/shard_map/ppermute | solution.py:354
  106.2 1.6 %collective-permute-done.32.got_l = bf16[2,64,1024]{2,1,0:T(8,128)(2,1)S(1)} collective-permute-done((bf16[2,64,1024]{2,1,0:T(8,128)(2,1)S(1)}, bf16[2,64,1024]{2,1,0:T(8,128)(2,1)S(1)}, u32[]{:S(2)}, u32[]{:S(2)}) %collective-permute-start.32) | collective-permute-done | bytes 262176 | tf_op jit(solution)/shard_map/ppermute | solution.py:354
  107.9 1.6 %collective-permute-start.35 = (bf16[2,64,1024]{2,1,0:T(8,128)(2,1)S(1)}, bf16[2,64,1024]{2,1,0:T(8,128)(2,1)S(1)}, u32[]{:S(2)}, u32[]{:S(2)}) collective-permute-start(bf16[2,64,1024]{2,1,0:T(8,128)(2,1)S(1)} %get-tuple-element.147.refs_0_), channel_id=1, source_target_pairs={{0,2},{2,4},{4,6},{6,7},{7,5},{5,3},{3,1},{1,0},{8,10},{10,12},{12... | collective-permute-start | bytes 786440 | tf_op jit(solution)/shard_map/ppermute | solution.py:354
  109.9 1.8 %collective-permute-done.29.got_r = bf16[2,64,1024]{2,1,0:T(8,128)(2,1)S(1)} collective-permute-done((bf16[2,64,1024]{2,1,0:T(8,128)(2,1)S(1)}, bf16[2,64,1024]{2,1,0:T(8,128)(2,1)S(1)}, u32[]{:S(2)}, u32[]{:S(2)}) %collective-permute-start.29) | collective-permute-done | bytes 262176 | tf_op jit(solution)/shard_map/ppermute | solution.py:354
  111.8 1.6 %collective-permute-done.30.got_l = bf16[2,64,1024]{2,1,0:T(8,128)(2,1)S(1)} collective-permute-done((bf16[2,64,1024]{2,1,0:T(8,128)(2,1)S(1)}, bf16[2,64,1024]{2,1,0:T(8,128)(2,1)S(1)}, u32[]{:S(2)}, u32[]{:S(2)}) %collective-permute-start.30) | collective-permute-done | bytes 262176 | tf_op jit(solution)/shard_map/ppermute | solution.py:354
  117.4 1.6 %collective-permute-done.36.got_l = bf16[2,64,1024]{2,1,0:T(8,128)(2,1)S(1)} collective-permute-done((bf16[2,64,1024]{2,1,0:T(8,128)(2,1)S(1)}, bf16[2,64,1024]{2,1,0:T(8,128)(2,1)S(1)}, u32[]{:S(2)}, u32[]{:S(2)}) %collective-permute-start.36) | collective-permute-done | bytes 262176 | tf_op jit(solution)/shard_map/ppermute | solution.py:354
  119.6 1.6 %collective-permute-start.39 = (bf16[2,64,1024]{2,1,0:T(8,128)(2,1)S(1)}, bf16[2,64,1024]{2,1,0:T(8,128)(2,1)S(1)}, u32[]{:S(2)}, u32[]{:S(2)}) collective-permute-start(bf16[2,64,1024]{2,1,0:T(8,128)(2,1)S(1)} %get-tuple-element.155.refs_0_), channel_id=1, source_target_pairs={{0,2},{2,4},{4,6},{6,7},{7,5},{5,3},{3,1},{1,0},{8,10},{10,12},{12... | collective-permute-start | bytes 786440 | tf_op jit(solution)/shard_map/ppermute | solution.py:354
  121.2 1.8 %collective-permute-done.33.got_r = bf16[2,64,1024]{2,1,0:T(8,128)(2,1)S(1)} collective-permute-done((bf16[2,64,1024]{2,1,0:T(8,128)(2,1)S(1)}, bf16[2,64,1024]{2,1,0:T(8,128)(2,1)S(1)}, u32[]{:S(2)}, u32[]{:S(2)}) %collective-permute-start.33) | collective-permute-done | bytes 262176 | tf_op jit(solution)/shard_map/ppermute | solution.py:354
  123.0 1.6 %collective-permute-done.34.got_l = bf16[2,64,1024]{2,1,0:T(8,128)(2,1)S(1)} collective-permute-done((bf16[2,64,1024]{2,1,0:T(8,128)(2,1)S(1)}, bf16[2,64,1024]{2,1,0:T(8,128)(2,1)S(1)}, u32[]{:S(2)}, u32[]{:S(2)}) %collective-permute-start.34) | collective-permute-done | bytes 262176 | tf_op jit(solution)/shard_map/ppermute | solution.py:354
  129.0 2.1 %collective-permute-done.37.low_r = bf16[2,64,1024]{2,1,0:T(8,128)(2,1)S(1)} collective-permute-done((bf16[2,64,1024]{2,1,0:T(8,128)(2,1)S(1)}, bf16[2,64,1024]{2,1,0:T(8,128)(2,1)S(1)}, u32[]{:S(2)}, u32[]{:S(2)}) %collective-permute-start.37) | collective-permute-done | bytes 262176 | tf_op jit(solution)/shard_map/ppermute | solution.py:354
  (90 shorter events, 47.9 us)
Async XLA Ops:
  0.6 12.3 %collective-permute-start = (bf16[3,64,1024]{2,1,0:T(8,128)(2,1)}, bf16[3,64,1024]{2,1,0:T(8,128)(2,1)S(1)}, u32[]{:S(2)}, u32[]{:S(2)}) collective-permute-start(bf16[3,64,1024]{2,1,0:T(8,128)(2,1)} %bitcast.35), channel_id=1, source_target_pairs={{0,2},{2,4},{4,6},{6,7},{7,5},{5,3},{3,1},{1,0},{8,10},{10,12},{12... | collective-permute-start | bytes 1179656 | tf_op jit(solution)/shard_map/ppermute | solution.py:315
  3.7 11.1 %collective-permute-start.4 = (bf16[3,64,1024]{2,1,0:T(8,128)(2,1)}, bf16[3,64,1024]{2,1,0:T(8,128)(2,1)S(1)}, u32[]{:S(2)}, u32[]{:S(2)}) collective-permute-start(bf16[3,64,1024]{2,1,0:T(8,128)(2,1)} %bitcast.36), channel_id=1, source_target_pairs={{2,0},{4,2},{6,4},{7,6},{5,7},{3,5},{1,3},{0,1},{10,8},{12,10},{14... | collective-permute-start | bytes 1179656 | tf_op jit(solution)/shard_map/ppermute | solution.py:316
  13.0 12.1 %collective-permute-start.1 = (bf16[3,64,1024]{2,1,0:T(8,128)(2,1)S(1)}, bf16[3,64,1024]{2,1,0:T(8,128)(2,1)S(1)}, u32[]{:S(2)}, u32[]{:S(2)}) collective-permute-start(bf16[3,64,1024]{2,1,0:T(8,128)(2,1)S(1)} %collective-permute-done.refs_0_), channel_id=1, source_target_pairs={{0,2},{2,4},{4,6},{6,7},{7,5},{5,3},{3,1},{1,0},{8,10},{10,12},{12... | collective-permute-start | bytes 1179656 | tf_op jit(solution)/shard_map/ppermute | solution.py:315
  14.8 12.1 %collective-permute-start.5 = (bf16[3,64,1024]{2,1,0:T(8,128)(2,1)S(1)}, bf16[3,64,1024]{2,1,0:T(8,128)(2,1)S(1)}, u32[]{:S(2)}, u32[]{:S(2)}) collective-permute-start(bf16[3,64,1024]{2,1,0:T(8,128)(2,1)S(1)} %collective-permute-done.4.refs_1_), channel_id=1, source_target_pairs={{2,0},{4,2},{6,4},{7,6},{5,7},{3,5},{1,3},{0,1},{10,8},{12,10},{14... | collective-permute-start | bytes 1179656 | tf_op jit(solution)/shard_map/ppermute | solution.py:316
  15.0 12.8 %collective-permute-start.8 = (bf16[1,64,1024]{2,1,0:T(8,128)(2,1)}, bf16[1,64,1024]{2,1,0:T(8,128)(2,1)S(1)}, u32[]{:S(2)}, u32[]{:S(2)}) collective-permute-start(bf16[1,64,1024]{2,1,0:T(8,128)(2,1)} %refs_1_.1), channel_id=1, source_target_pairs={{0,2},{2,4},{4,6},{6,7},{7,5},{5,3},{3,1},{1,0},{8,10},{10,12},{12... | collective-permute-start | bytes 393224 | tf_op jit(solution)/shard_map/ppermute | solution.py:317
  16.8 12.6 %collective-permute-start.9 = (bf16[1,64,1024]{2,1,0:T(8,128)(2,1)}, bf16[1,64,1024]{2,1,0:T(8,128)(2,1)S(1)}, u32[]{:S(2)}, u32[]{:S(2)}) collective-permute-start(bf16[1,64,1024]{2,1,0:T(8,128)(2,1)} %refs_1_.1), channel_id=1, source_target_pairs={{2,0},{4,2},{6,4},{7,6},{5,7},{3,5},{1,3},{0,1},{10,8},{12,10},{14... | collective-permute-start | bytes 393224 | tf_op jit(solution)/shard_map/ppermute | solution.py:318
  25.0 17.2 %collective-permute-start.2 = (bf16[3,64,1024]{2,1,0:T(8,128)(2,1)S(1)}, bf16[3,64,1024]{2,1,0:T(8,128)(2,1)S(1)}, u32[]{:S(2)}, u32[]{:S(2)}) collective-permute-start(bf16[3,64,1024]{2,1,0:T(8,128)(2,1)S(1)} %collective-permute-done.1.refs_0_), channel_id=1, source_target_pairs={{0,2},{2,4},{4,6},{6,7},{7,5},{5,3},{3,1},{1,0},{8,10},{10,12},{12... | collective-permute-start | bytes 1179656 | tf_op jit(solution)/shard_map/ppermute | solution.py:315
  26.8 20.1 %collective-permute-start.6 = (bf16[3,64,1024]{2,1,0:T(8,128)(2,1)S(1)}, bf16[3,64,1024]{2,1,0:T(8,128)(2,1)S(1)}, u32[]{:S(2)}, u32[]{:S(2)}) collective-permute-start(bf16[3,64,1024]{2,1,0:T(8,128)(2,1)S(1)} %collective-permute-done.5.refs_1_), channel_id=1, source_target_pairs={{2,0},{4,2},{6,4},{7,6},{5,7},{3,5},{1,3},{0,1},{10,8},{12,10},{14... | collective-permute-start | bytes 1179656 | tf_op jit(solution)/shard_map/ppermute | solution.py:316
  31.1 6.3 %collective-permute-start.10 = (bf16[1,64,1024]{2,1,0:T(8,128)(2,1)S(1)}, bf16[1,64,1024]{2,1,0:T(8,128)(2,1)S(1)}, u32[]{:S(2)}, u32[]{:S(2)}) collective-permute-start(bf16[1,64,1024]{2,1,0:T(8,128)(2,1)S(1)} %get-tuple-element.85), channel_id=1, source_target_pairs={{0,2},{2,4},{4,6},{6,7},{7,5},{5,3},{3,1},{1,0},{8,10},{10,12},{12... | collective-permute-start | bytes 393224 | tf_op jit(solution)/shard_map/ppermute | solution.py:317
  32.7 5.8 %collective-permute-start.11 = (bf16[1,64,1024]{2,1,0:T(8,128)(2,1)S(1)}, bf16[1,64,1024]{2,1,0:T(8,128)(2,1)S(1)}, u32[]{:S(2)}, u32[]{:S(2)}) collective-permute-start(bf16[1,64,1024]{2,1,0:T(8,128)(2,1)S(1)} %get-tuple-element.86), channel_id=1, source_target_pairs={{2,0},{4,2},{6,4},{7,6},{5,7},{3,5},{1,3},{0,1},{10,8},{12,10},{14... | collective-permute-start | bytes 393224 | tf_op jit(solution)/shard_map/ppermute | solution.py:318
  40.2 5.3 %collective-permute-start.12 = (bf16[1,64,1024]{2,1,0:T(8,128)(2,1)S(1)}, bf16[1,64,1024]{2,1,0:T(8,128)(2,1)S(1)}, u32[]{:S(2)}, u32[]{:S(2)}) collective-permute-start(bf16[1,64,1024]{2,1,0:T(8,128)(2,1)S(1)} %get-tuple-element.89), channel_id=1, source_target_pairs={{0,2},{2,4},{4,6},{6,7},{7,5},{5,3},{3,1},{1,0},{8,10},{10,12},{12... | collective-permute-start | bytes 393224 | tf_op jit(solution)/shard_map/ppermute | solution.py:317
  41.8 5.1 %collective-permute-start.13 = (bf16[1,64,1024]{2,1,0:T(8,128)(2,1)S(1)}, bf16[1,64,1024]{2,1,0:T(8,128)(2,1)S(1)}, u32[]{:S(2)}, u32[]{:S(2)}) collective-permute-start(bf16[1,64,1024]{2,1,0:T(8,128)(2,1)S(1)} %get-tuple-element.90), channel_id=1, source_target_pairs={{2,0},{4,2},{6,4},{7,6},{5,7},{3,5},{1,3},{0,1},{10,8},{12,10},{14... | collective-permute-start | bytes 393224 | tf_op jit(solution)/shard_map/ppermute | solution.py:318
  42.3 12.7 %collective-permute-start.3 = (bf16[2,64,1024]{2,1,0:T(8,128)(2,1)S(1)}, bf16[2,64,1024]{2,1,0:T(8,128)(2,1)S(1)}, u32[]{:S(2)}, u32[]{:S(2)}) collective-permute-start(bf16[2,64,1024]{2,1,0:T(8,128)(2,1)S(1)} %slice.26), channel_id=1, source_target_pairs={{0,2},{2,4},{4,6},{6,7},{7,5},{5,3},{3,1},{1,0},{8,10},{10,12},{12... | collective-permute-start | bytes 786440 | tf_op jit(solution)/shard_map/ppermute | solution.py:323
  49.1 5.9 %collective-permute-start.7 = (bf16[1,64,1024]{2,1,0:T(8,128)(2,1)S(1)}, bf16[1,64,1024]{2,1,0:T(8,128)(2,1)S(1)}, u32[]{:S(2)}, u32[]{:S(2)}) collective-permute-start(bf16[1,64,1024]{2,1,0:T(8,128)(2,1)S(1)} %slice.27), channel_id=1, source_target_pairs={{2,0},{4,2},{6,4},{7,6},{5,7},{3,5},{1,3},{0,1},{10,8},{12,10},{14... | collective-permute-start | bytes 393224 | tf_op jit(solution)/shard_map/ppermute | solution.py:324
  63.2 17.2 %collective-permute-start.19 = (bf16[256,512]{1,0:T(8,128)(2,1)S(1)}, bf16[256,512]{1,0:T(8,128)(2,1)S(1)}, u32[]{:S(2)}, u32[]{:S(2)}) collective-permute-start(bf16[256,512]{1,0:T(8,128)(2,1)S(1)} %get-tuple-element.107.refs_1_), channel_id=1, source_target_pairs={{8,0},{9,1},{10,2},{11,3},{12,4},{13,5},{14,6},{15,7}} | collective-permute-start | bytes 786440 | tf_op jit(solution)/shard_map/ppermute | solution.py:345
  64.5 17.2 %collective-permute-start.20 = (bf16[256,512]{1,0:T(8,128)(2,1)S(1)}, bf16[256,512]{1,0:T(8,128)(2,1)S(1)}, u32[]{:S(2)}, u32[]{:S(2)}) collective-permute-start(bf16[256,512]{1,0:T(8,128)(2,1)S(1)} %get-tuple-element.108.refs_2_), channel_id=1, source_target_pairs={{8,0},{9,1},{10,2},{11,3},{12,4},{13,5},{14,6},{15,7}} | collective-permute-start | bytes 786440 | tf_op jit(solution)/shard_map/ppermute | solution.py:345
  65.8 20.2 %collective-permute-start.25 = (bf16[256,512]{1,0:T(8,128)(2,1)S(1)}, bf16[256,512]{1,0:T(8,128)(2,1)S(1)}, u32[]{:S(2)}, u32[]{:S(2)}) collective-permute-start(bf16[256,512]{1,0:T(8,128)(2,1)S(1)} %get-tuple-element.123.refs_1_), channel_id=1, source_target_pairs={{8,0},{9,1},{10,2},{11,3},{12,4},{13,5},{14,6},{15,7}} | collective-permute-start | bytes 786440 | tf_op jit(solution)/shard_map/ppermute | solution.py:345
  67.3 20.2 %collective-permute-start.26 = (bf16[256,512]{1,0:T(8,128)(2,1)S(1)}, bf16[256,512]{1,0:T(8,128)(2,1)S(1)}, u32[]{:S(2)}, u32[]{:S(2)}) collective-permute-start(bf16[256,512]{1,0:T(8,128)(2,1)S(1)} %get-tuple-element.124.refs_2_), channel_id=1, source_target_pairs={{8,0},{9,1},{10,2},{11,3},{12,4},{13,5},{14,6},{15,7}} | collective-permute-start | bytes 786440 | tf_op jit(solution)/shard_map/ppermute | solution.py:345
  91.2 9.3 %collective-permute-start.27 = (bf16[2,64,1024]{2,1,0:T(8,128)(2,1)S(1)}, bf16[2,64,1024]{2,1,0:T(8,128)(2,1)S(1)}, u32[]{:S(2)}, u32[]{:S(2)}) collective-permute-start(bf16[2,64,1024]{2,1,0:T(8,128)(2,1)S(1)} %get-tuple-element.135.refs_6_), channel_id=1, source_target_pairs={{0,2},{2,4},{4,6},{6,7},{7,5},{5,3},{3,1},{1,0},{8,10},{10,12},{12... | collective-permute-start | bytes 786440 | tf_op jit(solution)/shard_map/ppermute | solution.py:354
  92.9 9.2 %collective-permute-start.28 = (bf16[2,64,1024]{2,1,0:T(8,128)(2,1)S(1)}, bf16[2,64,1024]{2,1,0:T(8,128)(2,1)S(1)}, u32[]{:S(2)}, u32[]{:S(2)}) collective-permute-start(bf16[2,64,1024]{2,1,0:T(8,128)(2,1)S(1)} %get-tuple-element.138), channel_id=1, source_target_pairs={{2,0},{4,2},{6,4},{7,6},{5,7},{3,5},{1,3},{0,1},{10,8},{12,10},{14... | collective-permute-start | bytes 786440 | tf_op jit(solution)/shard_map/ppermute | solution.py:354
  94.6 11.6 %collective-permute-start.31 = (bf16[2,64,1024]{2,1,0:T(8,128)(2,1)S(1)}, bf16[2,64,1024]{2,1,0:T(8,128)(2,1)S(1)}, u32[]{:S(2)}, u32[]{:S(2)}) collective-permute-start(bf16[2,64,1024]{2,1,0:T(8,128)(2,1)S(1)} %get-tuple-element.145), channel_id=1, source_target_pairs={{0,2},{2,4},{4,6},{6,7},{7,5},{5,3},{3,1},{1,0},{8,10},{10,12},{12... | collective-permute-start | bytes 786440 | tf_op jit(solution)/shard_map/ppermute | solution.py:354
  96.2 11.5 %collective-permute-start.32 = (bf16[2,64,1024]{2,1,0:T(8,128)(2,1)S(1)}, bf16[2,64,1024]{2,1,0:T(8,128)(2,1)S(1)}, u32[]{:S(2)}, u32[]{:S(2)}) collective-permute-start(bf16[2,64,1024]{2,1,0:T(8,128)(2,1)S(1)} %get-tuple-element.146), channel_id=1, source_target_pairs={{2,0},{4,2},{6,4},{7,6},{5,7},{3,5},{1,3},{0,1},{10,8},{12,10},{14... | collective-permute-start | bytes 786440 | tf_op jit(solution)/shard_map/ppermute | solution.py:354
  102.2 9.5 %collective-permute-start.29 = (bf16[2,64,1024]{2,1,0:T(8,128)(2,1)S(1)}, bf16[2,64,1024]{2,1,0:T(8,128)(2,1)S(1)}, u32[]{:S(2)}, u32[]{:S(2)}) collective-permute-start(bf16[2,64,1024]{2,1,0:T(8,128)(2,1)S(1)} %get-tuple-element.139.refs_6_.refs_0_), channel_id=1, source_target_pairs={{0,2},{2,4},{4,6},{6,7},{7,5},{5,3},{3,1},{1,0},{8,10},{10,12},{12... | collective-permute-start | bytes 786440 | tf_op jit(solution)/shard_map/ppermute | solution.py:354
  103.8 9.5 %collective-permute-start.30 = (bf16[2,64,1024]{2,1,0:T(8,128)(2,1)S(1)}, bf16[2,64,1024]{2,1,0:T(8,128)(2,1)S(1)}, u32[]{:S(2)}, u32[]{:S(2)}) collective-permute-start(bf16[2,64,1024]{2,1,0:T(8,128)(2,1)S(1)} %get-tuple-element.142), channel_id=1, source_target_pairs={{2,0},{4,2},{6,4},{7,6},{5,7},{3,5},{1,3},{0,1},{10,8},{12,10},{14... | collective-permute-start | bytes 786440 | tf_op jit(solution)/shard_map/ppermute | solution.py:354
  107.9 9.5 %collective-permute-start.35 = (bf16[2,64,1024]{2,1,0:T(8,128)(2,1)S(1)}, bf16[2,64,1024]{2,1,0:T(8,128)(2,1)S(1)}, u32[]{:S(2)}, u32[]{:S(2)}) collective-permute-start(bf16[2,64,1024]{2,1,0:T(8,128)(2,1)S(1)} %get-tuple-element.147.refs_0_), channel_id=1, source_target_pairs={{0,2},{2,4},{4,6},{6,7},{7,5},{5,3},{3,1},{1,0},{8,10},{10,12},{12... | collective-permute-start | bytes 786440 | tf_op jit(solution)/shard_map/ppermute | solution.py:354
  109.4 9.5 %collective-permute-start.36 = (bf16[2,64,1024]{2,1,0:T(8,128)(2,1)S(1)}, bf16[2,64,1024]{2,1,0:T(8,128)(2,1)S(1)}, u32[]{:S(2)}, u32[]{:S(2)}) collective-permute-start(bf16[2,64,1024]{2,1,0:T(8,128)(2,1)S(1)} %get-tuple-element.154), channel_id=1, source_target_pairs={{2,0},{4,2},{6,4},{7,6},{5,7},{3,5},{1,3},{0,1},{10,8},{12,10},{14... | collective-permute-start | bytes 786440 | tf_op jit(solution)/shard_map/ppermute | solution.py:354
  113.5 9.5 %collective-permute-start.33 = (bf16[2,64,1024]{2,1,0:T(8,128)(2,1)S(1)}, bf16[2,64,1024]{2,1,0:T(8,128)(2,1)S(1)}, u32[]{:S(2)}, u32[]{:S(2)}) collective-permute-start(bf16[2,64,1024]{2,1,0:T(8,128)(2,1)S(1)} %get-tuple-element.148.refs_6_.refs_0_), channel_id=1, source_target_pairs={{0,2},{2,4},{4,6},{6,7},{7,5},{5,3},{3,1},{1,0},{8,10},{10,12},{12... | collective-permute-start | bytes 786440 | tf_op jit(solution)/shard_map/ppermute | solution.py:354
  115.1 9.5 %collective-permute-start.34 = (bf16[2,64,1024]{2,1,0:T(8,128)(2,1)S(1)}, bf16[2,64,1024]{2,1,0:T(8,128)(2,1)S(1)}, u32[]{:S(2)}, u32[]{:S(2)}) collective-permute-start(bf16[2,64,1024]{2,1,0:T(8,128)(2,1)S(1)} %get-tuple-element.151), channel_id=1, source_target_pairs={{2,0},{4,2},{6,4},{7,6},{5,7},{3,5},{1,3},{0,1},{10,8},{12,10},{14... | collective-permute-start | bytes 786440 | tf_op jit(solution)/shard_map/ppermute | solution.py:354
  119.1 9.9 %collective-permute-start.38 = (bf16[2,64,1024]{2,1,0:T(8,128)(2,1)S(1)}, bf16[2,64,1024]{2,1,0:T(8,128)(2,1)S(1)}, u32[]{:S(2)}, u32[]{:S(2)}) collective-permute-start(bf16[2,64,1024]{2,1,0:T(8,128)(2,1)S(1)} %get-tuple-element.159), channel_id=1, source_target_pairs={{2,0},{4,2},{6,4},{7,6},{5,7},{3,5},{1,3},{0,1},{10,8},{12,10},{14... | collective-permute-start | bytes 786440 | tf_op jit(solution)/shard_map/ppermute | solution.py:354
  119.6 9.5 %collective-permute-start.39 = (bf16[2,64,1024]{2,1,0:T(8,128)(2,1)S(1)}, bf16[2,64,1024]{2,1,0:T(8,128)(2,1)S(1)}, u32[]{:S(2)}, u32[]{:S(2)}) collective-permute-start(bf16[2,64,1024]{2,1,0:T(8,128)(2,1)S(1)} %get-tuple-element.155.refs_0_), channel_id=1, source_target_pairs={{0,2},{2,4},{4,6},{6,7},{7,5},{5,3},{3,1},{1,0},{8,10},{10,12},{12... | collective-permute-start | bytes 786440 | tf_op jit(solution)/shard_map/ppermute | solution.py:354
  124.7 6.4 %collective-permute-start.37 = (bf16[2,64,1024]{2,1,0:T(8,128)(2,1)S(1)}, bf16[2,64,1024]{2,1,0:T(8,128)(2,1)S(1)}, u32[]{:S(2)}, u32[]{:S(2)}) collective-permute-start(bf16[2,64,1024]{2,1,0:T(8,128)(2,1)S(1)} %get-tuple-element.156.refs_6_), channel_id=1, source_target_pairs={{0,2},{2,4},{4,6},{6,7},{7,5},{5,3},{3,1},{1,0},{8,10},{10,12},{12... | collective-permute-start | bytes 786440 | tf_op jit(solution)/shard_map/ppermute | solution.py:354
  126.3 6.4 %collective-permute-start.40 = (bf16[2,64,1024]{2,1,0:T(8,128)(2,1)S(1)}, bf16[2,64,1024]{2,1,0:T(8,128)(2,1)S(1)}, u32[]{:S(2)}, u32[]{:S(2)}) collective-permute-start(bf16[2,64,1024]{2,1,0:T(8,128)(2,1)S(1)} %get-tuple-element.160), channel_id=1, source_target_pairs={{2,0},{4,2},{6,4},{7,6},{5,7},{3,5},{1,3},{0,1},{10,8},{12,10},{14... | collective-permute-start | bytes 786440 | tf_op jit(solution)/shard_map/ppermute | solution.py:354
  (14 other events, 37.4 us)

commit v5 on v4

--- a/solution.py
+++ b/solution.py
@@ -65,109 +65,107 @@
     )(x)
 
 
-def tap_rows(taps_t, row, part, columns, first=0, last=3):
+def tap_rows(taps_t, row, part, columns):
     channels = taps_t.shape[0] // 3
-    return jnp.concatenate(
-        [taps_t[pl.ds(k * channels + row, part), columns] for k in range(first, last)], axis=0
+    return jnp.concatenate([taps_t[pl.ds(k * channels + row, part), columns] for k in range(3)], axis=0)
+
+
+def place_rows(replicas, items, blocks):
+    part = blocks[0].shape[1]
+    return [(owner_row(replicas, part, offset), first, block) for (offset, first), block in zip(items, blocks)]
+
+
+def shard_term(taps_t, columns, placed):
+    channels = taps_t.shape[0] // 3
+    part, wide = placed[0][2].shape[1:]
+    rows, weights = [], []
+    for row, first, block in placed:
+        count = min(2, 3 - first)
+        rows += [taps_t[pl.ds((first + k) * channels + row, part), columns] for k in range(count)]
+        weights.append(block[:count].reshape(count * part, wide))
+    return lax.dot_general(
+        jnp.concatenate(rows, axis=0), jnp.concatenate(weights, axis=0), TN, preferred_element_type=F32
     )
 
 
-def partial_kernel(replicas, offsets, taps_t, *refs):
-    count = len(offsets)
-    convs, mixes, refs = refs[:count], refs[count : 2 * count], refs[2 * count :]
-    first = len(refs) == 2
+def store_shards(w, placed):
+    channels = w.shape[0] // 4
+    for row, first, block in placed:
+        for k in range(2):
+            w[pl.ds((first + k) * channels + row, block.shape[1]), :] = block[k]
+
+
+def partial_kernel(replicas, items, first, taps_t, *refs):
+    count = len(items)
+    placed = place_rows(replicas, items, refs[:count])
+    refs = refs[count:]
     acc, w = refs[:2] if first else refs[2:4]
     rows = taps_t.shape[1]
-    channels = w.shape[0] // 4
-    part = convs[0].shape[1]
     chunk = min(256, rows)
-    places = [owner_row(replicas, part, offset) for offset in offsets]
     for at in range(0, rows, chunk):
         columns = slice(at, at + chunk)
-        total = None if first else refs[0][columns, :]
-        for row, conv in zip(places, convs):
-            term = lax.dot_general(
-                tap_rows(taps_t, row, part, columns),
-                conv[...].reshape(3 * part, -1),
-                TN,
-                preferred_element_type=F32,
-            )
-            total = term if total is None else total + term
-        acc[columns, :] = total
-    for row, conv, mix in zip(places, convs, mixes):
-        for k in range(3):
-            w[pl.ds(k * channels + row, part), :] = conv[k]
-        w[pl.ds(3 * channels + row, part), :] = mix[0]
-
-
-def partial_call(replicas, offsets, taps_t, convs, mixes, held):
-    part, wide = convs[0].shape[1:]
+        term = shard_term(taps_t, columns, placed)
+        acc[columns, :] = term if first else refs[0][columns, :] + term
+    store_shards(w, placed)
+
+
+def partial_call(replicas, items, taps_t, blocks, held):
+    part, wide = blocks[0].shape[1:]
     rows = taps_t.shape[1]
-    count = len(offsets)
-    inputs = in_vmem(taps_t, *convs, *mixes, *held)
-    return pl.pallas_call(
-        functools.partial(partial_kernel, replicas, offsets),
+    count = len(items)
+    inputs = in_vmem(taps_t, *blocks, *held)
+    aliases = {1 + count + i: i for i in range(len(held))}
+    if held:
+        aliases |= {1 + i: 2 + i for i in range(count)}
+    return pl.pallas_call(
+        functools.partial(partial_kernel, replicas, items, not held),
         out_shape=[pltpu.VMEM((rows, wide), F32), pltpu.VMEM((2 * wide, wide), BF16)]
-        + [pltpu.VMEM(mix.shape, BF16) for mix in mixes if held],
+        + [pltpu.VMEM(block.shape, BF16) for block in blocks if held],
         in_specs=[VMEM] * len(inputs),
         out_specs=[VMEM] * (2 + count if held else 2),
-        input_output_aliases={1 + 2 * count: 0, 2 + 2 * count: 1, **{1 + count + i: 2 + i for i in range(count)}}
-        if held
-        else {},
-        compiler_params=PARAMS,
-        cost_estimate=cost(6 * rows * part * count * wide, 2**20),
-    )(*inputs)
-
-
-def forward_kernel(replicas, index, store, taps_t, conv_a, conv_b, mix, acc, w_in, *refs):
+        input_output_aliases=aliases,
+        compiler_params=PARAMS,
+        cost_estimate=cost(3 * rows * part * count * wide, 2**20),
+    )(*inputs)
+
+
+def forward_kernel(replicas, index, store, taps_t, low, high, acc, w_in, *refs):
     a1, a2, hid_t = refs[:3]
     samples, channels = a1.shape
-    part = mix.shape[1]
-    row = owner_row(replicas, part, replicas // 2)
-    ahead = conv_a.shape[0]
+    placed = place_rows(replicas, ((replicas // 2, 0), (replicas // 2, 2)), (low, high))
     chunk = min(256, samples)
     for at in range(0, samples, chunk):
         columns = slice(index * samples + at, index * samples + at + chunk)
-        pre = acc[columns, :]
-        for conv, first, last in ((conv_a, 0, ahead), (conv_b, ahead, 3)):
-            pre = pre + lax.dot_general(
-                tap_rows(taps_t, row, part, columns, first, last),
-                conv[...].reshape((last - first) * part, -1),
-                TN,
-                preferred_element_type=F32,
-            )
+        pre = acc[columns, :] + shard_term(taps_t, columns, placed)
         filt = jnp.tanh(pre[:, :channels])
         gate = jax.nn.sigmoid(pre[:, channels:])
         a1[at : at + chunk, :] = (gate * (1.0 - filt * filt)).astype(BF16)
         a2[at : at + chunk, :] = (filt * gate * (1.0 - gate)).astype(BF16)
         hid_t[:, at : at + chunk] = (filt * gate).T.astype(BF16)
     if store:
-        w = refs[3]
-        blocks = [conv_a[k] for k in range(ahead)] + [conv_b[k] for k in range(3 - ahead)] + [mix[0]]
-        for k, block in enumerate(blocks):
-            w[pl.ds(k * channels + row, part), :] = block
-
-
-def forward_call(replicas, index, micro, store, taps_t, conv_a, conv_b, mix, acc, w):
+        store_shards(refs[3], placed)
+
+
+def forward_call(replicas, index, micro, store, taps_t, low, high, acc, w):
     rows, wide = acc.shape
     channels = wide // 2
     samples = rows // micro
-    inputs = in_vmem(taps_t, conv_a, conv_b, mix, acc, w)
+    inputs = in_vmem(taps_t, low, high, acc, w)
     return pl.pallas_call(
         functools.partial(forward_kernel, replicas, index, store),
         out_shape=[pltpu.VMEM((samples, channels), BF16)] * 2
         + [pltpu.VMEM((channels, samples), BF16)]
         + ([pltpu.VMEM(w.shape, BF16)] if store else []),
-        in_specs=[VMEM] * 6,
+        in_specs=[VMEM] * 5,
         out_specs=[VMEM] * (4 if store else 3),
-        input_output_aliases={5: 3} if store else {},
+        input_output_aliases={4: 3} if store else {},
         compiler_params=PARAMS,
         cost_estimate=cost(2**28, 2**22),
     )(*inputs)
 
 
-def chain_kernel(stage, index, g_low, g_high, skip, a1, a2, w, *refs):
-    pg, ig_low, ig_high, gk, bt = refs[-5:]
+def chain_kernel(stage, index, g, skip, a1, a2, w, *refs):
+    pg, ig, gk, bt = refs[-4:]
     samples, channels = gk.shape
     chunk = samples // 2
     padding = bt.shape[1] - samples
@@ -177,10 +175,10 @@
     def _():
         for k in (1, 2):
             bt[k, samples:, :] = jnp.zeros((padding, channels), F32)
-        for at, g, ig in ((chunk, g_high, ig_high), (0, g_low, ig_low)):
+        for at in (chunk, 0):
             rows = slice(at, at + chunk)
             hid = lax.dot_general(
-                g[...], w[3 * channels :, :channels], NT, preferred_element_type=F32
+                g[rows, :], w[3 * channels :, :channels], NT, preferred_element_type=F32
             ) + lax.dot_general(
                 skip[index, rows, :], w[3 * channels :, channels:], NT, preferred_element_type=F32
             )
@@ -193,25 +191,24 @@
             piece = 64
             for first in range(at + chunk - piece, at - 1, -piece):
                 last = first + piece
-                here = slice(first - at, last - at)
-                total = g[here, :].astype(F32) + bt[0, first:last, :]
+                total = g[first:last, :].astype(F32) + bt[0, first:last, :]
                 total = total + bt[1, first + dilation : last + dilation, :]
                 total = total + bt[2, first + 2 * dilation : last + 2 * dilation, :]
-                ig[here, :] = total.astype(BF16)
-            gk[rows, :] = g[...]
+                ig[first:last, :] = total.astype(BF16)
+            gk[rows, :] = g[rows, :]
 
 
 def chain_call(stage, index, padding, g, skip, a1, a2, w, held):
     samples, channels = a1.shape
-    half = pltpu.VMEM((samples // 2, channels), BF16)
-    inputs = in_vmem(*g, skip, a1, a2, w, *held)
+    tile = pltpu.VMEM((samples, channels), BF16)
+    inputs = in_vmem(g, skip, a1, a2, w, *held)
     return pl.pallas_call(
         functools.partial(chain_kernel, stage, index),
-        out_shape=[pltpu.VMEM((samples, 2 * channels), BF16), half, half, pltpu.VMEM((samples, channels), BF16)],
+        out_shape=[pltpu.VMEM((samples, 2 * channels), BF16), tile, tile],
         in_specs=[VMEM] * len(inputs),
-        out_specs=[VMEM] * 4,
+        out_specs=[VMEM] * 3,
         scratch_shapes=[pltpu.VMEM((3, samples + padding, channels), F32)],
-        input_output_aliases={6 + i: i for i in range(len(held))},
+        input_output_aliases={5 + i: i for i in range(len(held))},
         compiler_params=PARAMS,
         cost_estimate=cost(8 * samples * channels * channels, 2**22),
     )(*inputs)
@@ -307,31 +304,32 @@
     half = replicas // 2
     right, left = ring_pairs(replicas)
 
+    def send(to_right, to_left):
+        return lax.ppermute(to_right, "dp", right), lax.ppermute(to_left, "dp", left)
+
     taps_t = prepare_call(x_ckpt[0].reshape(micro * seqs, samples, channels))
     conv = w_conv[0].transpose(1, 0, 2)
-    conv_r, conv_l, mix_r, mix_l = conv, conv, w_mix, w_mix
-    held = partial_call(replicas, (0,), taps_t, [conv], [w_mix], [])
+    low = conv[:2]
+    high = jnp.concatenate([conv[2:], w_mix], axis=0)
+    streams = {0: (low, low), 2: (high, high)}
+    held = partial_call(replicas, ((0, 0), (0, 2)), taps_t, [low, high], [])
     for step in range(1, half):
-        conv_r = lax.ppermute(conv_r, "dp", right)
-        conv_l = lax.ppermute(conv_l, "dp", left)
-        mix_r = lax.ppermute(mix_r, "dp", right)
-        mix_l = lax.ppermute(mix_l, "dp", left)
-        *held, mix_r, mix_l = partial_call(
-            replicas, (-step, step), taps_t, [conv_r, conv_l], [mix_r, mix_l], held
-        )
+        for first, (to_right, to_left) in streams.items():
+            got = send(to_right, to_left)
+            items = ((-step, first), (step, first))
+            *held, to_right, to_left = partial_call(replicas, items, taps_t, got, held)
+            streams[first] = (to_right, to_left)
     acc, w_full = held
-    conv_r = lax.ppermute(conv_r[:2], "dp", right)
-    conv_l = lax.ppermute(conv_l[2:], "dp", left)
-    mix_l = lax.ppermute(mix_l, "dp", left)
+    low = lax.ppermute(streams[0][0], "dp", right)
+    high = lax.ppermute(streams[2][1], "dp", left)
 
     skip = skip_cot.reshape(micro, block, channels)
-    top = top_cot.reshape(micro, 2, block // 2, channels)
-    g = [(top[m, 0], top[m, 1]) for m in range(micro)]
+    g = list(top_cot.reshape(micro, block, channels))
     padding = max(16, 2 * 2 ** (sections - 1))
     hid_t, held, ready = [], [()] * micro, []
     for m in range(micro):
         a1, a2, hid, *stored = forward_call(
-            replicas, m, micro, m == 0, taps_t, conv_r, conv_l, mix_l, acc, w_full
+            replicas, m, micro, m == 0, taps_t, low, high, acc, w_full
         )
         if stored:
             w_full = stored[0]
@@ -341,17 +339,13 @@
         for m in range(micro):
             held[m] = chain_call(stage, m, padding, g[m], skip, *ready[m], w_full, held[m])
             if stage:
-                hop = [(stage, stage - 1)]
-                g[m] = [lax.ppermute(piece, "pipe", hop) for piece in held[m][1:3]]
-    pre_grads, lows, highs, gs = zip(*held)
-    cot = jnp.concatenate([piece for pieces in zip(lows, highs) for piece in pieces], axis=0)
+                g[m] = lax.ppermute(held[m][1], "pipe", [(stage, stage - 1)])
+    pre_grads, cots, gs = zip(*held)
+    cot = jnp.stack(cots, axis=0)
 
     def terms(dist, tokens, kind=BF16):
         offsets = (dist,) if dist in (0, half) else (dist, -dist)
         return term_call(replicas, offsets, kind, taps_t, skip, hid_t, pre_grads, gs, tokens)
-
-    def send(to_right, to_left):
-        return lax.ppermute(to_right, "dp", right), lax.ppermute(to_left, "dp", left)
 
     low, high = terms(half, ())
     got_one = send(low, high)

time: 134 us -> 124 us (0.925)
  waiting for transfers between devices: 66.6 us -> 58.3 us
  starting transfers between devices: 41.3 us -> 35.6 us
  local copies, waits for them, and re-layouts: 1.42 us -> 3.51 us
    ppermute x27 -> x8, waiting for transfers between devices: 46.1 us -> 22.6 us  [the longest x6 17.8 us: local(): g[m] = lax.ppermute(held[m][1], 'pipe', [(stage, stage - 1)])]
    ppermute x27 -> x8, starting transfers between devices: 26.7 us -> 7.61 us  [the longest x6 5.53 us: local(): g[m] = lax.ppermute(held[m][1], 'pipe', [(stage, stage - 1)])]
    ppermute x7 -> x13, starting transfers between devices: 11.2 us -> 22.5 us  [send(): lax.ppermute(to_right, 'dp', right)]
    ppermute x7 -> x13, waiting for transfers between devices: 9.74 us -> 19.5 us  [send(): lax.ppermute(to_left, 'dp', left)]
    ppermute x7 -> x13, waiting for transfers between devices: 10.8 us -> 16.2 us  [send(): lax.ppermute(to_right, 'dp', right)]
    ppermute x7 -> x13, starting transfers between devices: 3.37 us -> 5.48 us  [send(): lax.ppermute(to_left, 'dp', left)]
    slice x2, local copies, waits for them, and re-layouts: 0.03 us -> 1.88 us  [the longest x1 0.97 us: local(): low = conv[:2]]
    pallas_call x4 -> x7, Pallas kernels: 5.75 us -> 6.62 us  [partial_call(): pl.pallas_call(functools.partial(partial_kernel, replicas, items, not hel...]
  transfers between devices with their start and end apart: 41 -> 34, of which waited for: 27 -> 28; matrix products, arithmetic and copies ran while one was open for 1% -> 2% of each run, Pallas kernels for 12% -> 13%
where the time goes in v5:
time: 124 us; the launch traced here: 123 us
  waiting for transfers between devices  58.3 us (47%)
  starting transfers between devices  35.6 us (29%)
  Pallas kernels  22.9 us (18%)
  local copies, waits for them, and re-layouts  3.51 us (3%)
  other arithmetic  1.99 us (2%)
    ppermute x13, starting transfers between devices, send(): lax.ppermute(to_right, 'dp', right)  22.5 us
    ppermute x13, waiting for transfers between devices, send(): lax.ppermute(to_left, 'dp', left)  19.5 us
    ppermute x6, waiting for transfers between devices, local(): g[m] = lax.ppermute(held[m][1], 'pipe', [(stage, stage - 1)])  17.8 us
    ppermute x13, waiting for transfers between devices, send(): lax.ppermute(to_right, 'dp', right)  16.2 us
    pallas_call x7, Pallas kernels, partial_call(): pl.pallas_call(functools.partial(partial_kernel, replicas, items, not hel...  6.62 us
    pallas_call x8, Pallas kernels, chain_call(): pl.pallas_call(functools.partial(chain_kernel, stage, index), out_shape=[...  5.89 us
    pallas_call x5, Pallas kernels, term_call(): pl.pallas_call(functools.partial(term_kernel, replicas, offsets, micro),...  5.58 us
    ppermute x6, starting transfers between devices, local(): g[m] = lax.ppermute(held[m][1], 'pipe', [(stage, stage - 1)])  5.53 us
  transfers between devices with their start and end apart: 34, of which 28 were waited for; matrix products, arithmetic and copies ran while one was open for 2% of the time, Pallas kernels for 13%

profile of v5, /device:TPU:0, one launch (start us, length us, event | category | flops | bytes accessed | tf_op | source)
XLA Modules:
  0.0 123.2 jit_solution(9470912988468729709)
XLA Ops:
  1.6 3.1 %collective-permute-start = (bf16[2,64,1024]{2,1,0:T(8,128)(2,1)S(1)}, bf16[2,64,1024]{2,1,0:T(8,128)(2,1)S(1)}, u32[]{:S(2)}, u32[]{:S(2)}) collective-permute-start(bf16[2,64,1024]{2,1,0:T(8,128)(2,1)S(1)} %slice.10.refs_0_), channel_id=1, source_target_pairs={{0,2},{2,4},{4,6},{6,7},{7,5},{5,3},{3,1},{1,0},{8,10},{10,12},{12... | collective-permute-start | bytes 786440 | tf_op jit(solution)/shard_map/ppermute | solution.py:308
  6.5 2.1 %collective-permute-start.4 = (bf16[2,64,1024]{2,1,0:T(8,128)(2,1)S(1)}, bf16[2,64,1024]{2,1,0:T(8,128)(2,1)S(1)}, u32[]{:S(2)}, u32[]{:S(2)}) collective-permute-start(bf16[2,64,1024]{2,1,0:T(8,128)(2,1)S(1)} %pad_maximum_fusion.refs_1_), channel_id=1, source_target_pairs={{0,2},{2,4},{4,6},{6,7},{7,5},{5,3},{3,1},{1,0},{8,10},{10,12},{12... | collective-permute-start | bytes 786440 | tf_op jit(solution)/shard_map/ppermute | solution.py:308
  12.0 1.9 %collective-permute-done.1.refs_1_ = bf16[2,64,1024]{2,1,0:T(8,128)(2,1)S(1)} collective-permute-done((bf16[2,64,1024]{2,1,0:T(8,128)(2,1)S(1)}, bf16[2,64,1024]{2,1,0:T(8,128)(2,1)S(1)}, u32[]{:S(2)}, u32[]{:S(2)}) %collective-permute-start.1) | collective-permute-done | bytes 262176 | tf_op jit(solution)/shard_map/ppermute | solution.py:308
  14.9 1.6 %collective-permute-start.2 = (bf16[2,64,1024]{2,1,0:T(8,128)(2,1)S(1)}, bf16[2,64,1024]{2,1,0:T(8,128)(2,1)S(1)}, u32[]{:S(2)}, u32[]{:S(2)}) collective-permute-start(bf16[2,64,1024]{2,1,0:T(8,128)(2,1)S(1)} %get-tuple-element.88), channel_id=1, source_target_pairs={{0,2},{2,4},{4,6},{6,7},{7,5},{5,3},{3,1},{1,0},{8,10},{10,12},{12... | collective-permute-start | bytes 786440 | tf_op jit(solution)/shard_map/ppermute | solution.py:308
  17.4 2.2 %collective-permute-done.5.refs_1_ = bf16[2,64,1024]{2,1,0:T(8,128)(2,1)S(1)} collective-permute-done((bf16[2,64,1024]{2,1,0:T(8,128)(2,1)S(1)}, bf16[2,64,1024]{2,1,0:T(8,128)(2,1)S(1)}, u32[]{:S(2)}, u32[]{:S(2)}) %collective-permute-start.5) | collective-permute-done | bytes 262176 | tf_op jit(solution)/shard_map/ppermute | solution.py:308
  20.5 1.6 %collective-permute-start.8 = (bf16[2,64,1024]{2,1,0:T(8,128)(2,1)S(1)}, bf16[2,64,1024]{2,1,0:T(8,128)(2,1)S(1)}, u32[]{:S(2)}, u32[]{:S(2)}) collective-permute-start(bf16[2,64,1024]{2,1,0:T(8,128)(2,1)S(1)} %get-tuple-element.96), channel_id=1, source_target_pairs={{0,2},{2,4},{4,6},{6,7},{7,5},{5,3},{3,1},{1,0},{8,10},{10,12},{12... | collective-permute-start | bytes 786440 | tf_op jit(solution)/shard_map/ppermute | solution.py:308
  23.9 1.7 %collective-permute-done.3.refs_1_ = bf16[2,64,1024]{2,1,0:T(8,128)(2,1)S(1)} collective-permute-done((bf16[2,64,1024]{2,1,0:T(8,128)(2,1)S(1)}, bf16[2,64,1024]{2,1,0:T(8,128)(2,1)S(1)}, u32[]{:S(2)}, u32[]{:S(2)}) %collective-permute-start.3) | collective-permute-done | bytes 262176 | tf_op jit(solution)/shard_map/ppermute | solution.py:308
  26.7 1.6 %collective-permute-start.6 = (bf16[2,64,1024]{2,1,0:T(8,128)(2,1)S(1)}, bf16[2,64,1024]{2,1,0:T(8,128)(2,1)S(1)}, u32[]{:S(2)}, u32[]{:S(2)}) collective-permute-start(bf16[2,64,1024]{2,1,0:T(8,128)(2,1)S(1)} %get-tuple-element.94), channel_id=1, source_target_pairs={{0,2},{2,4},{4,6},{6,7},{7,5},{5,3},{3,1},{1,0},{8,10},{10,12},{12... | collective-permute-start | bytes 786440 | tf_op jit(solution)/shard_map/ppermute | solution.py:308
  29.8 1.5 %collective-permute-done.9.refs_1_ = bf16[2,64,1024]{2,1,0:T(8,128)(2,1)S(1)} collective-permute-done((bf16[2,64,1024]{2,1,0:T(8,128)(2,1)S(1)}, bf16[2,64,1024]{2,1,0:T(8,128)(2,1)S(1)}, u32[]{:S(2)}, u32[]{:S(2)}) %collective-permute-start.9) | collective-permute-done | bytes 262176 | tf_op jit(solution)/shard_map/ppermute | solution.py:308
  32.3 1.6 %collective-permute-start.11 = (bf16[2,64,1024]{2,1,0:T(8,128)(2,1)S(1)}, bf16[2,64,1024]{2,1,0:T(8,128)(2,1)S(1)}, u32[]{:S(2)}, u32[]{:S(2)}) collective-permute-start(bf16[2,64,1024]{2,1,0:T(8,128)(2,1)S(1)} %get-tuple-element.103), channel_id=1, source_target_pairs={{0,2},{2,4},{4,6},{6,7},{7,5},{5,3},{3,1},{1,0},{8,10},{10,12},{12... | collective-permute-start | bytes 786440 | tf_op jit(solution)/shard_map/ppermute | solution.py:308
  34.3 1.5 %collective-permute-done.6.refs_0_ = bf16[2,64,1024]{2,1,0:T(8,128)(2,1)S(1)} collective-permute-done((bf16[2,64,1024]{2,1,0:T(8,128)(2,1)S(1)}, bf16[2,64,1024]{2,1,0:T(8,128)(2,1)S(1)}, u32[]{:S(2)}, u32[]{:S(2)}) %collective-permute-start.6) | collective-permute-done | bytes 262176 | tf_op jit(solution)/shard_map/ppermute | solution.py:308
  35.8 1.7 %collective-permute-done.7.refs_1_ = bf16[2,64,1024]{2,1,0:T(8,128)(2,1)S(1)} collective-permute-done((bf16[2,64,1024]{2,1,0:T(8,128)(2,1)S(1)}, bf16[2,64,1024]{2,1,0:T(8,128)(2,1)S(1)}, u32[]{:S(2)}, u32[]{:S(2)}) %collective-permute-start.7) | collective-permute-done | bytes 262176 | tf_op jit(solution)/shard_map/ppermute | solution.py:308
  39.0 1.5 %collective-permute-done.12.refs_1_ = bf16[2,64,1024]{2,1,0:T(8,128)(2,1)S(1)} collective-permute-done((bf16[2,64,1024]{2,1,0:T(8,128)(2,1)S(1)}, bf16[2,64,1024]{2,1,0:T(8,128)(2,1)S(1)}, u32[]{:S(2)}, u32[]{:S(2)}) %collective-permute-start.12) | collective-permute-done | bytes 262176 | tf_op jit(solution)/shard_map/ppermute | solution.py:308
  41.8 1.7 %collective-permute-start.10 = (bf16[2,64,1024]{2,1,0:T(8,128)(2,1)S(1)}, bf16[2,64,1024]{2,1,0:T(8,128)(2,1)S(1)}, u32[]{:S(2)}, u32[]{:S(2)}) collective-permute-start(bf16[2,64,1024]{2,1,0:T(8,128)(2,1)S(1)} %get-tuple-element.102), channel_id=1, source_target_pairs={{0,2},{2,4},{4,6},{6,7},{7,5},{5,3},{3,1},{1,0},{8,10},{10,12},{12... | collective-permute-start | bytes 786440 | tf_op jit(solution)/shard_map/ppermute | solution.py:323
  43.6 4.3 %collective-permute-done.13.high = bf16[2,64,1024]{2,1,0:T(8,128)(2,1)S(1)} collective-permute-done((bf16[2,64,1024]{2,1,0:T(8,128)(2,1)S(1)}, bf16[2,64,1024]{2,1,0:T(8,128)(2,1)S(1)}, u32[]{:S(2)}, u32[]{:S(2)}) %collective-permute-start.13) | collective-permute-done | bytes 262176 | tf_op jit(solution)/shard_map/ppermute | solution.py:324
  56.6 14.9 %collective-permute-done.16.g = bf16[512,512]{1,0:T(8,128)(2,1)S(1)} collective-permute-done((bf16[512,512]{1,0:T(8,128)(2,1)S(1)}, bf16[512,512]{1,0:T(8,128)(2,1)S(1)}, u32[]{:S(2)}, u32[]{:S(2)}) %collective-permute-start.16) | collective-permute-done | bytes 524320 | tf_op jit(solution)/shard_map/ppermute | solution.py:342
  71.5 2.8 %shard_map.88 = (bf16[512,1024]{1,0:T(8,128)(2,1)S(1)}, bf16[512,512]{1,0:T(8,128)(2,1)S(1)}, bf16[512,512]{1,0:T(8,128)(2,1)S(1)}) custom-call(bf16[512,512]{1,0:T(8,128)(2,1)S(1)} %collective-permute-done.16.g, bf16[2,512,512]{2,1,0:T(8,128)(2,1)S(1)} %bitcast.25, ...), custom_call_target="tpu_custom_call", output_to_operand_aliasing={{0}: (5, {}), {1}: (6, {}), {2}: (7, {})} | custom-call | flops 1073741824 | bytes 4194304 | tf_op jit(solution)/shard_map/pallas_call | solution.py:205
  74.3 2.8 %collective-permute-done.19.g = bf16[512,512]{1,0:T(8,128)(2,1)S(1)} collective-permute-done((bf16[512,512]{1,0:T(8,128)(2,1)S(1)}, bf16[512,512]{1,0:T(8,128)(2,1)S(1)}, u32[]{:S(2)}, u32[]{:S(2)}) %collective-permute-start.19) | collective-permute-done | bytes 524320 | tf_op jit(solution)/shard_map/ppermute | solution.py:342
  77.1 2.8 %shard_map.93 = (bf16[512,1024]{1,0:T(8,128)(2,1)S(1)}, bf16[512,512]{1,0:T(8,128)(2,1)S(1)}, bf16[512,512]{1,0:T(8,128)(2,1)S(1)}) custom-call(bf16[512,512]{1,0:T(8,128)(2,1)S(1)} %collective-permute-done.19.g, bf16[2,512,512]{2,1,0:T(8,128)(2,1)S(1)} %bitcast.26, ...), custom_call_target="tpu_custom_call", output_to_operand_aliasing={{0}: (5, {}), {1}: (6, {}), {2}: (7, {})} | custom-call | flops 1073741824 | bytes 4194304 | tf_op jit(solution)/shard_map/pallas_call | solution.py:205
  80.9 1.5 %collective-permute-start.20 = (bf16[2,64,1024]{2,1,0:T(8,128)(2,1)S(1)}, bf16[2,64,1024]{2,1,0:T(8,128)(2,1)S(1)}, u32[]{:S(2)}, u32[]{:S(2)}) collective-permute-start(bf16[2,64,1024]{2,1,0:T(8,128)(2,1)S(1)} %get-tuple-element.141.refs_6_), channel_id=1, source_target_pairs={{0,2},{2,4},{4,6},{6,7},{7,5},{5,3},{3,1},{1,0},{8,10},{10,12},{12... | collective-permute-start | bytes 786440 | tf_op jit(solution)/shard_map/ppermute | solution.py:308
  84.2 1.5 %collective-permute-start.24 = (bf16[2,64,1024]{2,1,0:T(8,128)(2,1)S(1)}, bf16[2,64,1024]{2,1,0:T(8,128)(2,1)S(1)}, u32[]{:S(2)}, u32[]{:S(2)}) collective-permute-start(bf16[2,64,1024]{2,1,0:T(8,128)(2,1)S(1)} %get-tuple-element.151), channel_id=1, source_target_pairs={{0,2},{2,4},{4,6},{6,7},{7,5},{5,3},{3,1},{1,0},{8,10},{10,12},{12... | collective-permute-start | bytes 786440 | tf_op jit(solution)/shard_map/ppermute | solution.py:308
  86.3 3.9 %collective-permute-done.20.got_r = bf16[2,64,1024]{2,1,0:T(8,128)(2,1)S(1)} collective-permute-done((bf16[2,64,1024]{2,1,0:T(8,128)(2,1)S(1)}, bf16[2,64,1024]{2,1,0:T(8,128)(2,1)S(1)}, u32[]{:S(2)}, u32[]{:S(2)}) %collective-permute-start.20) | collective-permute-done | bytes 262176 | tf_op jit(solution)/shard_map/ppermute | solution.py:308
  90.2 1.4 %collective-permute-done.21.got_l = bf16[2,64,1024]{2,1,0:T(8,128)(2,1)S(1)} collective-permute-done((bf16[2,64,1024]{2,1,0:T(8,128)(2,1)S(1)}, bf16[2,64,1024]{2,1,0:T(8,128)(2,1)S(1)}, u32[]{:S(2)}, u32[]{:S(2)}) %collective-permute-start.21) | collective-permute-done | bytes 262176 | tf_op jit(solution)/shard_map/ppermute | solution.py:308
  91.7 1.6 %collective-permute-start.22 = (bf16[2,64,1024]{2,1,0:T(8,128)(2,1)S(1)}, bf16[2,64,1024]{2,1,0:T(8,128)(2,1)S(1)}, u32[]{:S(2)}, u32[]{:S(2)}) collective-permute-start(bf16[2,64,1024]{2,1,0:T(8,128)(2,1)S(1)} %get-tuple-element.145.refs_6_.refs_0_), channel_id=1, source_target_pairs={{0,2},{2,4},{4,6},{6,7},{7,5},{5,3},{3,1},{1,0},{8,10},{10,12},{12... | collective-permute-start | bytes 786440 | tf_op jit(solution)/shard_map/ppermute | solution.py:308
  97.3 1.6 %collective-permute-start.28 = (bf16[2,64,1024]{2,1,0:T(8,128)(2,1)S(1)}, bf16[2,64,1024]{2,1,0:T(8,128)(2,1)S(1)}, u32[]{:S(2)}, u32[]{:S(2)}) collective-permute-start(bf16[2,64,1024]{2,1,0:T(8,128)(2,1)S(1)} %get-tuple-element.153.refs_0_), channel_id=1, source_target_pairs={{0,2},{2,4},{4,6},{6,7},{7,5},{5,3},{3,1},{1,0},{8,10},{10,12},{12... | collective-permute-start | bytes 786440 | tf_op jit(solution)/shard_map/ppermute | solution.py:308
  99.4 2.0 %collective-permute-done.22.got_r = bf16[2,64,1024]{2,1,0:T(8,128)(2,1)S(1)} collective-permute-done((bf16[2,64,1024]{2,1,0:T(8,128)(2,1)S(1)}, bf16[2,64,1024]{2,1,0:T(8,128)(2,1)S(1)}, u32[]{:S(2)}, u32[]{:S(2)}) %collective-permute-start.22) | collective-permute-done | bytes 262176 | tf_op jit(solution)/shard_map/ppermute | solution.py:308
  102.9 1.6 %collective-permute-start.26 = (bf16[2,64,1024]{2,1,0:T(8,128)(2,1)S(1)}, bf16[2,64,1024]{2,1,0:T(8,128)(2,1)S(1)}, u32[]{:S(2)}, u32[]{:S(2)}) collective-permute-start(bf16[2,64,1024]{2,1,0:T(8,128)(2,1)S(1)} %get-tuple-element.154.refs_6_.refs_0_), channel_id=1, source_target_pairs={{0,2},{2,4},{4,6},{6,7},{7,5},{5,3},{3,1},{1,0},{8,10},{10,12},{12... | collective-permute-start | bytes 786440 | tf_op jit(solution)/shard_map/ppermute | solution.py:308
  109.2 1.4 %collective-permute-start.32 = (bf16[2,64,1024]{2,1,0:T(8,128)(2,1)S(1)}, bf16[2,64,1024]{2,1,0:T(8,128)(2,1)S(1)}, u32[]{:S(2)}, u32[]{:S(2)}) collective-permute-start(bf16[2,64,1024]{2,1,0:T(8,128)(2,1)S(1)} %get-tuple-element.161.refs_0_), channel_id=1, source_target_pairs={{0,2},{2,4},{4,6},{6,7},{7,5},{5,3},{3,1},{1,0},{8,10},{10,12},{12... | collective-permute-start | bytes 786440 | tf_op jit(solution)/shard_map/ppermute | solution.py:308
  110.6 2.0 %collective-permute-done.26.got_r = bf16[2,64,1024]{2,1,0:T(8,128)(2,1)S(1)} collective-permute-done((bf16[2,64,1024]{2,1,0:T(8,128)(2,1)S(1)}, bf16[2,64,1024]{2,1,0:T(8,128)(2,1)S(1)}, u32[]{:S(2)}, u32[]{:S(2)}) %collective-permute-start.26) | collective-permute-done | bytes 262176 | tf_op jit(solution)/shard_map/ppermute | solution.py:308
  114.2 1.6 %collective-permute-start.30 = (bf16[2,64,1024]{2,1,0:T(8,128)(2,1)S(1)}, bf16[2,64,1024]{2,1,0:T(8,128)(2,1)S(1)}, u32[]{:S(2)}, u32[]{:S(2)}) collective-permute-start(bf16[2,64,1024]{2,1,0:T(8,128)(2,1)S(1)} %get-tuple-element.162.refs_6_), channel_id=1, source_target_pairs={{0,2},{2,4},{4,6},{6,7},{7,5},{5,3},{3,1},{1,0},{8,10},{10,12},{12... | collective-permute-start | bytes 786440 | tf_op jit(solution)/shard_map/ppermute | solution.py:308
  118.5 2.1 %collective-permute-done.30.low_r = bf16[2,64,1024]{2,1,0:T(8,128)(2,1)S(1)} collective-permute-done((bf16[2,64,1024]{2,1,0:T(8,128)(2,1)S(1)}, bf16[2,64,1024]{2,1,0:T(8,128)(2,1)S(1)}, u32[]{:S(2)}, u32[]{:S(2)}) %collective-permute-start.30) | collective-permute-done | bytes 262176 | tf_op jit(solution)/shard_map/ppermute | solution.py:308
  120.6 1.6 %collective-permute-done.33.high_l = bf16[2,64,1024]{2,1,0:T(8,128)(2,1)S(1)} collective-permute-done((bf16[2,64,1024]{2,1,0:T(8,128)(2,1)S(1)}, bf16[2,64,1024]{2,1,0:T(8,128)(2,1)S(1)}, u32[]{:S(2)}, u32[]{:S(2)}) %collective-permute-start.33) | collective-permute-done | bytes 262176 | tf_op jit(solution)/shard_map/ppermute | solution.py:308
  (76 shorter events, 45.4 us)
Async XLA Ops:
  1.6 10.4 %collective-permute-start = (bf16[2,64,1024]{2,1,0:T(8,128)(2,1)S(1)}, bf16[2,64,1024]{2,1,0:T(8,128)(2,1)S(1)}, u32[]{:S(2)}, u32[]{:S(2)}) collective-permute-start(bf16[2,64,1024]{2,1,0:T(8,128)(2,1)S(1)} %slice.10.refs_0_), channel_id=1, source_target_pairs={{0,2},{2,4},{4,6},{6,7},{7,5},{5,3},{3,1},{1,0},{8,10},{10,12},{12... | collective-permute-start | bytes 786440 | tf_op jit(solution)/shard_map/ppermute | solution.py:308
  4.7 9.2 %collective-permute-start.1 = (bf16[2,64,1024]{2,1,0:T(8,128)(2,1)S(1)}, bf16[2,64,1024]{2,1,0:T(8,128)(2,1)S(1)}, u32[]{:S(2)}, u32[]{:S(2)}) collective-permute-start(bf16[2,64,1024]{2,1,0:T(8,128)(2,1)S(1)} %slice.10.refs_0_), channel_id=1, source_target_pairs={{2,0},{4,2},{6,4},{7,6},{5,7},{3,5},{1,3},{0,1},{10,8},{12,10},{14... | collective-permute-start | bytes 786440 | tf_op jit(solution)/shard_map/ppermute | solution.py:308
  6.5 10.8 %collective-permute-start.4 = (bf16[2,64,1024]{2,1,0:T(8,128)(2,1)S(1)}, bf16[2,64,1024]{2,1,0:T(8,128)(2,1)S(1)}, u32[]{:S(2)}, u32[]{:S(2)}) collective-permute-start(bf16[2,64,1024]{2,1,0:T(8,128)(2,1)S(1)} %pad_maximum_fusion.refs_1_), channel_id=1, source_target_pairs={{0,2},{2,4},{4,6},{6,7},{7,5},{5,3},{3,1},{1,0},{8,10},{10,12},{12... | collective-permute-start | bytes 786440 | tf_op jit(solution)/shard_map/ppermute | solution.py:308
  8.6 10.9 %collective-permute-start.5 = (bf16[2,64,1024]{2,1,0:T(8,128)(2,1)S(1)}, bf16[2,64,1024]{2,1,0:T(8,128)(2,1)S(1)}, u32[]{:S(2)}, u32[]{:S(2)}) collective-permute-start(bf16[2,64,1024]{2,1,0:T(8,128)(2,1)S(1)} %pad_maximum_fusion.refs_1_), channel_id=1, source_target_pairs={{2,0},{4,2},{6,4},{7,6},{5,7},{3,5},{1,3},{0,1},{10,8},{12,10},{14... | collective-permute-start | bytes 786440 | tf_op jit(solution)/shard_map/ppermute | solution.py:308
  14.9 9.0 %collective-permute-start.2 = (bf16[2,64,1024]{2,1,0:T(8,128)(2,1)S(1)}, bf16[2,64,1024]{2,1,0:T(8,128)(2,1)S(1)}, u32[]{:S(2)}, u32[]{:S(2)}) collective-permute-start(bf16[2,64,1024]{2,1,0:T(8,128)(2,1)S(1)} %get-tuple-element.88), channel_id=1, source_target_pairs={{0,2},{2,4},{4,6},{6,7},{7,5},{5,3},{3,1},{1,0},{8,10},{10,12},{12... | collective-permute-start | bytes 786440 | tf_op jit(solution)/shard_map/ppermute | solution.py:308
  16.5 9.1 %collective-permute-start.3 = (bf16[2,64,1024]{2,1,0:T(8,128)(2,1)S(1)}, bf16[2,64,1024]{2,1,0:T(8,128)(2,1)S(1)}, u32[]{:S(2)}, u32[]{:S(2)}) collective-permute-start(bf16[2,64,1024]{2,1,0:T(8,128)(2,1)S(1)} %get-tuple-element.89), channel_id=1, source_target_pairs={{2,0},{4,2},{6,4},{7,6},{5,7},{3,5},{1,3},{0,1},{10,8},{12,10},{14... | collective-permute-start | bytes 786440 | tf_op jit(solution)/shard_map/ppermute | solution.py:308
  20.5 9.3 %collective-permute-start.8 = (bf16[2,64,1024]{2,1,0:T(8,128)(2,1)S(1)}, bf16[2,64,1024]{2,1,0:T(8,128)(2,1)S(1)}, u32[]{:S(2)}, u32[]{:S(2)}) collective-permute-start(bf16[2,64,1024]{2,1,0:T(8,128)(2,1)S(1)} %get-tuple-element.96), channel_id=1, source_target_pairs={{0,2},{2,4},{4,6},{6,7},{7,5},{5,3},{3,1},{1,0},{8,10},{10,12},{12... | collective-permute-start | bytes 786440 | tf_op jit(solution)/shard_map/ppermute | solution.py:308
  22.1 9.2 %collective-permute-start.9 = (bf16[2,64,1024]{2,1,0:T(8,128)(2,1)S(1)}, bf16[2,64,1024]{2,1,0:T(8,128)(2,1)S(1)}, u32[]{:S(2)}, u32[]{:S(2)}) collective-permute-start(bf16[2,64,1024]{2,1,0:T(8,128)(2,1)S(1)} %get-tuple-element.97), channel_id=1, source_target_pairs={{2,0},{4,2},{6,4},{7,6},{5,7},{3,5},{1,3},{0,1},{10,8},{12,10},{14... | collective-permute-start | bytes 786440 | tf_op jit(solution)/shard_map/ppermute | solution.py:308
  26.7 9.1 %collective-permute-start.6 = (bf16[2,64,1024]{2,1,0:T(8,128)(2,1)S(1)}, bf16[2,64,1024]{2,1,0:T(8,128)(2,1)S(1)}, u32[]{:S(2)}, u32[]{:S(2)}) collective-permute-start(bf16[2,64,1024]{2,1,0:T(8,128)(2,1)S(1)} %get-tuple-element.94), channel_id=1, source_target_pairs={{0,2},{2,4},{4,6},{6,7},{7,5},{5,3},{3,1},{1,0},{8,10},{10,12},{12... | collective-permute-start | bytes 786440 | tf_op jit(solution)/shard_map/ppermute | solution.py:308
  28.3 9.2 %collective-permute-start.7 = (bf16[2,64,1024]{2,1,0:T(8,128)(2,1)S(1)}, bf16[2,64,1024]{2,1,0:T(8,128)(2,1)S(1)}, u32[]{:S(2)}, u32[]{:S(2)}) collective-permute-start(bf16[2,64,1024]{2,1,0:T(8,128)(2,1)S(1)} %get-tuple-element.95), channel_id=1, source_target_pairs={{2,0},{4,2},{6,4},{7,6},{5,7},{3,5},{1,3},{0,1},{10,8},{12,10},{14... | collective-permute-start | bytes 786440 | tf_op jit(solution)/shard_map/ppermute | solution.py:308
  32.3 6.8 %collective-permute-start.11 = (bf16[2,64,1024]{2,1,0:T(8,128)(2,1)S(1)}, bf16[2,64,1024]{2,1,0:T(8,128)(2,1)S(1)}, u32[]{:S(2)}, u32[]{:S(2)}) collective-permute-start(bf16[2,64,1024]{2,1,0:T(8,128)(2,1)S(1)} %get-tuple-element.103), channel_id=1, source_target_pairs={{0,2},{2,4},{4,6},{6,7},{7,5},{5,3},{3,1},{1,0},{8,10},{10,12},{12... | collective-permute-start | bytes 786440 | tf_op jit(solution)/shard_map/ppermute | solution.py:308
  33.9 6.7 %collective-permute-start.12 = (bf16[2,64,1024]{2,1,0:T(8,128)(2,1)S(1)}, bf16[2,64,1024]{2,1,0:T(8,128)(2,1)S(1)}, u32[]{:S(2)}, u32[]{:S(2)}) collective-permute-start(bf16[2,64,1024]{2,1,0:T(8,128)(2,1)S(1)} %get-tuple-element.104), channel_id=1, source_target_pairs={{2,0},{4,2},{6,4},{7,6},{5,7},{3,5},{1,3},{0,1},{10,8},{12,10},{14... | collective-permute-start | bytes 786440 | tf_op jit(solution)/shard_map/ppermute | solution.py:308
  41.5 6.4 %collective-permute-start.13 = (bf16[2,64,1024]{2,1,0:T(8,128)(2,1)S(1)}, bf16[2,64,1024]{2,1,0:T(8,128)(2,1)S(1)}, u32[]{:S(2)}, u32[]{:S(2)}) collective-permute-start(bf16[2,64,1024]{2,1,0:T(8,128)(2,1)S(1)} %get-tuple-element.107), channel_id=1, source_target_pairs={{2,0},{4,2},{6,4},{7,6},{5,7},{3,5},{1,3},{0,1},{10,8},{12,10},{14... | collective-permute-start | bytes 786440 | tf_op jit(solution)/shard_map/ppermute | solution.py:324
  41.8 6.7 %collective-permute-start.10 = (bf16[2,64,1024]{2,1,0:T(8,128)(2,1)S(1)}, bf16[2,64,1024]{2,1,0:T(8,128)(2,1)S(1)}, u32[]{:S(2)}, u32[]{:S(2)}) collective-permute-start(bf16[2,64,1024]{2,1,0:T(8,128)(2,1)S(1)} %get-tuple-element.102), channel_id=1, source_target_pairs={{0,2},{2,4},{4,6},{6,7},{7,5},{5,3},{3,1},{1,0},{8,10},{10,12},{12... | collective-permute-start | bytes 786440 | tf_op jit(solution)/shard_map/ppermute | solution.py:323
  49.7 2.5 %collective-permute-start.14 = (bf16[512,512]{1,0:T(8,128)(2,1)S(1)}, bf16[512,512]{1,0:T(8,128)(2,1)S(1)}, u32[]{:S(2)}, u32[]{:S(2)}) collective-permute-start(bf16[512,512]{1,0:T(8,128)(2,1)S(1)} %get-tuple-element.113.refs_1_), channel_id=1, source_target_pairs={{24,16},{25,17},{26,18},{27,19},{28,20},{29,21},{30,22},{31,23}} | collective-permute-start | bytes 1572872 | tf_op jit(solution)/shard_map/ppermute | solution.py:342
  53.0 2.0 %collective-permute-start.18 = (bf16[512,512]{1,0:T(8,128)(2,1)S(1)}, bf16[512,512]{1,0:T(8,128)(2,1)S(1)}, u32[]{:S(2)}, u32[]{:S(2)}) collective-permute-start(bf16[512,512]{1,0:T(8,128)(2,1)S(1)} %get-tuple-element.128.refs_1_), channel_id=1, source_target_pairs={{16,8},{17,9},{18,10},{19,11},{20,12},{21,13},{22,14},{23,15}} | collective-permute-start | bytes 1572872 | tf_op jit(solution)/shard_map/ppermute | solution.py:342
  53.7 17.8 %collective-permute-start.16 = (bf16[512,512]{1,0:T(8,128)(2,1)S(1)}, bf16[512,512]{1,0:T(8,128)(2,1)S(1)}, u32[]{:S(2)}, u32[]{:S(2)}) collective-permute-start(bf16[512,512]{1,0:T(8,128)(2,1)S(1)} %get-tuple-element.119.refs_1_), channel_id=1, source_target_pairs={{8,0},{9,1},{10,2},{11,3},{12,4},{13,5},{14,6},{15,7}} | collective-permute-start | bytes 1572872 | tf_op jit(solution)/shard_map/ppermute | solution.py:342
  55.3 21.9 %collective-permute-start.19 = (bf16[512,512]{1,0:T(8,128)(2,1)S(1)}, bf16[512,512]{1,0:T(8,128)(2,1)S(1)}, u32[]{:S(2)}, u32[]{:S(2)}) collective-permute-start(bf16[512,512]{1,0:T(8,128)(2,1)S(1)} %get-tuple-element.131.refs_1_), channel_id=1, source_target_pairs={{8,0},{9,1},{10,2},{11,3},{12,4},{13,5},{14,6},{15,7}} | collective-permute-start | bytes 1572872 | tf_op jit(solution)/shard_map/ppermute | solution.py:342
  80.9 9.3 %collective-permute-start.20 = (bf16[2,64,1024]{2,1,0:T(8,128)(2,1)S(1)}, bf16[2,64,1024]{2,1,0:T(8,128)(2,1)S(1)}, u32[]{:S(2)}, u32[]{:S(2)}) collective-permute-start(bf16[2,64,1024]{2,1,0:T(8,128)(2,1)S(1)} %get-tuple-element.141.refs_6_), channel_id=1, source_target_pairs={{0,2},{2,4},{4,6},{6,7},{7,5},{5,3},{3,1},{1,0},{8,10},{10,12},{12... | collective-permute-start | bytes 786440 | tf_op jit(solution)/shard_map/ppermute | solution.py:308
  82.3 9.2 %collective-permute-start.21 = (bf16[2,64,1024]{2,1,0:T(8,128)(2,1)S(1)}, bf16[2,64,1024]{2,1,0:T(8,128)(2,1)S(1)}, u32[]{:S(2)}, u32[]{:S(2)}) collective-permute-start(bf16[2,64,1024]{2,1,0:T(8,128)(2,1)S(1)} %get-tuple-element.144), channel_id=1, source_target_pairs={{2,0},{4,2},{6,4},{7,6},{5,7},{3,5},{1,3},{0,1},{10,8},{12,10},{14... | collective-permute-start | bytes 786440 | tf_op jit(solution)/shard_map/ppermute | solution.py:308
  84.2 11.6 %collective-permute-start.24 = (bf16[2,64,1024]{2,1,0:T(8,128)(2,1)S(1)}, bf16[2,64,1024]{2,1,0:T(8,128)(2,1)S(1)}, u32[]{:S(2)}, u32[]{:S(2)}) collective-permute-start(bf16[2,64,1024]{2,1,0:T(8,128)(2,1)S(1)} %get-tuple-element.151), channel_id=1, source_target_pairs={{0,2},{2,4},{4,6},{6,7},{7,5},{5,3},{3,1},{1,0},{8,10},{10,12},{12... | collective-permute-start | bytes 786440 | tf_op jit(solution)/shard_map/ppermute | solution.py:308
  85.7 11.5 %collective-permute-start.25 = (bf16[2,64,1024]{2,1,0:T(8,128)(2,1)S(1)}, bf16[2,64,1024]{2,1,0:T(8,128)(2,1)S(1)}, u32[]{:S(2)}, u32[]{:S(2)}) collective-permute-start(bf16[2,64,1024]{2,1,0:T(8,128)(2,1)S(1)} %get-tuple-element.152), channel_id=1, source_target_pairs={{2,0},{4,2},{6,4},{7,6},{5,7},{3,5},{1,3},{0,1},{10,8},{12,10},{14... | collective-permute-start | bytes 786440 | tf_op jit(solution)/shard_map/ppermute | solution.py:308
  91.7 9.7 %collective-permute-start.22 = (bf16[2,64,1024]{2,1,0:T(8,128)(2,1)S(1)}, bf16[2,64,1024]{2,1,0:T(8,128)(2,1)S(1)}, u32[]{:S(2)}, u32[]{:S(2)}) collective-permute-start(bf16[2,64,1024]{2,1,0:T(8,128)(2,1)S(1)} %get-tuple-element.145.refs_6_.refs_0_), channel_id=1, source_target_pairs={{0,2},{2,4},{4,6},{6,7},{7,5},{5,3},{3,1},{1,0},{8,10},{10,12},{12... | collective-permute-start | bytes 786440 | tf_op jit(solution)/shard_map/ppermute | solution.py:308
  93.3 9.5 %collective-permute-start.23 = (bf16[2,64,1024]{2,1,0:T(8,128)(2,1)S(1)}, bf16[2,64,1024]{2,1,0:T(8,128)(2,1)S(1)}, u32[]{:S(2)}, u32[]{:S(2)}) collective-permute-start(bf16[2,64,1024]{2,1,0:T(8,128)(2,1)S(1)} %get-tuple-element.148), channel_id=1, source_target_pairs={{2,0},{4,2},{6,4},{7,6},{5,7},{3,5},{1,3},{0,1},{10,8},{12,10},{14... | collective-permute-start | bytes 786440 | tf_op jit(solution)/shard_map/ppermute | solution.py:308
  97.3 9.7 %collective-permute-start.28 = (bf16[2,64,1024]{2,1,0:T(8,128)(2,1)S(1)}, bf16[2,64,1024]{2,1,0:T(8,128)(2,1)S(1)}, u32[]{:S(2)}, u32[]{:S(2)}) collective-permute-start(bf16[2,64,1024]{2,1,0:T(8,128)(2,1)S(1)} %get-tuple-element.153.refs_0_), channel_id=1, source_target_pairs={{0,2},{2,4},{4,6},{6,7},{7,5},{5,3},{3,1},{1,0},{8,10},{10,12},{12... | collective-permute-start | bytes 786440 | tf_op jit(solution)/shard_map/ppermute | solution.py:308
  98.9 9.5 %collective-permute-start.29 = (bf16[2,64,1024]{2,1,0:T(8,128)(2,1)S(1)}, bf16[2,64,1024]{2,1,0:T(8,128)(2,1)S(1)}, u32[]{:S(2)}, u32[]{:S(2)}) collective-permute-start(bf16[2,64,1024]{2,1,0:T(8,128)(2,1)S(1)} %get-tuple-element.160), channel_id=1, source_target_pairs={{2,0},{4,2},{6,4},{7,6},{5,7},{3,5},{1,3},{0,1},{10,8},{12,10},{14... | collective-permute-start | bytes 786440 | tf_op jit(solution)/shard_map/ppermute | solution.py:308
  102.9 9.7 %collective-permute-start.26 = (bf16[2,64,1024]{2,1,0:T(8,128)(2,1)S(1)}, bf16[2,64,1024]{2,1,0:T(8,128)(2,1)S(1)}, u32[]{:S(2)}, u32[]{:S(2)}) collective-permute-start(bf16[2,64,1024]{2,1,0:T(8,128)(2,1)S(1)} %get-tuple-element.154.refs_6_.refs_0_), channel_id=1, source_target_pairs={{0,2},{2,4},{4,6},{6,7},{7,5},{5,3},{3,1},{1,0},{8,10},{10,12},{12... | collective-permute-start | bytes 786440 | tf_op jit(solution)/shard_map/ppermute | solution.py:308
  104.6 9.5 %collective-permute-start.27 = (bf16[2,64,1024]{2,1,0:T(8,128)(2,1)S(1)}, bf16[2,64,1024]{2,1,0:T(8,128)(2,1)S(1)}, u32[]{:S(2)}, u32[]{:S(2)}) collective-permute-start(bf16[2,64,1024]{2,1,0:T(8,128)(2,1)S(1)} %get-tuple-element.157), channel_id=1, source_target_pairs={{2,0},{4,2},{6,4},{7,6},{5,7},{3,5},{1,3},{0,1},{10,8},{12,10},{14... | collective-permute-start | bytes 786440 | tf_op jit(solution)/shard_map/ppermute | solution.py:308
  108.6 9.9 %collective-permute-start.31 = (bf16[2,64,1024]{2,1,0:T(8,128)(2,1)S(1)}, bf16[2,64,1024]{2,1,0:T(8,128)(2,1)S(1)}, u32[]{:S(2)}, u32[]{:S(2)}) collective-permute-start(bf16[2,64,1024]{2,1,0:T(8,128)(2,1)S(1)} %get-tuple-element.165), channel_id=1, source_target_pairs={{2,0},{4,2},{6,4},{7,6},{5,7},{3,5},{1,3},{0,1},{10,8},{12,10},{14... | collective-permute-start | bytes 786440 | tf_op jit(solution)/shard_map/ppermute | solution.py:308
  109.2 9.3 %collective-permute-start.32 = (bf16[2,64,1024]{2,1,0:T(8,128)(2,1)S(1)}, bf16[2,64,1024]{2,1,0:T(8,128)(2,1)S(1)}, u32[]{:S(2)}, u32[]{:S(2)}) collective-permute-start(bf16[2,64,1024]{2,1,0:T(8,128)(2,1)S(1)} %get-tuple-element.161.refs_0_), channel_id=1, source_target_pairs={{0,2},{2,4},{4,6},{6,7},{7,5},{5,3},{3,1},{1,0},{8,10},{10,12},{12... | collective-permute-start | bytes 786440 | tf_op jit(solution)/shard_map/ppermute | solution.py:308
  114.2 6.4 %collective-permute-start.30 = (bf16[2,64,1024]{2,1,0:T(8,128)(2,1)S(1)}, bf16[2,64,1024]{2,1,0:T(8,128)(2,1)S(1)}, u32[]{:S(2)}, u32[]{:S(2)}) collective-permute-start(bf16[2,64,1024]{2,1,0:T(8,128)(2,1)S(1)} %get-tuple-element.162.refs_6_), channel_id=1, source_target_pairs={{0,2},{2,4},{4,6},{6,7},{7,5},{5,3},{3,1},{1,0},{8,10},{10,12},{12... | collective-permute-start | bytes 786440 | tf_op jit(solution)/shard_map/ppermute | solution.py:308
  115.8 6.4 %collective-permute-start.33 = (bf16[2,64,1024]{2,1,0:T(8,128)(2,1)S(1)}, bf16[2,64,1024]{2,1,0:T(8,128)(2,1)S(1)}, u32[]{:S(2)}, u32[]{:S(2)}) collective-permute-start(bf16[2,64,1024]{2,1,0:T(8,128)(2,1)S(1)} %get-tuple-element.166), channel_id=1, source_target_pairs={{2,0},{4,2},{6,4},{7,6},{5,7},{3,5},{1,3},{0,1},{10,8},{12,10},{14... | collective-permute-start | bytes 786440 | tf_op jit(solution)/shard_map/ppermute | solution.py:308
  (5 other events, 8.4 us)

commit v6 on v5

--- a/solution.py
+++ b/solution.py
@@ -36,6 +36,31 @@
     at = lax.rem(place + (offset + replicas), replicas)
     owner = jnp.where(at < replicas // 2, 2 * at, 2 * (replicas - 1 - at) + 1)
     return pl.multiple_of(owner * part, part)
+
+
+def split_kernel(conv, mix, low, high, sems):
+    copies = [
+        pltpu.make_async_copy(conv.at[0:2], low, sems.at[0]),
+        pltpu.make_async_copy(conv.at[2], high.at[0], sems.at[1]),
+        pltpu.make_async_copy(mix.at[0], high.at[1], sems.at[2]),
+    ]
+    for copy in copies:
+        copy.start()
+    for copy in copies:
+        copy.wait()
+
+
+def split_call(conv, mix):
+    anywhere = pl.BlockSpec(memory_space=pl.ANY)
+    return pl.pallas_call(
+        split_kernel,
+        out_shape=[pltpu.VMEM((2, *conv.shape[1:]), BF16)] * 2,
+        in_specs=[anywhere] * 2,
+        out_specs=[VMEM] * 2,
+        scratch_shapes=[pltpu.SemaphoreType.DMA((3,))],
+        compiler_params=PARAMS,
+        cost_estimate=cost(0, 2**20),
+    )(*[pltpu.with_memory_space_constraint(array, pltpu.HBM) for array in (conv, mix)])
 
 
 def prepare_kernel(x, taps_t):
@@ -164,53 +189,71 @@
     )(*inputs)
 
 
-def chain_kernel(stage, index, g, skip, a1, a2, w, *refs):
-    pg, ig, gk, bt = refs[-4:]
+def chain_kernel(stage, index, halves, padding, before, held, g, skip, a1, a2, w, *refs):
+    bt = refs[-1]
+    carried = refs[0] if halves == (0,) else None
+    pg, ig, gk, *extra = refs[before + held : -1]
     samples, channels = gk.shape
     chunk = samples // 2
-    padding = bt.shape[1] - samples
+    base = min(halves) * chunk
+    count = len(halves) * chunk
     dilation = 2**stage
+    g_base = base if g.shape[0] == samples else 0
 
     @pl.when(lax.axis_index("pipe") == stage)
     def _():
         for k in (1, 2):
-            bt[k, samples:, :] = jnp.zeros((padding, channels), F32)
-        for at in (chunk, 0):
+            bt[k, count:, :] = jnp.zeros((padding, channels), F32) if carried is None else carried[k - 1]
+        for half in halves:
+            at = half * chunk
             rows = slice(at, at + chunk)
+            here = slice(at - base, at - base + chunk)
+            g_rows = slice(at - base + g_base, at - base + g_base + chunk)
             hid = lax.dot_general(
-                g[rows, :], w[3 * channels :, :channels], NT, preferred_element_type=F32
+                g[g_rows, :], w[3 * channels :, :channels], NT, preferred_element_type=F32
             ) + lax.dot_general(
                 skip[index, rows, :], w[3 * channels :, channels:], NT, preferred_element_type=F32
             )
             pg[rows, :channels] = (hid * a1[rows, :].astype(F32)).astype(BF16)
             pg[rows, channels:] = (hid * a2[rows, :].astype(F32)).astype(BF16)
             for k in range(3):
-                bt[k, rows, :] = lax.dot_general(
+                bt[k, here, :] = lax.dot_general(
                     pg[rows, :], w[k * channels : (k + 1) * channels, :], NT, preferred_element_type=F32
                 )
             piece = 64
-            for first in range(at + chunk - piece, at - 1, -piece):
+            for first in range(at - base + chunk - piece, at - base - 1, -piece):
                 last = first + piece
-                total = g[first:last, :].astype(F32) + bt[0, first:last, :]
+                total = g[first + g_base : last + g_base, :].astype(F32) + bt[0, first:last, :]
                 total = total + bt[1, first + dilation : last + dilation, :]
                 total = total + bt[2, first + 2 * dilation : last + 2 * dilation, :]
-                ig[first:last, :] = total.astype(BF16)
-            gk[rows, :] = g[rows, :]
-
-
-def chain_call(stage, index, padding, g, skip, a1, a2, w, held):
+                ig[first + base : last + base, :] = total.astype(BF16)
+                if extra:
+                    extra[0][first:last, :] = total.astype(BF16)
+            gk[rows, :] = g[g_rows, :]
+        if halves == (1,):
+            for k in (1, 2):
+                extra[1][k - 1] = bt[k, :padding, :]
+
+
+def chain_call(stage, index, halves, padding, g, skip, a1, a2, w, carried, held):
     samples, channels = a1.shape
+    chunk = samples // 2
     tile = pltpu.VMEM((samples, channels), BF16)
-    inputs = in_vmem(g, skip, a1, a2, w, *held)
-    return pl.pallas_call(
-        functools.partial(chain_kernel, stage, index),
-        out_shape=[pltpu.VMEM((samples, 2 * channels), BF16), tile, tile],
+    outs = [pltpu.VMEM((samples, 2 * channels), BF16), tile, tile]
+    if len(halves) == 1:
+        outs.append(pltpu.VMEM((chunk, channels), BF16))
+    if halves == (1,):
+        outs.append(pltpu.VMEM((2, padding, channels), F32))
+    inputs = in_vmem(g, skip, a1, a2, w, *carried, *held)
+    return pl.pallas_call(
+        functools.partial(chain_kernel, stage, index, halves, padding, len(carried), len(held)),
+        out_shape=outs,
         in_specs=[VMEM] * len(inputs),
-        out_specs=[VMEM] * 3,
-        scratch_shapes=[pltpu.VMEM((3, samples + padding, channels), F32)],
-        input_output_aliases={5 + i: i for i in range(len(held))},
-        compiler_params=PARAMS,
-        cost_estimate=cost(8 * samples * channels * channels, 2**22),
+        out_specs=[VMEM] * len(outs),
+        scratch_shapes=[pltpu.VMEM((3, len(halves) * chunk + padding, channels), F32)],
+        input_output_aliases={len(inputs) - len(held) + i: i for i in range(len(held))},
+        compiler_params=PARAMS,
+        cost_estimate=cost(8 * len(halves) * chunk * channels * channels, 2**22),
     )(*inputs)
 
 
@@ -308,9 +351,7 @@
         return lax.ppermute(to_right, "dp", right), lax.ppermute(to_left, "dp", left)
 
     taps_t = prepare_call(x_ckpt[0].reshape(micro * seqs, samples, channels))
-    conv = w_conv[0].transpose(1, 0, 2)
-    low = conv[:2]
-    high = jnp.concatenate([conv[2:], w_mix], axis=0)
+    low, high = split_call(w_conv[0].transpose(1, 0, 2), w_mix)
     streams = {0: (low, low), 2: (high, high)}
     held = partial_call(replicas, ((0, 0), (0, 2)), taps_t, [low, high], [])
     for step in range(1, half):
@@ -335,11 +376,22 @@
             w_full = stored[0]
         hid_t.append(hid)
         ready.append((a1, a2))
-    for stage in range(sections - 1, -1, -1):
+    last = sections - 1
+    g = [[piece, piece] for piece in g]
+    for m in range(micro):
+        held[m] = chain_call(last, m, (1, 0), padding, g[m][0], skip, *ready[m], w_full, (), ())
+        g[m] = [lax.ppermute(held[m][1], "pipe", [(last, last - 1)])] * 2
+    for stage in range(last - 1, -1, -1):
+        piece = None
         for m in range(micro):
-            held[m] = chain_call(stage, m, padding, g[m], skip, *ready[m], w_full, held[m])
-            if stage:
-                g[m] = lax.ppermute(held[m][1], "pipe", [(stage, stage - 1)])
+            carried = () if piece is None else (piece,)
+            for half_at in (1, 0):
+                out = chain_call(
+                    stage, m, (half_at,), padding, g[m][half_at], skip, *ready[m], w_full, carried, held[m]
+                )
+                held[m], piece, carried = out[:3], out[3], out[4:]
+                if stage:
+                    g[m][half_at] = lax.ppermute(piece, "pipe", [(stage, stage - 1)])
     pre_grads, cots, gs = zip(*held)
     cot = jnp.stack(cots, axis=0)
 

time: 124 us -> 121 us (0.976)
  waiting for transfers between devices: 58.3 us -> 51.2 us
  starting transfers between devices: 35.6 us -> 39.7 us
  Pallas kernels: 22.9 us -> 26.4 us
  local copies, waits for them, and re-layouts: 3.51 us -> 1.63 us
    ppermute x6 -> x10, waiting for transfers between devices: 17.8 us -> 7.98 us  [the longest x8 7.98 us: local(): g[m][half_at] = lax.ppermute(piece, 'pipe', [(stage, stage - 1)])]
    ppermute x6 -> x10, starting transfers between devices: 5.53 us -> 9.66 us  [the longest x8 8.1 us: local(): g[m][half_at] = lax.ppermute(piece, 'pipe', [(stage, stage - 1)])]
    pallas_call x8 -> x15, Pallas kernels: 5.89 us -> 9.42 us  [the longest x14 8.35 us: chain_call(): pl.pallas_call(functools.partial(chain_kernel, stage, index, halves, padd...]
    slice x2 -> x0, local copies, waits for them, and re-layouts: 1.88 us -> none  [the longest x1 0.97 us: local(): low = conv[:2]]
    ppermute x13, waiting for transfers between devices: 16.2 us -> 17.9 us  [send(): lax.ppermute(to_right, 'dp', right)]
  transfers between devices with their start and end apart: 34 -> 38, of which waited for: 28 -> 31; matrix products, arithmetic and copies ran while one was open for 2% -> 1% of each run, Pallas kernels for 13% -> 16%
where the time goes in v6:
time: 121 us
  waiting for transfers between devices  51.2 us (42%)
  starting transfers between devices  39.7 us (33%)
  Pallas kernels  26.4 us (22%)
  local copies, waits for them, and re-layouts  1.63 us (1%)
    ppermute x13, starting transfers between devices, send(): lax.ppermute(to_right, 'dp', right)  22.5 us
    ppermute x13, waiting for transfers between devices, send(): lax.ppermute(to_left, 'dp', left)  20.5 us
    ppermute x13, waiting for transfers between devices, send(): lax.ppermute(to_right, 'dp', right)  17.9 us
    pallas_call x14, Pallas kernels, chain_call(): pl.pallas_call(functools.partial(chain_kernel, stage, index, halves, padd...  8.35 us
    ppermute x8, starting transfers between devices, local(): g[m][half_at] = lax.ppermute(piece, 'pipe', [(stage, stage - 1)])  8.1 us
    ppermute x8, waiting for transfers between devices, local(): g[m][half_at] = lax.ppermute(piece, 'pipe', [(stage, stage - 1)])  7.98 us
    pallas_call x7, Pallas kernels, partial_call(): pl.pallas_call(functools.partial(partial_kernel, replicas, items, not hel...  6.61 us
    pallas_call x5, Pallas kernels, term_call(): pl.pallas_call(functools.partial(term_kernel, replicas, offsets, micro),...  5.58 us
  transfers between devices with their start and end apart: 38, of which 31 were waited for; matrix products, arithmetic and copies ran while one was open for 1% of the time, Pallas kernels for 16%

profile of v6, /device:TPU:0, one launch (start us, length us, event | category | flops | bytes accessed | tf_op | source)
XLA Modules:
  0.0 121.0 jit_solution(6289289809679371201)
XLA Ops:
  1.7 3.1 %collective-permute-start = (bf16[2,64,1024]{2,1,0:T(8,128)(2,1)S(1)}, bf16[2,64,1024]{2,1,0:T(8,128)(2,1)S(1)}, u32[]{:S(2)}, u32[]{:S(2)}) collective-permute-start(bf16[2,64,1024]{2,1,0:T(8,128)(2,1)S(1)} %get-tuple-element.121.refs_0_), channel_id=1, source_target_pairs={{0,2},{2,4},{4,6},{6,7},{7,5},{5,3},{3,1},{1,0},{8,10},{10,12},{12... | collective-permute-start | bytes 786440 | tf_op jit(solution)/shard_map/ppermute | solution.py:351
  4.8 2.0 %collective-permute-start.4 = (bf16[2,64,1024]{2,1,0:T(8,128)(2,1)S(1)}, bf16[2,64,1024]{2,1,0:T(8,128)(2,1)S(1)}, u32[]{:S(2)}, u32[]{:S(2)}) collective-permute-start(bf16[2,64,1024]{2,1,0:T(8,128)(2,1)S(1)} %get-tuple-element.122.refs_1_), channel_id=1, source_target_pairs={{0,2},{2,4},{4,6},{6,7},{7,5},{5,3},{3,1},{1,0},{8,10},{10,12},{12... | collective-permute-start | bytes 786440 | tf_op jit(solution)/shard_map/ppermute | solution.py:351
  10.2 1.7 %collective-permute-done.refs_0_ = bf16[2,64,1024]{2,1,0:T(8,128)(2,1)S(1)} collective-permute-done((bf16[2,64,1024]{2,1,0:T(8,128)(2,1)S(1)}, bf16[2,64,1024]{2,1,0:T(8,128)(2,1)S(1)}, u32[]{:S(2)}, u32[]{:S(2)}) %collective-permute-start) | collective-permute-done | bytes 262176 | tf_op jit(solution)/shard_map/ppermute | solution.py:351
  11.9 2.2 %collective-permute-done.1.refs_1_ = bf16[2,64,1024]{2,1,0:T(8,128)(2,1)S(1)} collective-permute-done((bf16[2,64,1024]{2,1,0:T(8,128)(2,1)S(1)}, bf16[2,64,1024]{2,1,0:T(8,128)(2,1)S(1)}, u32[]{:S(2)}, u32[]{:S(2)}) %collective-permute-start.1) | collective-permute-done | bytes 262176 | tf_op jit(solution)/shard_map/ppermute | solution.py:351
  15.0 1.6 %collective-permute-start.2 = (bf16[2,64,1024]{2,1,0:T(8,128)(2,1)S(1)}, bf16[2,64,1024]{2,1,0:T(8,128)(2,1)S(1)}, u32[]{:S(2)}, u32[]{:S(2)}) collective-permute-start(bf16[2,64,1024]{2,1,0:T(8,128)(2,1)S(1)} %get-tuple-element.125), channel_id=1, source_target_pairs={{0,2},{2,4},{4,6},{6,7},{7,5},{5,3},{3,1},{1,0},{8,10},{10,12},{12... | collective-permute-start | bytes 786440 | tf_op jit(solution)/shard_map/ppermute | solution.py:351
  17.5 2.2 %collective-permute-done.5.refs_1_ = bf16[2,64,1024]{2,1,0:T(8,128)(2,1)S(1)} collective-permute-done((bf16[2,64,1024]{2,1,0:T(8,128)(2,1)S(1)}, bf16[2,64,1024]{2,1,0:T(8,128)(2,1)S(1)}, u32[]{:S(2)}, u32[]{:S(2)}) %collective-permute-start.5) | collective-permute-done | bytes 262176 | tf_op jit(solution)/shard_map/ppermute | solution.py:351
  20.6 1.6 %collective-permute-start.8 = (bf16[2,64,1024]{2,1,0:T(8,128)(2,1)S(1)}, bf16[2,64,1024]{2,1,0:T(8,128)(2,1)S(1)}, u32[]{:S(2)}, u32[]{:S(2)}) collective-permute-start(bf16[2,64,1024]{2,1,0:T(8,128)(2,1)S(1)} %get-tuple-element.133), channel_id=1, source_target_pairs={{0,2},{2,4},{4,6},{6,7},{7,5},{5,3},{3,1},{1,0},{8,10},{10,12},{12... | collective-permute-start | bytes 786440 | tf_op jit(solution)/shard_map/ppermute | solution.py:351
  24.1 1.7 %collective-permute-done.3.refs_1_ = bf16[2,64,1024]{2,1,0:T(8,128)(2,1)S(1)} collective-permute-done((bf16[2,64,1024]{2,1,0:T(8,128)(2,1)S(1)}, bf16[2,64,1024]{2,1,0:T(8,128)(2,1)S(1)}, u32[]{:S(2)}, u32[]{:S(2)}) %collective-permute-start.3) | collective-permute-done | bytes 262176 | tf_op jit(solution)/shard_map/ppermute | solution.py:351
  26.8 1.6 %collective-permute-start.6 = (bf16[2,64,1024]{2,1,0:T(8,128)(2,1)S(1)}, bf16[2,64,1024]{2,1,0:T(8,128)(2,1)S(1)}, u32[]{:S(2)}, u32[]{:S(2)}) collective-permute-start(bf16[2,64,1024]{2,1,0:T(8,128)(2,1)S(1)} %get-tuple-element.131), channel_id=1, source_target_pairs={{0,2},{2,4},{4,6},{6,7},{7,5},{5,3},{3,1},{1,0},{8,10},{10,12},{12... | collective-permute-start | bytes 786440 | tf_op jit(solution)/shard_map/ppermute | solution.py:351
  29.9 1.5 %collective-permute-done.9.refs_1_ = bf16[2,64,1024]{2,1,0:T(8,128)(2,1)S(1)} collective-permute-done((bf16[2,64,1024]{2,1,0:T(8,128)(2,1)S(1)}, bf16[2,64,1024]{2,1,0:T(8,128)(2,1)S(1)}, u32[]{:S(2)}, u32[]{:S(2)}) %collective-permute-start.9) | collective-permute-done | bytes 262176 | tf_op jit(solution)/shard_map/ppermute | solution.py:351
  32.4 1.6 %collective-permute-start.11 = (bf16[2,64,1024]{2,1,0:T(8,128)(2,1)S(1)}, bf16[2,64,1024]{2,1,0:T(8,128)(2,1)S(1)}, u32[]{:S(2)}, u32[]{:S(2)}) collective-permute-start(bf16[2,64,1024]{2,1,0:T(8,128)(2,1)S(1)} %get-tuple-element.140), channel_id=1, source_target_pairs={{0,2},{2,4},{4,6},{6,7},{7,5},{5,3},{3,1},{1,0},{8,10},{10,12},{12... | collective-permute-start | bytes 786440 | tf_op jit(solution)/shard_map/ppermute | solution.py:351
  34.4 1.5 %collective-permute-done.6.refs_0_ = bf16[2,64,1024]{2,1,0:T(8,128)(2,1)S(1)} collective-permute-done((bf16[2,64,1024]{2,1,0:T(8,128)(2,1)S(1)}, bf16[2,64,1024]{2,1,0:T(8,128)(2,1)S(1)}, u32[]{:S(2)}, u32[]{:S(2)}) %collective-permute-start.6) | collective-permute-done | bytes 262176 | tf_op jit(solution)/shard_map/ppermute | solution.py:351
  35.9 1.7 %collective-permute-done.7.refs_1_ = bf16[2,64,1024]{2,1,0:T(8,128)(2,1)S(1)} collective-permute-done((bf16[2,64,1024]{2,1,0:T(8,128)(2,1)S(1)}, bf16[2,64,1024]{2,1,0:T(8,128)(2,1)S(1)}, u32[]{:S(2)}, u32[]{:S(2)}) %collective-permute-start.7) | collective-permute-done | bytes 262176 | tf_op jit(solution)/shard_map/ppermute | solution.py:351
  39.1 1.5 %collective-permute-done.12.refs_1_ = bf16[2,64,1024]{2,1,0:T(8,128)(2,1)S(1)} collective-permute-done((bf16[2,64,1024]{2,1,0:T(8,128)(2,1)S(1)}, bf16[2,64,1024]{2,1,0:T(8,128)(2,1)S(1)}, u32[]{:S(2)}, u32[]{:S(2)}) %collective-permute-start.12) | collective-permute-done | bytes 262176 | tf_op jit(solution)/shard_map/ppermute | solution.py:351
  41.9 1.7 %collective-permute-start.10 = (bf16[2,64,1024]{2,1,0:T(8,128)(2,1)S(1)}, bf16[2,64,1024]{2,1,0:T(8,128)(2,1)S(1)}, u32[]{:S(2)}, u32[]{:S(2)}) collective-permute-start(bf16[2,64,1024]{2,1,0:T(8,128)(2,1)S(1)} %get-tuple-element.139), channel_id=1, source_target_pairs={{0,2},{2,4},{4,6},{6,7},{7,5},{5,3},{3,1},{1,0},{8,10},{10,12},{12... | collective-permute-start | bytes 786440 | tf_op jit(solution)/shard_map/ppermute | solution.py:364
  43.8 4.3 %collective-permute-done.13.high = bf16[2,64,1024]{2,1,0:T(8,128)(2,1)S(1)} collective-permute-done((bf16[2,64,1024]{2,1,0:T(8,128)(2,1)S(1)}, bf16[2,64,1024]{2,1,0:T(8,128)(2,1)S(1)}, u32[]{:S(2)}, u32[]{:S(2)}) %collective-permute-start.13) | collective-permute-done | bytes 262176 | tf_op jit(solution)/shard_map/ppermute | solution.py:365
  57.9 1.5 %collective-permute-start.23 = (bf16[256,512]{1,0:T(8,128)(2,1)S(1)}, bf16[256,512]{1,0:T(8,128)(2,1)S(1)}, u32[]{:S(2)}, u32[]{:S(2)}) collective-permute-start(bf16[256,512]{1,0:T(8,128)(2,1)S(1)} %get-tuple-element.195), channel_id=1, source_target_pairs={{8,0},{9,1},{10,2},{11,3},{12,4},{13,5},{14,6},{15,7}} | collective-permute-start | bytes 786440 | tf_op jit(solution)/shard_map/ppermute | solution.py:394
  60.8 5.1 %collective-permute-done.18.g = bf16[256,512]{1,0:T(8,128)(2,1)S(1)} collective-permute-done((bf16[256,512]{1,0:T(8,128)(2,1)S(1)}, bf16[256,512]{1,0:T(8,128)(2,1)S(1)}, u32[]{:S(2)}, u32[]{:S(2)}) %collective-permute-start.18) | collective-permute-done | bytes 262176 | tf_op jit(solution)/shard_map/ppermute | solution.py:394
  65.9 2.2 %shard_map.91 = (bf16[512,1024]{1,0:T(8,128)(2,1)S(1)}, bf16[512,512]{1,0:T(8,128)(2,1)S(1)}, bf16[512,512]{1,0:T(8,128)(2,1)S(1)}, bf16[256,512]{1,0:T(8,128)(2,1)}, f32[2,16,512]{2,1,0:T(8,128)S(1)}) custom-call(bf16[256,512]{1,0:T(8,128)(2,1)S(1)} %collective-permute-done.18.g, ...), custom_call_target="tpu_custom_call", output_to_operand_aliasing={{0}: (5, {}), {1}: (6, {}), {2}: (7, {})} | custom-call | flops 536870912 | bytes 4194304 | tf_op jit(solution)/shard_map/pallas_call | solution.py:248
  68.7 1.5 %shard_map.92 = (bf16[512,1024]{1,0:T(8,128)(2,1)S(1)}, bf16[512,512]{1,0:T(8,128)(2,1)S(1)}, bf16[512,512]{1,0:T(8,128)(2,1)S(1)}, bf16[256,512]{1,0:T(8,128)(2,1)S(1)}) custom-call(bf16[256,512]{1,0:T(8,128)(2,1)S(1)} %collective-permute-done.17.g, bf16[2,512,512]{2,1,0:T(8,128)(2,1)S(1)} %bitcast.30, ...), custom_call_target="tpu_custom_call", output_to_operand_aliasing={{0}: (6, {}), {1}: (7, {}), {2}: (8, {})} | custom-call | flops 536870912 | bytes 4194304 | tf_op jit(solution)/shard_map/pallas_call | solution.py:248
  71.6 2.2 %shard_map.99 = (bf16[512,1024]{1,0:T(8,128)(2,1)S(1)}, bf16[512,512]{1,0:T(8,128)(2,1)S(1)}, bf16[512,512]{1,0:T(8,128)(2,1)S(1)}, bf16[256,512]{1,0:T(8,128)(2,1)}, f32[2,16,512]{2,1,0:T(8,128)S(1)}) custom-call(bf16[256,512]{1,0:T(8,128)(2,1)S(1)} %collective-permute-done.23.g, ...), custom_call_target="tpu_custom_call", output_to_operand_aliasing={{0}: (6, {}), {1}: (7, {}), {2}: (8, {})} | custom-call | flops 536870912 | bytes 4194304 | tf_op jit(solution)/shard_map/pallas_call | solution.py:248
  74.7 2.2 %shard_map.100 = (bf16[512,1024]{1,0:T(8,128)(2,1)S(1)}, bf16[512,512]{1,0:T(8,128)(2,1)S(1)}, bf16[512,512]{1,0:T(8,128)(2,1)S(1)}, bf16[256,512]{1,0:T(8,128)(2,1)}) custom-call(bf16[256,512]{1,0:T(8,128)(2,1)S(1)} %collective-permute-done.22.g, bf16[2,512,512]{2,1,0:T(8,128)(2,1)S(1)} %bitcast.32, ...), custom_call_target="tpu_custom_call", output_to_operand_aliasing={{0}: (6, {}), {1}: (7, {}), {2}: (8, {})} | custom-call | flops 536870912 | bytes 4194304 | tf_op jit(solution)/shard_map/pallas_call | solution.py:248
  77.8 1.5 %collective-permute-start.24 = (bf16[2,64,1024]{2,1,0:T(8,128)(2,1)S(1)}, bf16[2,64,1024]{2,1,0:T(8,128)(2,1)S(1)}, u32[]{:S(2)}, u32[]{:S(2)}) collective-permute-start(bf16[2,64,1024]{2,1,0:T(8,128)(2,1)S(1)} %get-tuple-element.211.refs_6_), channel_id=1, source_target_pairs={{0,2},{2,4},{4,6},{6,7},{7,5},{5,3},{3,1},{1,0},{8,10},{10,12},{12... | collective-permute-start | bytes 786440 | tf_op jit(solution)/shard_map/ppermute | solution.py:351
  81.2 1.5 %collective-permute-start.28 = (bf16[2,64,1024]{2,1,0:T(8,128)(2,1)S(1)}, bf16[2,64,1024]{2,1,0:T(8,128)(2,1)S(1)}, u32[]{:S(2)}, u32[]{:S(2)}) collective-permute-start(bf16[2,64,1024]{2,1,0:T(8,128)(2,1)S(1)} %get-tuple-element.221), channel_id=1, source_target_pairs={{0,2},{2,4},{4,6},{6,7},{7,5},{5,3},{3,1},{1,0},{8,10},{10,12},{12... | collective-permute-start | bytes 786440 | tf_op jit(solution)/shard_map/ppermute | solution.py:351
  83.2 3.9 %collective-permute-done.24.got_r = bf16[2,64,1024]{2,1,0:T(8,128)(2,1)S(1)} collective-permute-done((bf16[2,64,1024]{2,1,0:T(8,128)(2,1)S(1)}, bf16[2,64,1024]{2,1,0:T(8,128)(2,1)S(1)}, u32[]{:S(2)}, u32[]{:S(2)}) %collective-permute-start.24) | collective-permute-done | bytes 262176 | tf_op jit(solution)/shard_map/ppermute | solution.py:351
  88.7 1.6 %collective-permute-start.26 = (bf16[2,64,1024]{2,1,0:T(8,128)(2,1)S(1)}, bf16[2,64,1024]{2,1,0:T(8,128)(2,1)S(1)}, u32[]{:S(2)}, u32[]{:S(2)}) collective-permute-start(bf16[2,64,1024]{2,1,0:T(8,128)(2,1)S(1)} %get-tuple-element.215.refs_6_.refs_0_), channel_id=1, source_target_pairs={{0,2},{2,4},{4,6},{6,7},{7,5},{5,3},{3,1},{1,0},{8,10},{10,12},{12... | collective-permute-start | bytes 786440 | tf_op jit(solution)/shard_map/ppermute | solution.py:351
  94.3 1.6 %collective-permute-start.32 = (bf16[2,64,1024]{2,1,0:T(8,128)(2,1)S(1)}, bf16[2,64,1024]{2,1,0:T(8,128)(2,1)S(1)}, u32[]{:S(2)}, u32[]{:S(2)}) collective-permute-start(bf16[2,64,1024]{2,1,0:T(8,128)(2,1)S(1)} %get-tuple-element.223.refs_0_), channel_id=1, source_target_pairs={{0,2},{2,4},{4,6},{6,7},{7,5},{5,3},{3,1},{1,0},{8,10},{10,12},{12... | collective-permute-start | bytes 786440 | tf_op jit(solution)/shard_map/ppermute | solution.py:351
  96.4 2.0 %collective-permute-done.26.got_r = bf16[2,64,1024]{2,1,0:T(8,128)(2,1)S(1)} collective-permute-done((bf16[2,64,1024]{2,1,0:T(8,128)(2,1)S(1)}, bf16[2,64,1024]{2,1,0:T(8,128)(2,1)S(1)}, u32[]{:S(2)}, u32[]{:S(2)}) %collective-permute-start.26) | collective-permute-done | bytes 262176 | tf_op jit(solution)/shard_map/ppermute | solution.py:351
  99.9 1.6 %collective-permute-start.30 = (bf16[2,64,1024]{2,1,0:T(8,128)(2,1)S(1)}, bf16[2,64,1024]{2,1,0:T(8,128)(2,1)S(1)}, u32[]{:S(2)}, u32[]{:S(2)}) collective-permute-start(bf16[2,64,1024]{2,1,0:T(8,128)(2,1)S(1)} %get-tuple-element.224.refs_6_.refs_0_), channel_id=1, source_target_pairs={{0,2},{2,4},{4,6},{6,7},{7,5},{5,3},{3,1},{1,0},{8,10},{10,12},{12... | collective-permute-start | bytes 786440 | tf_op jit(solution)/shard_map/ppermute | solution.py:351
  107.6 2.0 %collective-permute-done.30.got_r = bf16[2,64,1024]{2,1,0:T(8,128)(2,1)S(1)} collective-permute-done((bf16[2,64,1024]{2,1,0:T(8,128)(2,1)S(1)}, bf16[2,64,1024]{2,1,0:T(8,128)(2,1)S(1)}, u32[]{:S(2)}, u32[]{:S(2)}) %collective-permute-start.30) | collective-permute-done | bytes 262176 | tf_op jit(solution)/shard_map/ppermute | solution.py:351
  111.2 1.6 %collective-permute-start.34 = (bf16[2,64,1024]{2,1,0:T(8,128)(2,1)S(1)}, bf16[2,64,1024]{2,1,0:T(8,128)(2,1)S(1)}, u32[]{:S(2)}, u32[]{:S(2)}) collective-permute-start(bf16[2,64,1024]{2,1,0:T(8,128)(2,1)S(1)} %get-tuple-element.232.refs_6_), channel_id=1, source_target_pairs={{0,2},{2,4},{4,6},{6,7},{7,5},{5,3},{3,1},{1,0},{8,10},{10,12},{12... | collective-permute-start | bytes 786440 | tf_op jit(solution)/shard_map/ppermute | solution.py:351
  116.7 2.1 %collective-permute-done.34.low_r = bf16[2,64,1024]{2,1,0:T(8,128)(2,1)S(1)} collective-permute-done((bf16[2,64,1024]{2,1,0:T(8,128)(2,1)S(1)}, bf16[2,64,1024]{2,1,0:T(8,128)(2,1)S(1)}, u32[]{:S(2)}, u32[]{:S(2)}) %collective-permute-start.34) | collective-permute-done | bytes 262176 | tf_op jit(solution)/shard_map/ppermute | solution.py:351
  (88 shorter events, 54.1 us)
Async XLA Ops:
  1.7 10.2 %collective-permute-start = (bf16[2,64,1024]{2,1,0:T(8,128)(2,1)S(1)}, bf16[2,64,1024]{2,1,0:T(8,128)(2,1)S(1)}, u32[]{:S(2)}, u32[]{:S(2)}) collective-permute-start(bf16[2,64,1024]{2,1,0:T(8,128)(2,1)S(1)} %get-tuple-element.121.refs_0_), channel_id=1, source_target_pairs={{0,2},{2,4},{4,6},{6,7},{7,5},{5,3},{3,1},{1,0},{8,10},{10,12},{12... | collective-permute-start | bytes 786440 | tf_op jit(solution)/shard_map/ppermute | solution.py:351
  4.8 9.2 %collective-permute-start.1 = (bf16[2,64,1024]{2,1,0:T(8,128)(2,1)S(1)}, bf16[2,64,1024]{2,1,0:T(8,128)(2,1)S(1)}, u32[]{:S(2)}, u32[]{:S(2)}) collective-permute-start(bf16[2,64,1024]{2,1,0:T(8,128)(2,1)S(1)} %get-tuple-element.121.refs_0_), channel_id=1, source_target_pairs={{2,0},{4,2},{6,4},{7,6},{5,7},{3,5},{1,3},{0,1},{10,8},{12,10},{14... | collective-permute-start | bytes 786440 | tf_op jit(solution)/shard_map/ppermute | solution.py:351
  4.8 12.7 %collective-permute-start.4 = (bf16[2,64,1024]{2,1,0:T(8,128)(2,1)S(1)}, bf16[2,64,1024]{2,1,0:T(8,128)(2,1)S(1)}, u32[]{:S(2)}, u32[]{:S(2)}) collective-permute-start(bf16[2,64,1024]{2,1,0:T(8,128)(2,1)S(1)} %get-tuple-element.122.refs_1_), channel_id=1, source_target_pairs={{0,2},{2,4},{4,6},{6,7},{7,5},{5,3},{3,1},{1,0},{8,10},{10,12},{12... | collective-permute-start | bytes 786440 | tf_op jit(solution)/shard_map/ppermute | solution.py:351
  6.8 12.8 %collective-permute-start.5 = (bf16[2,64,1024]{2,1,0:T(8,128)(2,1)S(1)}, bf16[2,64,1024]{2,1,0:T(8,128)(2,1)S(1)}, u32[]{:S(2)}, u32[]{:S(2)}) collective-permute-start(bf16[2,64,1024]{2,1,0:T(8,128)(2,1)S(1)} %get-tuple-element.122.refs_1_), channel_id=1, source_target_pairs={{2,0},{4,2},{6,4},{7,6},{5,7},{3,5},{1,3},{0,1},{10,8},{12,10},{14... | collective-permute-start | bytes 786440 | tf_op jit(solution)/shard_map/ppermute | solution.py:351
  15.0 9.0 %collective-permute-start.2 = (bf16[2,64,1024]{2,1,0:T(8,128)(2,1)S(1)}, bf16[2,64,1024]{2,1,0:T(8,128)(2,1)S(1)}, u32[]{:S(2)}, u32[]{:S(2)}) collective-permute-start(bf16[2,64,1024]{2,1,0:T(8,128)(2,1)S(1)} %get-tuple-element.125), channel_id=1, source_target_pairs={{0,2},{2,4},{4,6},{6,7},{7,5},{5,3},{3,1},{1,0},{8,10},{10,12},{12... | collective-permute-start | bytes 786440 | tf_op jit(solution)/shard_map/ppermute | solution.py:351
  16.6 9.2 %collective-permute-start.3 = (bf16[2,64,1024]{2,1,0:T(8,128)(2,1)S(1)}, bf16[2,64,1024]{2,1,0:T(8,128)(2,1)S(1)}, u32[]{:S(2)}, u32[]{:S(2)}) collective-permute-start(bf16[2,64,1024]{2,1,0:T(8,128)(2,1)S(1)} %get-tuple-element.126), channel_id=1, source_target_pairs={{2,0},{4,2},{6,4},{7,6},{5,7},{3,5},{1,3},{0,1},{10,8},{12,10},{14... | collective-permute-start | bytes 786440 | tf_op jit(solution)/shard_map/ppermute | solution.py:351
  20.6 9.3 %collective-permute-start.8 = (bf16[2,64,1024]{2,1,0:T(8,128)(2,1)S(1)}, bf16[2,64,1024]{2,1,0:T(8,128)(2,1)S(1)}, u32[]{:S(2)}, u32[]{:S(2)}) collective-permute-start(bf16[2,64,1024]{2,1,0:T(8,128)(2,1)S(1)} %get-tuple-element.133), channel_id=1, source_target_pairs={{0,2},{2,4},{4,6},{6,7},{7,5},{5,3},{3,1},{1,0},{8,10},{10,12},{12... | collective-permute-start | bytes 786440 | tf_op jit(solution)/shard_map/ppermute | solution.py:351
  22.2 9.2 %collective-permute-start.9 = (bf16[2,64,1024]{2,1,0:T(8,128)(2,1)S(1)}, bf16[2,64,1024]{2,1,0:T(8,128)(2,1)S(1)}, u32[]{:S(2)}, u32[]{:S(2)}) collective-permute-start(bf16[2,64,1024]{2,1,0:T(8,128)(2,1)S(1)} %get-tuple-element.134), channel_id=1, source_target_pairs={{2,0},{4,2},{6,4},{7,6},{5,7},{3,5},{1,3},{0,1},{10,8},{12,10},{14... | collective-permute-start | bytes 786440 | tf_op jit(solution)/shard_map/ppermute | solution.py:351
  26.8 9.1 %collective-permute-start.6 = (bf16[2,64,1024]{2,1,0:T(8,128)(2,1)S(1)}, bf16[2,64,1024]{2,1,0:T(8,128)(2,1)S(1)}, u32[]{:S(2)}, u32[]{:S(2)}) collective-permute-start(bf16[2,64,1024]{2,1,0:T(8,128)(2,1)S(1)} %get-tuple-element.131), channel_id=1, source_target_pairs={{0,2},{2,4},{4,6},{6,7},{7,5},{5,3},{3,1},{1,0},{8,10},{10,12},{12... | collective-permute-start | bytes 786440 | tf_op jit(solution)/shard_map/ppermute | solution.py:351
  28.4 9.2 %collective-permute-start.7 = (bf16[2,64,1024]{2,1,0:T(8,128)(2,1)S(1)}, bf16[2,64,1024]{2,1,0:T(8,128)(2,1)S(1)}, u32[]{:S(2)}, u32[]{:S(2)}) collective-permute-start(bf16[2,64,1024]{2,1,0:T(8,128)(2,1)S(1)} %get-tuple-element.132), channel_id=1, source_target_pairs={{2,0},{4,2},{6,4},{7,6},{5,7},{3,5},{1,3},{0,1},{10,8},{12,10},{14... | collective-permute-start | bytes 786440 | tf_op jit(solution)/shard_map/ppermute | solution.py:351
  32.4 6.8 %collective-permute-start.11 = (bf16[2,64,1024]{2,1,0:T(8,128)(2,1)S(1)}, bf16[2,64,1024]{2,1,0:T(8,128)(2,1)S(1)}, u32[]{:S(2)}, u32[]{:S(2)}) collective-permute-start(bf16[2,64,1024]{2,1,0:T(8,128)(2,1)S(1)} %get-tuple-element.140), channel_id=1, source_target_pairs={{0,2},{2,4},{4,6},{6,7},{7,5},{5,3},{3,1},{1,0},{8,10},{10,12},{12... | collective-permute-start | bytes 786440 | tf_op jit(solution)/shard_map/ppermute | solution.py:351
  34.0 6.6 %collective-permute-start.12 = (bf16[2,64,1024]{2,1,0:T(8,128)(2,1)S(1)}, bf16[2,64,1024]{2,1,0:T(8,128)(2,1)S(1)}, u32[]{:S(2)}, u32[]{:S(2)}) collective-permute-start(bf16[2,64,1024]{2,1,0:T(8,128)(2,1)S(1)} %get-tuple-element.141), channel_id=1, source_target_pairs={{2,0},{4,2},{6,4},{7,6},{5,7},{3,5},{1,3},{0,1},{10,8},{12,10},{14... | collective-permute-start | bytes 786440 | tf_op jit(solution)/shard_map/ppermute | solution.py:351
  41.6 6.4 %collective-permute-start.13 = (bf16[2,64,1024]{2,1,0:T(8,128)(2,1)S(1)}, bf16[2,64,1024]{2,1,0:T(8,128)(2,1)S(1)}, u32[]{:S(2)}, u32[]{:S(2)}) collective-permute-start(bf16[2,64,1024]{2,1,0:T(8,128)(2,1)S(1)} %get-tuple-element.144), channel_id=1, source_target_pairs={{2,0},{4,2},{6,4},{7,6},{5,7},{3,5},{1,3},{0,1},{10,8},{12,10},{14... | collective-permute-start | bytes 786440 | tf_op jit(solution)/shard_map/ppermute | solution.py:365
  41.9 6.7 %collective-permute-start.10 = (bf16[2,64,1024]{2,1,0:T(8,128)(2,1)S(1)}, bf16[2,64,1024]{2,1,0:T(8,128)(2,1)S(1)}, u32[]{:S(2)}, u32[]{:S(2)}) collective-permute-start(bf16[2,64,1024]{2,1,0:T(8,128)(2,1)S(1)} %get-tuple-element.139), channel_id=1, source_target_pairs={{0,2},{2,4},{4,6},{6,7},{7,5},{5,3},{3,1},{1,0},{8,10},{10,12},{12... | collective-permute-start | bytes 786440 | tf_op jit(solution)/shard_map/ppermute | solution.py:364
  55.2 10.7 %collective-permute-start.18 = (bf16[256,512]{1,0:T(8,128)(2,1)S(1)}, bf16[256,512]{1,0:T(8,128)(2,1)S(1)}, u32[]{:S(2)}, u32[]{:S(2)}) collective-permute-start(bf16[256,512]{1,0:T(8,128)(2,1)S(1)} %get-tuple-element.167), channel_id=1, source_target_pairs={{8,0},{9,1},{10,2},{11,3},{12,4},{13,5},{14,6},{15,7}} | collective-permute-start | bytes 786440 | tf_op jit(solution)/shard_map/ppermute | solution.py:394
  56.6 12.2 %collective-permute-start.17 = (bf16[256,512]{1,0:T(8,128)(2,1)S(1)}, bf16[256,512]{1,0:T(8,128)(2,1)S(1)}, u32[]{:S(2)}, u32[]{:S(2)}) collective-permute-start(bf16[256,512]{1,0:T(8,128)(2,1)S(1)} %get-tuple-element.166.refs_0_), channel_id=1, source_target_pairs={{8,0},{9,1},{10,2},{11,3},{12,4},{13,5},{14,6},{15,7}} | collective-permute-start | bytes 786440 | tf_op jit(solution)/shard_map/ppermute | solution.py:394
  57.9 13.7 %collective-permute-start.23 = (bf16[256,512]{1,0:T(8,128)(2,1)S(1)}, bf16[256,512]{1,0:T(8,128)(2,1)S(1)}, u32[]{:S(2)}, u32[]{:S(2)}) collective-permute-start(bf16[256,512]{1,0:T(8,128)(2,1)S(1)} %get-tuple-element.195), channel_id=1, source_target_pairs={{8,0},{9,1},{10,2},{11,3},{12,4},{13,5},{14,6},{15,7}} | collective-permute-start | bytes 786440 | tf_op jit(solution)/shard_map/ppermute | solution.py:394
  59.5 15.2 %collective-permute-start.22 = (bf16[256,512]{1,0:T(8,128)(2,1)S(1)}, bf16[256,512]{1,0:T(8,128)(2,1)S(1)}, u32[]{:S(2)}, u32[]{:S(2)}) collective-permute-start(bf16[256,512]{1,0:T(8,128)(2,1)S(1)} %get-tuple-element.194), channel_id=1, source_target_pairs={{8,0},{9,1},{10,2},{11,3},{12,4},{13,5},{14,6},{15,7}} | collective-permute-start | bytes 786440 | tf_op jit(solution)/shard_map/ppermute | solution.py:394
  77.8 9.3 %collective-permute-start.24 = (bf16[2,64,1024]{2,1,0:T(8,128)(2,1)S(1)}, bf16[2,64,1024]{2,1,0:T(8,128)(2,1)S(1)}, u32[]{:S(2)}, u32[]{:S(2)}) collective-permute-start(bf16[2,64,1024]{2,1,0:T(8,128)(2,1)S(1)} %get-tuple-element.211.refs_6_), channel_id=1, source_target_pairs={{0,2},{2,4},{4,6},{6,7},{7,5},{5,3},{3,1},{1,0},{8,10},{10,12},{12... | collective-permute-start | bytes 786440 | tf_op jit(solution)/shard_map/ppermute | solution.py:351
  79.3 9.2 %collective-permute-start.25 = (bf16[2,64,1024]{2,1,0:T(8,128)(2,1)S(1)}, bf16[2,64,1024]{2,1,0:T(8,128)(2,1)S(1)}, u32[]{:S(2)}, u32[]{:S(2)}) collective-permute-start(bf16[2,64,1024]{2,1,0:T(8,128)(2,1)S(1)} %get-tuple-element.214), channel_id=1, source_target_pairs={{2,0},{4,2},{6,4},{7,6},{5,7},{3,5},{1,3},{0,1},{10,8},{12,10},{14... | collective-permute-start | bytes 786440 | tf_op jit(solution)/shard_map/ppermute | solution.py:351
  81.2 11.6 %collective-permute-start.28 = (bf16[2,64,1024]{2,1,0:T(8,128)(2,1)S(1)}, bf16[2,64,1024]{2,1,0:T(8,128)(2,1)S(1)}, u32[]{:S(2)}, u32[]{:S(2)}) collective-permute-start(bf16[2,64,1024]{2,1,0:T(8,128)(2,1)S(1)} %get-tuple-element.221), channel_id=1, source_target_pairs={{0,2},{2,4},{4,6},{6,7},{7,5},{5,3},{3,1},{1,0},{8,10},{10,12},{12... | collective-permute-start | bytes 786440 | tf_op jit(solution)/shard_map/ppermute | solution.py:351
  82.6 11.5 %collective-permute-start.29 = (bf16[2,64,1024]{2,1,0:T(8,128)(2,1)S(1)}, bf16[2,64,1024]{2,1,0:T(8,128)(2,1)S(1)}, u32[]{:S(2)}, u32[]{:S(2)}) collective-permute-start(bf16[2,64,1024]{2,1,0:T(8,128)(2,1)S(1)} %get-tuple-element.222), channel_id=1, source_target_pairs={{2,0},{4,2},{6,4},{7,6},{5,7},{3,5},{1,3},{0,1},{10,8},{12,10},{14... | collective-permute-start | bytes 786440 | tf_op jit(solution)/shard_map/ppermute | solution.py:351
  88.7 9.7 %collective-permute-start.26 = (bf16[2,64,1024]{2,1,0:T(8,128)(2,1)S(1)}, bf16[2,64,1024]{2,1,0:T(8,128)(2,1)S(1)}, u32[]{:S(2)}, u32[]{:S(2)}) collective-permute-start(bf16[2,64,1024]{2,1,0:T(8,128)(2,1)S(1)} %get-tuple-element.215.refs_6_.refs_0_), channel_id=1, source_target_pairs={{0,2},{2,4},{4,6},{6,7},{7,5},{5,3},{3,1},{1,0},{8,10},{10,12},{12... | collective-permute-start | bytes 786440 | tf_op jit(solution)/shard_map/ppermute | solution.py:351
  90.3 9.5 %collective-permute-start.27 = (bf16[2,64,1024]{2,1,0:T(8,128)(2,1)S(1)}, bf16[2,64,1024]{2,1,0:T(8,128)(2,1)S(1)}, u32[]{:S(2)}, u32[]{:S(2)}) collective-permute-start(bf16[2,64,1024]{2,1,0:T(8,128)(2,1)S(1)} %get-tuple-element.218), channel_id=1, source_target_pairs={{2,0},{4,2},{6,4},{7,6},{5,7},{3,5},{1,3},{0,1},{10,8},{12,10},{14... | collective-permute-start | bytes 786440 | tf_op jit(solution)/shard_map/ppermute | solution.py:351
  94.3 9.7 %collective-permute-start.32 = (bf16[2,64,1024]{2,1,0:T(8,128)(2,1)S(1)}, bf16[2,64,1024]{2,1,0:T(8,128)(2,1)S(1)}, u32[]{:S(2)}, u32[]{:S(2)}) collective-permute-start(bf16[2,64,1024]{2,1,0:T(8,128)(2,1)S(1)} %get-tuple-element.223.refs_0_), channel_id=1, source_target_pairs={{0,2},{2,4},{4,6},{6,7},{7,5},{5,3},{3,1},{1,0},{8,10},{10,12},{12... | collective-permute-start | bytes 786440 | tf_op jit(solution)/shard_map/ppermute | solution.py:351
  95.9 9.5 %collective-permute-start.33 = (bf16[2,64,1024]{2,1,0:T(8,128)(2,1)S(1)}, bf16[2,64,1024]{2,1,0:T(8,128)(2,1)S(1)}, u32[]{:S(2)}, u32[]{:S(2)}) collective-permute-start(bf16[2,64,1024]{2,1,0:T(8,128)(2,1)S(1)} %get-tuple-element.230), channel_id=1, source_target_pairs={{2,0},{4,2},{6,4},{7,6},{5,7},{3,5},{1,3},{0,1},{10,8},{12,10},{14... | collective-permute-start | bytes 786440 | tf_op jit(solution)/shard_map/ppermute | solution.py:351
  99.9 9.7 %collective-permute-start.30 = (bf16[2,64,1024]{2,1,0:T(8,128)(2,1)S(1)}, bf16[2,64,1024]{2,1,0:T(8,128)(2,1)S(1)}, u32[]{:S(2)}, u32[]{:S(2)}) collective-permute-start(bf16[2,64,1024]{2,1,0:T(8,128)(2,1)S(1)} %get-tuple-element.224.refs_6_.refs_0_), channel_id=1, source_target_pairs={{0,2},{2,4},{4,6},{6,7},{7,5},{5,3},{3,1},{1,0},{8,10},{10,12},{12... | collective-permute-start | bytes 786440 | tf_op jit(solution)/shard_map/ppermute | solution.py:351
  101.5 9.5 %collective-permute-start.31 = (bf16[2,64,1024]{2,1,0:T(8,128)(2,1)S(1)}, bf16[2,64,1024]{2,1,0:T(8,128)(2,1)S(1)}, u32[]{:S(2)}, u32[]{:S(2)}) collective-permute-start(bf16[2,64,1024]{2,1,0:T(8,128)(2,1)S(1)} %get-tuple-element.227), channel_id=1, source_target_pairs={{2,0},{4,2},{6,4},{7,6},{5,7},{3,5},{1,3},{0,1},{10,8},{12,10},{14... | collective-permute-start | bytes 786440 | tf_op jit(solution)/shard_map/ppermute | solution.py:351
  105.5 11.1 %collective-permute-start.35 = (bf16[2,64,1024]{2,1,0:T(8,128)(2,1)S(1)}, bf16[2,64,1024]{2,1,0:T(8,128)(2,1)S(1)}, u32[]{:S(2)}, u32[]{:S(2)}) collective-permute-start(bf16[2,64,1024]{2,1,0:T(8,128)(2,1)S(1)} %get-tuple-element.235), channel_id=1, source_target_pairs={{2,0},{4,2},{6,4},{7,6},{5,7},{3,5},{1,3},{0,1},{10,8},{12,10},{14... | collective-permute-start | bytes 786440 | tf_op jit(solution)/shard_map/ppermute | solution.py:351
  106.2 10.5 %collective-permute-start.36 = (bf16[2,64,1024]{2,1,0:T(8,128)(2,1)S(1)}, bf16[2,64,1024]{2,1,0:T(8,128)(2,1)S(1)}, u32[]{:S(2)}, u32[]{:S(2)}) collective-permute-start(bf16[2,64,1024]{2,1,0:T(8,128)(2,1)S(1)} %get-tuple-element.231.refs_0_), channel_id=1, source_target_pairs={{0,2},{2,4},{4,6},{6,7},{7,5},{5,3},{3,1},{1,0},{8,10},{10,12},{12... | collective-permute-start | bytes 786440 | tf_op jit(solution)/shard_map/ppermute | solution.py:351
  111.2 7.6 %collective-permute-start.34 = (bf16[2,64,1024]{2,1,0:T(8,128)(2,1)S(1)}, bf16[2,64,1024]{2,1,0:T(8,128)(2,1)S(1)}, u32[]{:S(2)}, u32[]{:S(2)}) collective-permute-start(bf16[2,64,1024]{2,1,0:T(8,128)(2,1)S(1)} %get-tuple-element.232.refs_6_), channel_id=1, source_target_pairs={{0,2},{2,4},{4,6},{6,7},{7,5},{5,3},{3,1},{1,0},{8,10},{10,12},{12... | collective-permute-start | bytes 786440 | tf_op jit(solution)/shard_map/ppermute | solution.py:351
  112.8 7.1 %collective-permute-start.37 = (bf16[2,64,1024]{2,1,0:T(8,128)(2,1)S(1)}, bf16[2,64,1024]{2,1,0:T(8,128)(2,1)S(1)}, u32[]{:S(2)}, u32[]{:S(2)}) collective-permute-start(bf16[2,64,1024]{2,1,0:T(8,128)(2,1)S(1)} %get-tuple-element.236), channel_id=1, source_target_pairs={{2,0},{4,2},{6,4},{7,6},{5,7},{3,5},{1,3},{0,1},{10,8},{12,10},{14... | collective-permute-start | bytes 786440 | tf_op jit(solution)/shard_map/ppermute | solution.py:351
  (9 other events, 25.4 us)
